TPU v7x, 256 devices: a whole 4x4x8 slice. The times are simulated.
256 devices in a mesh: group: 8 (over x, core), seq: 32 (over y, z).
Axes of the slice: x: 4, y: 4, z: 8, core: 2. Of those that a mesh axis runs over, the one named last changes fastest.
Arguments:
- tokens: bfloat16 [16, 32768, 1024], P('group', 'seq'), may hold values from -24 to 24
- slot_params: bfloat16 [1024, 256], replicated, may hold values from -1 to 1
- w_up: bfloat16 [1024, 262144], P(None, ('group', 'seq')), may hold values from -0.1875 to 0.1875
- w_down: bfloat16 [262144, 1024], P(('group', 'seq')), may hold values from -0.375 to 0.375
Outputs:
- mixed: bfloat16 [16, 32768, 1024], P('group', 'seq')
All inputs are finite; a program needn't handle non-finite values.
Results may differ from a plain program's by a relative error of at most 0.012.
Values may be sent and summed in bfloat16 or wider, within the bound.
No kernel may reach another device: no remote copies, remote signals or barrier semaphores. Data moves between devices by JAX's collectives and lax.ppermute only.
A program may use at most 192 MiB of HBM per device.

v0:
```python
import jax
import jax.numpy as jnp
from jax import lax
from jax.sharding import PartitionSpec as P

SLOT_P = 4
EXP_G = 8


def shards(tokens, slot_params, w_up, w_down):
    feature_width = tokens.shape[2]
    logits = jnp.einsum("ctd,ds->cts", tokens, slot_params, preferred_element_type=jnp.float32)
    col_peak = lax.pmax(jnp.max(logits, axis=1), "seq")
    spread = jnp.exp(logits - col_peak[:, None, :])
    col_local = jnp.sum(spread, axis=1)
    partial_in = jnp.einsum(
        "cts,ctd->csd", spread.astype(jnp.bfloat16), tokens, preferred_element_type=jnp.float32
    )
    combine = jax.nn.softmax(logits, axis=2).astype(jnp.bfloat16)
    total_in, col_total = lax.psum((partial_in, col_local), "seq")
    slot_in = (total_in / col_total[:, :, None]).astype(jnp.bfloat16)
    arrived = lax.all_to_all(slot_in, "group", split_axis=1, concat_axis=0, tiled=True)
    senders = arrived.shape[0]
    grouped = arrived.reshape(senders, EXP_G, SLOT_P, feature_width)
    devices_each = lax.axis_size("seq") // EXP_G
    own_expert = lax.axis_index("seq") // devices_each
    own_slots = lax.dynamic_index_in_dim(grouped, own_expert, 1, keepdims=False)
    hidden = jax.nn.gelu(
        jnp.einsum("npd,df->npf", own_slots, w_up, preferred_element_type=jnp.float32)
    ).astype(jnp.bfloat16)
    expert_term = jnp.einsum("npf,fd->npd", hidden, w_down, preferred_element_type=jnp.float32)
    selector = (jnp.arange(EXP_G, dtype=jnp.int32) == own_expert).astype(jnp.float32)
    partial_out = selector[None, :, None, None] * expert_term[:, None, :, :]
    expert_out = lax.psum(partial_out, "seq").astype(jnp.bfloat16)
    returned = lax.all_to_all(
        expert_out.reshape(senders, EXP_G * SLOT_P, feature_width),
        "group",
        split_axis=0,
        concat_axis=1,
        tiled=True,
    )
    mixed = jnp.einsum(
        "cts,csd->ctd", combine, returned, preferred_element_type=jnp.float32
    ).astype(jnp.bfloat16)
    return mixed


def solution(mesh):
    placed = (P("group", "seq", None), P(), P(None, ("group", "seq")), P(("group", "seq"), None))
    return jax.shard_map(
        shards, mesh=mesh, in_specs=placed, out_specs=P("group", "seq", None), check_vma=False
    )
```

profile of v0, /device:TPU:2, one launch (start us, length us, event | category | flops | bytes accessed | tf_op | source)
XLA Modules:
  0.0 475.5 jit_solution(13177479825515873334)
XLA Ops:
  6.5 0.0 copy-start
  6.5 0.0 all-reduce.3.cloned.1.call-start
  6.5 5.1 %fusion.40 = (f32[2,256]{1,0:T(2,128)S(1)}, f32[2,1024,256]{2,1,0:T(8,128)}) fusion(bf16[2,1024,1024]{2,1,0:T(8,128)(2,1)} %param.4, bf16[1024,256]{1,0:T(8,128)(2,1)} %param.5), kind=kOutput, calls=%fused_computation.41 | convolution fusion | flops 1074265600 | bytes 6817792 | tf_op jit(solution)/shard_map/ctd,ds->cts/dot_general | solution.py:12
  11.6 77.9 %pmax.7 = f32[2,256]{1,0:T(2,128)S(1)} all-reduce(f32[2,256]{1,0:T(2,128)S(1)} %get-tuple-element.5), channel_id=1, replica_groups=mesh['group'=8,'seq'=32] {'seq'}, use_global_device_ids=true, to_apply=%region_3.0 | all-reduce | flops 512 | bytes 4096 | tf_op jit(solution)/shard_map/pmax | solution.py:13
  89.5 5.5 %fusion.7 = f32[2,256,1024]{2,1,0:T(8,128)} fusion(bf16[2,1024,1024]{2,1,0:T(8,128)(2,1)} %param.4, f32[2,1024,256]{2,1,0:T(8,128)} %get-tuple-element.6, f32[2,256]{1,0:T(2,128)S(1)} %pmax.7), kind=kOutput, calls=%fused_computation.12 | convolution fusion | flops 1074790400 | bytes 8390656 | tf_op jit(solution)/shard_map/cts,ctd->csd/dot_general | solution.py:16
  95.0 0.0 all-reduce.3.cloned.1.call-update
  95.0 1.9 fusion.5
  96.9 69.7 %psum.22 = f32[2,256]{1,0:T(2,128)S(1)} all-reduce(f32[2,256]{1,0:T(2,128)S(1)} %fusion.5), channel_id=1, replica_groups=mesh['group'=8,'seq'=32] {'seq'}, use_global_device_ids=true, to_apply=%region_6.0 | all-reduce | flops 512 | bytes 4096 | tf_op jit(solution)/shard_map/psum | solution.py:20
  166.5 76.7 %all-reduce.3.cloned.1.call-done = f32[2,256,1024]{2,1,0:T(8,128)} async-done(((f32[2,256,1024]{2,1,0:T(8,128)}), f32[2,256,1024]{2,1,0:T(8,128)}) %all-reduce.3.cloned.1.call-update) | async-done | bytes 2097168 | tf_op jit(solution)/shard_map/psum | solution.py:20
  243.2 1.9 divide_convert_fusion
  245.1 2.0 copy.13
  247.1 4.8 %all-to-all-start = ((bf16[2,256,1024]{2,0,1:T(2,128)(2,1)}), bf16[2,256,1024]{2,0,1:T(2,128)(2,1)S(1)}, u32[]{:S(2)}, u32[]{:S(2)}) async-start(bf16[2,256,1024]{2,0,1:T(2,128)(2,1)} %copy.13), calls=%async_computation | async-start | bytes 2097152 | tf_op jit(solution)/shard_map/all_to_all | solution.py:22
  251.9 14.5 %all-to-all-done = bf16[2,256,1024]{2,0,1:T(2,128)(2,1)S(1)} async-done(((bf16[2,256,1024]{2,0,1:T(2,128)(2,1)}), bf16[2,256,1024]{2,0,1:T(2,128)(2,1)S(1)}, u32[]{:S(2)}, u32[]{:S(2)}) %all-to-all-start) | async-done | bytes 1048608 | tf_op jit(solution)/shard_map/all_to_all | solution.py:22
  266.4 1.3 copy.25
  267.7 1.5 reshape.17
  269.2 0.1 constant_dynamic-slice_fusion
  269.2 0.0 copy-done
  269.2 2.5 fusion.1
  271.7 0.2 copy.16
  271.9 1.9 broadcast_multiply_fusion
  273.8 164.9 %all-reduce.4 = bf16[16,8,4,1024]{3,2,1,0:T(4,128)(2,1)S(1)} all-reduce(f32[16,8,4,1024]{3,2,1,0:T(4,128)} %broadcast_multiply_fusion), channel_id=1, replica_groups=mesh['group'=8,'seq'=32] {'seq'}, use_global_device_ids=true, to_apply=%region_7.8 | all-reduce | flops 524288 | bytes 3145728 | tf_op jit(solution)/shard_map/psum | solution.py:34
  438.7 1.1 reshape.18
  439.8 4.9 %all-to-all-start.1 = ((bf16[16,32,1024]{2,1,0:T(8,128)(2,1)}), bf16[16,32,1024]{2,1,0:T(8,128)(2,1)S(1)}, u32[]{:S(2)}, u32[]{:S(2)}) async-start(bf16[16,32,1024]{2,1,0:T(8,128)(2,1)} %reshape.18), calls=%async_computation.1 | async-start | bytes 2097152 | tf_op jit(solution)/shard_map/all_to_all | solution.py:35
  444.7 2.9 fusion.41
  447.6 11.7 %all-to-all-done.1 = bf16[16,32,1024]{2,1,0:T(8,128)(2,1)S(1)} async-done(((bf16[16,32,1024]{2,1,0:T(8,128)(2,1)}), bf16[16,32,1024]{2,1,0:T(8,128)(2,1)S(1)}, u32[]{:S(2)}, u32[]{:S(2)}) %all-to-all-start.1) | async-done | bytes 1048608 | tf_op jit(solution)/shard_map/all_to_all | solution.py:35
  459.2 1.1 copy.17
  460.3 8.4 %convolution_convert_fusion = bf16[2,1024,1024]{2,1,0:T(8,128)(2,1)} fusion(bf16[2,256,1024]{2,1,0:T(8,128)(2,1)} %bitcast.39, f32[2,1024]{1,0:T(2,128)S(1)} %fusion.41, f32[2,1024,256]{2,1,0:T(8,128)} %get-tuple-element.6), kind=kOutput, calls=%fused_computation.1 | convolution fusion | flops 1077414144 | bytes 7348224 | tf_op jit(solution)/shard_map/cts,csd->ctd/dot_general | solution.py:42
  (1 shorter events, 0.0 us)
Async XLA Ops:
  6.5 262.7 %copy-start = (bf16[1024,1024]{1,0:T(8,128)(2,1)S(1)}, bf16[1024,1024]{1,0:T(8,128)(2,1)}, u32[]{:S(2)}) copy-start(bf16[1024,1024]{1,0:T(8,128)(2,1)} %param.7) | copy-start | bytes 6291460
  6.5 236.7 %all-reduce.3.cloned.1.call-start = ((), (), s32[]{:S(2)}) async-start(), calls=%async_computation.2 | async-start | bytes 4194304 | tf_op jit(solution)/shard_map/psum | solution.py:20
  247.1 19.3 %all-to-all-start = ((bf16[2,256,1024]{2,0,1:T(2,128)(2,1)}), bf16[2,256,1024]{2,0,1:T(2,128)(2,1)S(1)}, u32[]{:S(2)}, u32[]{:S(2)}) async-start(bf16[2,256,1024]{2,0,1:T(2,128)(2,1)} %copy.13), calls=%async_computation | async-start | bytes 2097152 | tf_op jit(solution)/shard_map/all_to_all | solution.py:22
  439.8 19.5 %all-to-all-start.1 = ((bf16[16,32,1024]{2,1,0:T(8,128)(2,1)}), bf16[16,32,1024]{2,1,0:T(8,128)(2,1)S(1)}, u32[]{:S(2)}, u32[]{:S(2)}) async-start(bf16[16,32,1024]{2,1,0:T(8,128)(2,1)} %reshape.18), calls=%async_computation.1 | async-start | bytes 2097152 | tf_op jit(solution)/shard_map/all_to_all | solution.py:35
Sparse Core Ops, SparseCore 0:
  95.1 148.0 all-reduce.2
where the time goes:
time: 477 us; the launch traced here: 476 us
  blocking collectives  312 us (65%)
  waiting for transfers between devices  103 us (22%)
  matrix products  21.3 us (4%)
  between operations  13.5 us (3%)
  starting transfers between devices  9.73 us (2%)
  other arithmetic  8.52 us (2%)
  local copies, waits for them, and re-layouts  7.19 us (2%)
    psum x1, blocking collectives, shards(): expert_out = lax.psum(partial_out, 'seq').astype(jnp.bfloat16)  165 us
    pmax x1, blocking collectives, shards(): col_peak = lax.pmax(jnp.max(logits, axis=1), 'seq')  77.9 us
    psum x1, waiting for transfers between devices, shards(): total_in, col_total = lax.psum((partial_in, col_local), 'seq')  76.7 us
    psum x1, blocking collectives, shards(): total_in, col_total = lax.psum((partial_in, col_local), 'seq')  69.7 us
    all_to_all x1, waiting for transfers between devices, shards(): lax.all_to_all(slot_in, 'group', split_axis=1, concat_axis=0, tiled=True)  14.5 us
    all_to_all x1, waiting for transfers between devices, shards(): lax.all_to_all(expert_out.reshape(senders, EXP_G * SLOT_P, feature_width)...  11.7 us
  transfers between devices with their start and end apart: 3, of which 3 were waited for; matrix products, arithmetic and copies ran while one was open for 1% of the time, Pallas kernels for 0%

commit v1 on v0

v1 whole, which is shorter than its diff:
```python
import functools

import jax
import jax.numpy as jnp
from jax import lax
from jax.experimental import pallas as pl
from jax.experimental.pallas import tpu as pltpu
from jax.sharding import Mesh
from jax.sharding import PartitionSpec as P

F32 = jnp.float32
BF16 = jnp.bfloat16
SLOT_P = 4
STAT = 128
MIB = 1 << 20


def vmem():
    return pl.BlockSpec(memory_space=pltpu.VMEM)


def params(mib=48):
    return pltpu.CompilerParams(vmem_limit_bytes=mib * MIB)


def device_order(slot_params, groups, ny, nz):
    slots = slot_params.shape[1]
    y = lax.axis_index("y")
    z = lax.axis_index("zh") * lax.axis_size("quarter") + lax.axis_index("quarter")
    row = lax.broadcasted_iota(jnp.int32, (slots, slots), 0)
    col = lax.broadcasted_iota(jnp.int32, (slots, slots), 1)
    at_y = (col // (nz * groups) + y) % ny
    at_z = (col // groups % nz + z) % nz
    perm = (row == (col % groups * ny + at_y) * nz + at_z).astype(F32).astype(BF16)
    return jnp.dot(slot_params, perm, preferred_element_type=F32).astype(BF16)


def gather_kernel(groups, ny, nz, tok_ref, sp_ref, *refs):
    out_refs, tick_ref = refs[:-1], refs[-1]
    tok = tok_ref[0]
    logits = jnp.dot(tok, device_order(sp_ref[...], groups, ny, nz), preferred_element_type=F32)
    peak = jnp.max(logits, axis=0, keepdims=True)
    spread = jnp.exp(logits - peak)
    total = jnp.sum(spread, axis=0, keepdims=True)
    summed = lax.dot_general(
        spread.astype(BF16), tok, (((0,), (0,)), ((), ())), preferred_element_type=F32
    )
    slots = logits.shape[1]
    both = jnp.concatenate([total, peak + jnp.log(total), jnp.zeros((6, slots), F32)], axis=0)
    cols = both.T
    wide = jnp.concatenate([summed / cols[:, 0:1], pack(cols[:, 1:2])], axis=1)
    wide = wide.reshape(ny, nz, groups, wide.shape[1]).astype(BF16)
    for i in range(ny):
        out_refs[i][:, 0] = wide[i]
    tick_ref[0] = both


def combine_kernel(groups, ny, nz, tok_ref, sp_ref, tick_ref, out_ref):
    logits = jnp.dot(tok_ref[0], device_order(sp_ref[...], groups, ny, nz), preferred_element_type=F32)
    spread = jnp.exp(logits - jnp.max(logits, axis=1, keepdims=True))
    out_ref[0] = (spread / jnp.sum(spread, axis=1, keepdims=True)).astype(BF16)


def pack(lse):
    hi = lse.astype(BF16).astype(F32)
    mid = (lse - hi).astype(BF16).astype(F32)
    low = lse - hi - mid
    lane = lax.broadcasted_iota(jnp.int32, lse.shape[:-1] + (STAT,), lse.ndim - 1)
    return jnp.where(lane == 0, hi, jnp.where(lane == 1, mid, jnp.where(lane == 2, low, 0.0)))


def merged(width, wides):
    lses = []
    for wide in wides:
        stat = wide[..., width:].astype(F32)
        lses.append(stat[..., 0:1] + stat[..., 1:2] + stat[..., 2:3])
    peak = functools.reduce(jnp.maximum, lses)
    weights = [jnp.exp(lse - peak) for lse in lses]
    total = sum(weights)
    mean = sum(wide[..., :width].astype(F32) * (w / total) for wide, w in zip(wides, weights))
    return mean, peak + jnp.log(total)


def halfway_kernel(width, ny, *refs):
    in_refs, out_refs = refs[:ny], refs[ny:]
    for k, out_ref in enumerate(out_refs):
        mean, lse = merged(width, [r[k] for r in in_refs])
        out_ref[...] = jnp.concatenate([mean, pack(lse)], axis=-1).astype(BF16)


def merge_kernel(width, *refs):
    in_refs, out_ref = refs[:-1], refs[-1]
    clips, groups = in_refs[0].shape[:2]
    acc, _ = merged(width, [r[...] for r in in_refs])
    for g in range(groups):
        rows = jnp.concatenate([acc[c, g : g + 1] for c in range(clips)], axis=0).astype(BF16)
        for q in range(SLOT_P):
            out_ref[g * SLOT_P + q] = rows


def expert_kernel(x_ref, up_ref, down_ref, out_ref):
    parts, clips, width = x_ref.shape
    x = x_ref[...].astype(F32).reshape(parts * clips, width).astype(BF16)
    hidden = jax.nn.gelu(jnp.dot(x, up_ref[...], preferred_element_type=F32)).astype(BF16)
    out = jnp.dot(hidden, down_ref[...], preferred_element_type=F32)
    out_ref[...] = out.reshape(parts, clips, width).astype(BF16)


def total_kernel(x_ref, out_ref):
    parts, clips, width = x_ref.shape
    x = x_ref[...].astype(F32).reshape(parts // SLOT_P, SLOT_P, clips, width)
    total = jnp.sum(x, axis=1)
    for c in range(clips):
        out_ref[c] = jnp.concatenate(
            [total[g, c : c + 1] for g in range(parts // SLOT_P)], axis=0
        ).astype(BF16)


def stack_kernel(*refs):
    for k, ref in enumerate(refs[:-1]):
        refs[-1][k] = ref[...]


def mix_kernel(comb_ref, *refs):
    slot_refs, out_ref = refs[:-1], refs[-1]
    nz, _, groups, width = slot_refs[0].shape
    slots = [r[:, 0].astype(F32).reshape(nz * groups, width) for r in slot_refs]
    slots = jnp.concatenate(slots, axis=0).astype(BF16)
    out_ref[0] = jnp.dot(comb_ref[0], slots, preferred_element_type=F32).astype(BF16)


def shards(tokens, slot_params, w_up, w_down):
    clips, length, width = tokens.shape
    slots = slot_params.shape[1]
    groups = lax.axis_size("group")
    around = ("zh", "quarter")
    ny, nz = lax.axis_size("y"), lax.axis_size(around)
    sharers = ("group", "quarter")

    def name(f, *a):
        def body(*refs):
            f(*a, *refs)

        return body

    def shift(x, axis, n, k):
        return lax.ppermute(x, axis, [(i, (i + k) % n) for i in range(n)])

    tok_spec = pl.BlockSpec((1, length, width), lambda c: (c, 0, 0))
    sp_spec = pl.BlockSpec((width, slots), lambda c: (0, 0))
    tick_spec = pl.BlockSpec((1, 8, slots), lambda c: (c, 0, 0))
    wide = width + STAT
    *means, tick = pl.pallas_call(
        name(gather_kernel, groups, ny, nz),
        grid=(clips,),
        in_specs=[tok_spec, sp_spec],
        out_specs=[pl.BlockSpec((nz, 1, groups, wide), lambda c: (0, c, 0, 0))] * ny + [tick_spec],
        out_shape=[jax.ShapeDtypeStruct((nz, clips, groups, wide), BF16)] * ny
        + [jax.ShapeDtypeStruct((clips, 8, slots), F32)],
        compiler_params=params(56),
        name="gather",
    )(tokens, slot_params)
    arrived = [means[0]] + [shift(means[k], "y", ny, k) for k in range(1, ny)]
    combine = pl.pallas_call(
        name(combine_kernel, groups, ny, nz),
        grid=(clips,),
        in_specs=[tok_spec, sp_spec, tick_spec],
        out_specs=pl.BlockSpec((1, length, slots), lambda c: (c, 0, 0)),
        out_shape=jax.ShapeDtypeStruct((clips, length, slots), BF16),
        compiler_params=params(56),
        cost_estimate=pl.CostEstimate(
            flops=2 * clips * length * width * slots,
            bytes_accessed=2 * clips * length * (width + slots),
            transcendentals=clips * length * slots,
        ),
        name="combine",
    )(tokens, slot_params, tick)
    halfway = pl.pallas_call(
        name(halfway_kernel, width, ny),
        in_specs=[vmem()] * ny,
        out_specs=[vmem()] * nz,
        out_shape=[jax.ShapeDtypeStruct((clips, groups, wide), BF16)] * nz,
        compiler_params=params(),
        name="halfway",
    )(*arrived)
    arrived = [halfway[0]] + [shift(halfway[k], around, nz, k) for k in range(1, nz)]
    slot_in = pl.pallas_call(
        name(merge_kernel, width),
        in_specs=[vmem()] * nz,
        out_specs=vmem(),
        out_shape=jax.ShapeDtypeStruct((groups * SLOT_P, clips, width), BF16),
        compiler_params=params(),
        name="merge",
    )(*arrived)
    own = lax.all_to_all(slot_in, sharers, 0, 0, tiled=True)
    partial = pl.pallas_call(
        expert_kernel,
        in_specs=[vmem()] * 3,
        out_specs=vmem(),
        out_shape=jax.ShapeDtypeStruct((groups * SLOT_P, clips, width), BF16),
        compiler_params=params(),
        name="expert",
    )(own, w_up, w_down)
    back = lax.all_to_all(partial, sharers, 0, 0, tiled=True)
    slot_out = pl.pallas_call(
        total_kernel,
        in_specs=[vmem()],
        out_specs=vmem(),
        out_shape=jax.ShapeDtypeStruct((clips, groups, width), BF16),
        compiler_params=params(),
        name="total",
    )(back)
    ring = pl.pallas_call(
        stack_kernel,
        in_specs=[vmem()] * nz,
        out_specs=vmem(),
        out_shape=jax.ShapeDtypeStruct((nz, clips, groups, width), BF16),
        compiler_params=params(),
        name="stack",
    )(slot_out, *[shift(slot_out, around, nz, -k) for k in range(1, nz)])
    rings = [ring] + [shift(ring, "y", ny, -k) for k in range(1, ny)]
    half = length // 2
    return pl.pallas_call(
        mix_kernel,
        grid=(clips, 2),
        in_specs=[
            pl.BlockSpec((1, half, slots), lambda c, t: (c, t, 0)),
        ]
        + [pl.BlockSpec((nz, 1, groups, width), lambda c, t: (0, c, 0, 0))] * ny,
        out_specs=pl.BlockSpec((1, half, width), lambda c, t: (c, t, 0)),
        out_shape=jax.ShapeDtypeStruct((clips, length, width), BF16),
        compiler_params=params(),
        name="mix",
    )(combine, *rings)


def solution(mesh):
    groups, n = mesh.devices.shape
    split = Mesh(mesh.devices.reshape(groups, 4, n // (4 * SLOT_P), SLOT_P), ("group", "y", "zh", "quarter"))
    seq = ("y", "zh", "quarter")
    everyone = ("group",) + seq
    placed = (P("group", seq, None), P(), P(None, everyone), P(everyone, None))
    return jax.shard_map(
        shards, mesh=split, in_specs=placed, out_specs=P("group", seq, None), check_vma=False
    )
```

time: 477 us -> 113 us (0.24)
  blocking collectives: 312 us -> 26.1 us
  waiting for transfers between devices: 103 us -> 19.9 us
  starting transfers between devices: 9.73 us -> 45 us
  matrix products: 21.3 us -> 0 us
  Pallas kernels: 0 us -> 18.7 us
  between operations: 13.5 us -> 0.07 us
  other arithmetic: 8.52 us -> 0 us
  local copies, waits for them, and re-layouts: 7.19 us -> 2.19 us
    psum x2 -> x0, blocking collectives: 235 us -> none  [the longest x1 165 us: shards(): expert_out = lax.psum(partial_out, 'seq').astype(jnp.bfloat16)]
    pmax x1 -> x0, blocking collectives: 77.9 us -> none  [shards(): col_peak = lax.pmax(jnp.max(logits, axis=1), 'seq')]
    psum x1 -> x0, waiting for transfers between devices: 76.7 us -> none  [shards(): total_in, col_total = lax.psum((partial_in, col_local), 'seq')]
    ppermute x0 -> x20, starting transfers between devices: none -> 45 us  [shift(): return lax.ppermute(x, axis, [(i, (i + k) % n) for i in range(n)])]
    all_to_all x2 -> x0, waiting for transfers between devices: 26.2 us -> none  [the longest x1 14.5 us: shards(): lax.all_to_all(slot_in, 'group', split_axis=1, concat_axis=0, tiled=True)]
    all_to_all x0 -> x2, blocking collectives: none -> 26.1 us  [the longest x1 13.6 us: shards(): own = lax.all_to_all(slot_in, sharers, 0, 0, tiled=True)]
    dot_general x4 -> x0, matrix products: 21.3 us -> none  [the longest x1 8.36 us: shards(): jnp.einsum('cts,csd->ctd', combine, returned, preferred_element_type=jnp....]
    ppermute x0 -> x20, waiting for transfers between devices: none -> 19.9 us  [shift(): return lax.ppermute(x, axis, [(i, (i + k) % n) for i in range(n)])]
  transfers between devices with their start and end apart: 3 -> 20, of which waited for: 3 -> 9; matrix products, arithmetic and copies ran while one was open for 1% -> 0% of each run, Pallas kernels for 0% -> 5%
where the time goes in v1:
time: 113 us; the launch traced here: 112 us
  starting transfers between devices  45 us (40%)
  blocking collectives  26.1 us (23%)
  waiting for transfers between devices  19.9 us (18%)
  Pallas kernels  18.7 us (17%)
  local copies, waits for them, and re-layouts  2.19 us (2%)
    ppermute x20, starting transfers between devices, shift(): return lax.ppermute(x, axis, [(i, (i + k) % n) for i in range(n)])  45 us
    ppermute x20, waiting for transfers between devices, shift(): return lax.ppermute(x, axis, [(i, (i + k) % n) for i in range(n)])  19.9 us
    all_to_all x1, blocking collectives, shards(): own = lax.all_to_all(slot_in, sharers, 0, 0, tiled=True)  13.6 us
    all_to_all x1, blocking collectives, shards(): back = lax.all_to_all(partial, sharers, 0, 0, tiled=True)  12.5 us
    pallas_call x1, Pallas kernels, shards(): pl.pallas_call(name(gather_kernel, groups, ny, nz), grid=(clips,), in_spe...  8.32 us
    pallas_call x1, Pallas kernels, shards(): pl.pallas_call(name(combine_kernel, groups, ny, nz), grid=(clips,), in_sp...  5.07 us
    pallas_call x1, Pallas kernels, shards(): pl.pallas_call(mix_kernel, grid=(clips, 2), in_specs=[pl.BlockSpec((1, ha...  3.39 us
  transfers between devices with their start and end apart: 20, of which 9 were waited for; matrix products, arithmetic and copies ran while one was open for 0% of the time, Pallas kernels for 5%

profile of v1, /device:TPU:2, one launch (start us, length us, event | category | flops | bytes accessed | tf_op | source)
XLA Modules:
  0.0 112.1 jit_solution(15322680384616861984)
XLA Ops:
  0.0 8.3 %gather.1 = (bf16[8,2,8,1152]{3,2,1,0:T(8,128)(2,1)}, bf16[8,2,8,1152]{3,2,1,0:T(8,128)(2,1)}, bf16[8,2,8,1152]{3,2,1,0:T(8,128)(2,1)}, bf16[8,2,8,1152]{3,2,1,0:T(8,128)(2,1)}, f32[2,8,256]{2,1,0:T(8,128)}) custom-call(bf16[2,1024,1024]{2,1,0:T(8,128)(2,1)} %refs_0_.3, bf16[1024,256]{1,0:T(8,128)(2,1)} %refs_1_.3), custom_call_target="tpu_custom_call" | custom-call | tf_op jit(solution)/shard_map/gather/pallas_call | solution.py:153
  8.3 1.6 %collective-permute-start = (bf16[8,2,8,1152]{3,2,1,0:T(8,128)(2,1)}, bf16[8,2,8,1152]{3,2,1,0:T(8,128)(2,1)S(1)}, u32[]{:S(2)}, u32[]{:S(2)}) collective-permute-start(bf16[8,2,8,1152]{3,2,1,0:T(8,128)(2,1)} %get-tuple-element.20), channel_id=1, source_target_pairs={{0,8},{8,16},{16,24},{24,0},{1,9},{9,17},{17,25},{25,1},{2,10},{10... | collective-permute-start | bytes 884744 | tf_op jit(solution)/shard_map/ppermute | solution.py:147
  9.9 2.9 %collective-permute-start.1 = (bf16[8,2,8,1152]{3,2,1,0:T(8,128)(2,1)}, bf16[8,2,8,1152]{3,2,1,0:T(8,128)(2,1)S(1)}, u32[]{:S(2)}, u32[]{:S(2)}) collective-permute-start(bf16[8,2,8,1152]{3,2,1,0:T(8,128)(2,1)} %get-tuple-element.21), channel_id=1, source_target_pairs={{0,16},{8,24},{16,0},{24,8},{1,17},{9,25},{17,1},{25,9},{2,18},{10... | collective-permute-start | bytes 884744 | tf_op jit(solution)/shard_map/ppermute | solution.py:147
  12.8 1.3 %collective-permute-start.2 = (bf16[8,2,8,1152]{3,2,1,0:T(8,128)(2,1)}, bf16[8,2,8,1152]{3,2,1,0:T(8,128)(2,1)S(1)}, u32[]{:S(2)}, u32[]{:S(2)}) collective-permute-start(bf16[8,2,8,1152]{3,2,1,0:T(8,128)(2,1)} %get-tuple-element.22), channel_id=1, source_target_pairs={{0,24},{8,0},{16,8},{24,16},{1,25},{9,1},{17,9},{25,17},{2,26},{10... | collective-permute-start | bytes 884744 | tf_op jit(solution)/shard_map/ppermute | solution.py:147
  14.1 4.4 %collective-permute-done.refs_1_ = bf16[8,2,8,1152]{3,2,1,0:T(8,128)(2,1)S(1)} collective-permute-done((bf16[8,2,8,1152]{3,2,1,0:T(8,128)(2,1)}, bf16[8,2,8,1152]{3,2,1,0:T(8,128)(2,1)S(1)}, u32[]{:S(2)}, u32[]{:S(2)}) %collective-permute-start) | collective-permute-done | bytes 294944 | tf_op jit(solution)/shard_map/ppermute | solution.py:147
  18.5 7.5 %collective-permute-done.1.refs_2_ = bf16[8,2,8,1152]{3,2,1,0:T(8,128)(2,1)S(1)} collective-permute-done((bf16[8,2,8,1152]{3,2,1,0:T(8,128)(2,1)}, bf16[8,2,8,1152]{3,2,1,0:T(8,128)(2,1)S(1)}, u32[]{:S(2)}, u32[]{:S(2)}) %collective-permute-start.1) | collective-permute-done | bytes 294944 | tf_op jit(solution)/shard_map/ppermute | solution.py:147
  26.0 1.0 copy-done.3
  27.6 2.0 %collective-permute-start.3 = (bf16[2,8,1152]{2,1,0:T(8,128)(2,1)S(1)}, bf16[2,8,1152]{2,1,0:T(8,128)(2,1)S(1)}, u32[]{:S(2)}, u32[]{:S(2)}) collective-permute-start(bf16[2,8,1152]{2,1,0:T(8,128)(2,1)S(1)} %get-tuple-element.24), channel_id=1, source_target_pairs={{0,1},{1,2},{2,3},{3,4},{4,5},{5,6},{6,7},{7,0},{8,9},{9,10},{10,1... | collective-permute-start | bytes 110600 | tf_op jit(solution)/shard_map/ppermute | solution.py:147
  29.6 3.3 %collective-permute-start.4 = (bf16[2,8,1152]{2,1,0:T(8,128)(2,1)S(1)}, bf16[2,8,1152]{2,1,0:T(8,128)(2,1)S(1)}, u32[]{:S(2)}, u32[]{:S(2)}) collective-permute-start(bf16[2,8,1152]{2,1,0:T(8,128)(2,1)S(1)} %get-tuple-element.25), channel_id=1, source_target_pairs={{0,2},{1,3},{2,4},{3,5},{4,6},{5,7},{6,0},{7,1},{8,10},{9,11},{10,... | collective-permute-start | bytes 110600 | tf_op jit(solution)/shard_map/ppermute | solution.py:147
  32.9 4.0 %collective-permute-start.5 = (bf16[2,8,1152]{2,1,0:T(8,128)(2,1)S(1)}, bf16[2,8,1152]{2,1,0:T(8,128)(2,1)S(1)}, u32[]{:S(2)}, u32[]{:S(2)}) collective-permute-start(bf16[2,8,1152]{2,1,0:T(8,128)(2,1)S(1)} %get-tuple-element.26), channel_id=1, source_target_pairs={{0,3},{1,4},{2,5},{3,6},{4,7},{5,0},{6,1},{7,2},{8,11},{9,12},{10,... | collective-permute-start | bytes 110600 | tf_op jit(solution)/shard_map/ppermute | solution.py:147
  37.4 5.0 %collective-permute-start.7 = (bf16[2,8,1152]{2,1,0:T(8,128)(2,1)S(1)}, bf16[2,8,1152]{2,1,0:T(8,128)(2,1)S(1)}, u32[]{:S(2)}, u32[]{:S(2)}) collective-permute-start(bf16[2,8,1152]{2,1,0:T(8,128)(2,1)S(1)} %get-tuple-element.28), channel_id=1, source_target_pairs={{0,5},{1,6},{2,7},{3,0},{4,1},{5,2},{6,3},{7,4},{8,13},{9,14},{10,... | collective-permute-start | bytes 110600 | tf_op jit(solution)/shard_map/ppermute | solution.py:147
  42.4 2.6 %collective-permute-start.8 = (bf16[2,8,1152]{2,1,0:T(8,128)(2,1)S(1)}, bf16[2,8,1152]{2,1,0:T(8,128)(2,1)S(1)}, u32[]{:S(2)}, u32[]{:S(2)}) collective-permute-start(bf16[2,8,1152]{2,1,0:T(8,128)(2,1)S(1)} %get-tuple-element.29), channel_id=1, source_target_pairs={{0,6},{1,7},{2,0},{3,1},{4,2},{5,3},{6,4},{7,5},{8,14},{9,15},{10,... | collective-permute-start | bytes 110600 | tf_op jit(solution)/shard_map/ppermute | solution.py:147
  45.0 1.0 collective-permute-start.9
  46.1 1.5 %collective-permute-done.8.refs_6_ = bf16[2,8,1152]{2,1,0:T(8,128)(2,1)S(1)} collective-permute-done((bf16[2,8,1152]{2,1,0:T(8,128)(2,1)S(1)}, bf16[2,8,1152]{2,1,0:T(8,128)(2,1)S(1)}, u32[]{:S(2)}, u32[]{:S(2)}) %collective-permute-start.8) | collective-permute-done | bytes 36896 | tf_op jit(solution)/shard_map/ppermute | solution.py:147
  47.6 1.4 %collective-permute-done.9.refs_7_ = bf16[2,8,1152]{2,1,0:T(8,128)(2,1)S(1)} collective-permute-done((bf16[2,8,1152]{2,1,0:T(8,128)(2,1)S(1)}, bf16[2,8,1152]{2,1,0:T(8,128)(2,1)S(1)}, u32[]{:S(2)}, u32[]{:S(2)}) %collective-permute-start.9) | collective-permute-done | bytes 36896 | tf_op jit(solution)/shard_map/ppermute | solution.py:147
  49.3 13.6 %all_to_all.10.x_ref = bf16[32,2,1024]{2,1,0:T(2,128)(2,1)S(1)} all-to-all(bf16[32,2,1024]{2,1,0:T(2,128)(2,1)S(1)} %merge.1), channel_id=1, replica_groups=mesh['group'=8,'y'=4,'zh'=2,'quarter'=4] {'group','quarter'}, dimensions={0} | all-to-all | bytes 262144 | tf_op jit(solution)/shard_map/all_to_all | solution.py:195
  62.9 1.0 expert.1
  63.8 12.5 %all_to_all.11.x_ref = bf16[32,2,1024]{2,1,0:T(2,128)(2,1)S(1)} all-to-all(bf16[32,2,1024]{2,1,0:T(2,128)(2,1)S(1)} %expert.1), channel_id=1, replica_groups=mesh['group'=8,'y'=4,'zh'=2,'quarter'=4] {'group','quarter'}, dimensions={0} | all-to-all | bytes 262144 | tf_op jit(solution)/shard_map/all_to_all | solution.py:204
  76.8 1.8 %collective-permute-start.15 = (bf16[2,8,1024]{2,1,0:T(8,128)(2,1)S(1)}, bf16[2,8,1024]{2,1,0:T(8,128)(2,1)S(1)}, u32[]{:S(2)}, u32[]{:S(2)}) collective-permute-start(bf16[2,8,1024]{2,1,0:T(8,128)(2,1)S(1)} %total.1.refs_0_), channel_id=1, source_target_pairs={{0,2},{1,3},{2,4},{3,5},{4,6},{5,7},{6,0},{7,1},{8,10},{9,11},{10,... | collective-permute-start | bytes 98312 | tf_op jit(solution)/shard_map/ppermute | solution.py:147
  78.6 3.1 %collective-permute-start.14 = (bf16[2,8,1024]{2,1,0:T(8,128)(2,1)S(1)}, bf16[2,8,1024]{2,1,0:T(8,128)(2,1)S(1)}, u32[]{:S(2)}, u32[]{:S(2)}) collective-permute-start(bf16[2,8,1024]{2,1,0:T(8,128)(2,1)S(1)} %total.1.refs_0_), channel_id=1, source_target_pairs={{0,3},{1,4},{2,5},{3,6},{4,7},{5,0},{6,1},{7,2},{8,11},{9,12},{10,... | collective-permute-start | bytes 98312 | tf_op jit(solution)/shard_map/ppermute | solution.py:147
  81.7 1.9 %collective-permute-start.13 = (bf16[2,8,1024]{2,1,0:T(8,128)(2,1)S(1)}, bf16[2,8,1024]{2,1,0:T(8,128)(2,1)S(1)}, u32[]{:S(2)}, u32[]{:S(2)}) collective-permute-start(bf16[2,8,1024]{2,1,0:T(8,128)(2,1)S(1)} %total.1.refs_0_), channel_id=1, source_target_pairs={{0,4},{1,5},{2,6},{3,7},{4,0},{5,1},{6,2},{7,3},{8,12},{9,13},{10,... | collective-permute-start | bytes 98312 | tf_op jit(solution)/shard_map/ppermute | solution.py:147
  83.6 4.1 %collective-permute-start.12 = (bf16[2,8,1024]{2,1,0:T(8,128)(2,1)S(1)}, bf16[2,8,1024]{2,1,0:T(8,128)(2,1)S(1)}, u32[]{:S(2)}, u32[]{:S(2)}) collective-permute-start(bf16[2,8,1024]{2,1,0:T(8,128)(2,1)S(1)} %total.1.refs_0_), channel_id=1, source_target_pairs={{0,5},{1,6},{2,7},{3,0},{4,1},{5,2},{6,3},{7,4},{8,13},{9,14},{10,... | collective-permute-start | bytes 98312 | tf_op jit(solution)/shard_map/ppermute | solution.py:147
  87.7 2.4 %collective-permute-start.11 = (bf16[2,8,1024]{2,1,0:T(8,128)(2,1)S(1)}, bf16[2,8,1024]{2,1,0:T(8,128)(2,1)S(1)}, u32[]{:S(2)}, u32[]{:S(2)}) collective-permute-start(bf16[2,8,1024]{2,1,0:T(8,128)(2,1)S(1)} %total.1.refs_0_), channel_id=1, source_target_pairs={{0,6},{1,7},{2,0},{3,1},{4,2},{5,3},{6,4},{7,5},{8,14},{9,15},{10,... | collective-permute-start | bytes 98312 | tf_op jit(solution)/shard_map/ppermute | solution.py:147
  90.1 1.9 %collective-permute-start.10 = (bf16[2,8,1024]{2,1,0:T(8,128)(2,1)S(1)}, bf16[2,8,1024]{2,1,0:T(8,128)(2,1)S(1)}, u32[]{:S(2)}, u32[]{:S(2)}) collective-permute-start(bf16[2,8,1024]{2,1,0:T(8,128)(2,1)S(1)} %total.1.refs_0_), channel_id=1, source_target_pairs={{0,7},{1,0},{2,1},{3,2},{4,3},{5,4},{6,5},{7,6},{8,15},{9,8},{10,9... | collective-permute-start | bytes 98312 | tf_op jit(solution)/shard_map/ppermute | solution.py:147
  92.6 1.4 %collective-permute-done.10.refs_1_ = bf16[2,8,1024]{2,1,0:T(8,128)(2,1)S(1)} collective-permute-done((bf16[2,8,1024]{2,1,0:T(8,128)(2,1)S(1)}, bf16[2,8,1024]{2,1,0:T(8,128)(2,1)S(1)}, u32[]{:S(2)}, u32[]{:S(2)}) %collective-permute-start.10) | collective-permute-done | bytes 32800 | tf_op jit(solution)/shard_map/ppermute | solution.py:147
  94.0 1.3 %collective-permute-start.19 = (bf16[8,2,8,1024]{3,2,1,0:T(8,128)(2,1)S(1)}, bf16[8,2,8,1024]{3,2,1,0:T(8,128)(2,1)S(1)}, u32[]{:S(2)}, u32[]{:S(2)}) collective-permute-start(bf16[8,2,8,1024]{3,2,1,0:T(8,128)(2,1)S(1)} %stack.1.refs_0_), channel_id=1, source_target_pairs={{0,8},{8,16},{16,24},{24,0},{1,9},{9,17},{17,25},{25,1},{2,10},{10... | collective-permute-start | bytes 786440 | tf_op jit(solution)/shard_map/ppermute | solution.py:147
  95.3 2.4 %collective-permute-start.18 = (bf16[8,2,8,1024]{3,2,1,0:T(8,128)(2,1)S(1)}, bf16[8,2,8,1024]{3,2,1,0:T(8,128)(2,1)S(1)}, u32[]{:S(2)}, u32[]{:S(2)}) collective-permute-start(bf16[8,2,8,1024]{3,2,1,0:T(8,128)(2,1)S(1)} %stack.1.refs_0_), channel_id=1, source_target_pairs={{0,16},{8,24},{16,0},{24,8},{1,17},{9,25},{17,1},{25,9},{2,18},{10... | collective-permute-start | bytes 786440 | tf_op jit(solution)/shard_map/ppermute | solution.py:147
  97.7 1.6 %collective-permute-start.17 = (bf16[8,2,8,1024]{3,2,1,0:T(8,128)(2,1)S(1)}, bf16[8,2,8,1024]{3,2,1,0:T(8,128)(2,1)S(1)}, u32[]{:S(2)}, u32[]{:S(2)}) collective-permute-start(bf16[8,2,8,1024]{3,2,1,0:T(8,128)(2,1)S(1)} %stack.1.refs_0_), channel_id=1, source_target_pairs={{0,24},{8,0},{16,8},{24,16},{1,25},{9,1},{17,9},{25,17},{2,26},{10... | collective-permute-start | bytes 786440 | tf_op jit(solution)/shard_map/ppermute | solution.py:147
  99.3 5.1 %combine.1.comb_ref = bf16[2,1024,256]{2,1,0:T(8,128)(2,1)} custom-call(bf16[2,1024,1024]{2,1,0:T(8,128)(2,1)} %refs_0_.3, bf16[1024,256]{1,0:T(8,128)(2,1)} %refs_1_.3, f32[2,8,256]{2,1,0:T(8,128)} %get-tuple-element.18.refs_2_), custom_call_target="tpu_custom_call" | custom-call | flops 1073741824 | bytes 5242880 | tf_op jit(solution)/shard_map/combine/pallas_call | solution.py:164
  104.4 2.8 %collective-permute-done.18.refs_2_ = bf16[8,2,8,1024]{3,2,1,0:T(8,128)(2,1)S(1)} collective-permute-done((bf16[8,2,8,1024]{3,2,1,0:T(8,128)(2,1)S(1)}, bf16[8,2,8,1024]{3,2,1,0:T(8,128)(2,1)S(1)}, u32[]{:S(2)}, u32[]{:S(2)}) %collective-permute-start.18) | collective-permute-done | bytes 262176 | tf_op jit(solution)/shard_map/ppermute | solution.py:147
  107.4 1.2 %copy-done = bf16[2,1024,256]{2,1,0:T(8,128)(2,1)S(1)} copy-done((bf16[2,1024,256]{2,1,0:T(8,128)(2,1)S(1)}, bf16[2,1024,256]{2,1,0:T(8,128)(2,1)}, u32[]{:S(2)}) %copy-start) | copy-done | bytes 1048600
  108.7 3.4 %mix.1 = bf16[2,1024,1024]{2,1,0:T(8,128)(2,1)} custom-call(bf16[2,1024,256]{2,1,0:T(8,128)(2,1)S(1)} %copy-done, bf16[8,2,8,1024]{3,2,1,0:T(8,128)(2,1)S(1)} %stack.1.refs_0_, bf16[8,2,8,1024]{3,2,1,0:T(8,128)(2,1)S(1)} %collective-permute-done.17.refs_1_, bf16[8,2,8,1024]{3,2,1,0:T(8,128)(2,1)S(1)} %collective-permute-done.18.refs_2_, ...), custom_call_target="tpu_custom_call" | custom-call | tf_op jit(solution)/shard_map/mix/pallas_call | solution.py:223
  (26 shorter events, 2.7 us)
Async XLA Ops:
  0.0 62.9 %copy-start.2 = (bf16[1024,1024]{1,0:T(8,128)(2,1)S(1)}, bf16[1024,1024]{1,0:T(8,128)(2,1)}, u32[]{:S(2)}) copy-start(bf16[1024,1024]{1,0:T(8,128)(2,1)} %down_ref.1) | copy-start | bytes 6291460
  0.0 62.9 %copy-start.1 = (bf16[1024,1024]{1,0:T(8,128)(2,1)S(1)}, bf16[1024,1024]{1,0:T(8,128)(2,1)}, u32[]{:S(2)}) copy-start(bf16[1024,1024]{1,0:T(8,128)(2,1)} %up_ref.1) | copy-start | bytes 6291460
  8.3 10.2 %collective-permute-start = (bf16[8,2,8,1152]{3,2,1,0:T(8,128)(2,1)}, bf16[8,2,8,1152]{3,2,1,0:T(8,128)(2,1)S(1)}, u32[]{:S(2)}, u32[]{:S(2)}) collective-permute-start(bf16[8,2,8,1152]{3,2,1,0:T(8,128)(2,1)} %get-tuple-element.20), channel_id=1, source_target_pairs={{0,8},{8,16},{16,24},{24,0},{1,9},{9,17},{17,25},{25,1},{2,10},{10... | collective-permute-start | bytes 884744 | tf_op jit(solution)/shard_map/ppermute | solution.py:147
  9.9 16.1 %collective-permute-start.1 = (bf16[8,2,8,1152]{3,2,1,0:T(8,128)(2,1)}, bf16[8,2,8,1152]{3,2,1,0:T(8,128)(2,1)S(1)}, u32[]{:S(2)}, u32[]{:S(2)}) collective-permute-start(bf16[8,2,8,1152]{3,2,1,0:T(8,128)(2,1)} %get-tuple-element.21), channel_id=1, source_target_pairs={{0,16},{8,24},{16,0},{24,8},{1,17},{9,25},{17,1},{25,9},{2,18},{10... | collective-permute-start | bytes 884744 | tf_op jit(solution)/shard_map/ppermute | solution.py:147
  12.8 13.2 %collective-permute-start.2 = (bf16[8,2,8,1152]{3,2,1,0:T(8,128)(2,1)}, bf16[8,2,8,1152]{3,2,1,0:T(8,128)(2,1)S(1)}, u32[]{:S(2)}, u32[]{:S(2)}) collective-permute-start(bf16[8,2,8,1152]{3,2,1,0:T(8,128)(2,1)} %get-tuple-element.22), channel_id=1, source_target_pairs={{0,24},{8,0},{16,8},{24,16},{1,25},{9,1},{17,9},{25,17},{2,26},{10... | collective-permute-start | bytes 884744 | tf_op jit(solution)/shard_map/ppermute | solution.py:147
  26.0 1.0 copy-start.3
  27.6 14.8 %collective-permute-start.3 = (bf16[2,8,1152]{2,1,0:T(8,128)(2,1)S(1)}, bf16[2,8,1152]{2,1,0:T(8,128)(2,1)S(1)}, u32[]{:S(2)}, u32[]{:S(2)}) collective-permute-start(bf16[2,8,1152]{2,1,0:T(8,128)(2,1)S(1)} %get-tuple-element.24), channel_id=1, source_target_pairs={{0,1},{1,2},{2,3},{3,4},{4,5},{5,6},{6,7},{7,0},{8,9},{9,10},{10,1... | collective-permute-start | bytes 110600 | tf_op jit(solution)/shard_map/ppermute | solution.py:147
  29.6 15.5 %collective-permute-start.4 = (bf16[2,8,1152]{2,1,0:T(8,128)(2,1)S(1)}, bf16[2,8,1152]{2,1,0:T(8,128)(2,1)S(1)}, u32[]{:S(2)}, u32[]{:S(2)}) collective-permute-start(bf16[2,8,1152]{2,1,0:T(8,128)(2,1)S(1)} %get-tuple-element.25), channel_id=1, source_target_pairs={{0,2},{1,3},{2,4},{3,5},{4,6},{5,7},{6,0},{7,1},{8,10},{9,11},{10,... | collective-permute-start | bytes 110600 | tf_op jit(solution)/shard_map/ppermute | solution.py:147
  32.9 13.2 %collective-permute-start.5 = (bf16[2,8,1152]{2,1,0:T(8,128)(2,1)S(1)}, bf16[2,8,1152]{2,1,0:T(8,128)(2,1)S(1)}, u32[]{:S(2)}, u32[]{:S(2)}) collective-permute-start(bf16[2,8,1152]{2,1,0:T(8,128)(2,1)S(1)} %get-tuple-element.26), channel_id=1, source_target_pairs={{0,3},{1,4},{2,5},{3,6},{4,7},{5,0},{6,1},{7,2},{8,11},{9,12},{10,... | collective-permute-start | bytes 110600 | tf_op jit(solution)/shard_map/ppermute | solution.py:147
  36.9 9.2 %collective-permute-start.6 = (bf16[2,8,1152]{2,1,0:T(8,128)(2,1)S(1)}, bf16[2,8,1152]{2,1,0:T(8,128)(2,1)S(1)}, u32[]{:S(2)}, u32[]{:S(2)}) collective-permute-start(bf16[2,8,1152]{2,1,0:T(8,128)(2,1)S(1)} %get-tuple-element.27), channel_id=1, source_target_pairs={{0,4},{1,5},{2,6},{3,7},{4,0},{5,1},{6,2},{7,3},{8,12},{9,13},{10,... | collective-permute-start | bytes 110600 | tf_op jit(solution)/shard_map/ppermute | solution.py:147
  37.4 8.6 %collective-permute-start.7 = (bf16[2,8,1152]{2,1,0:T(8,128)(2,1)S(1)}, bf16[2,8,1152]{2,1,0:T(8,128)(2,1)S(1)}, u32[]{:S(2)}, u32[]{:S(2)}) collective-permute-start(bf16[2,8,1152]{2,1,0:T(8,128)(2,1)S(1)} %get-tuple-element.28), channel_id=1, source_target_pairs={{0,5},{1,6},{2,7},{3,0},{4,1},{5,2},{6,3},{7,4},{8,13},{9,14},{10,... | collective-permute-start | bytes 110600 | tf_op jit(solution)/shard_map/ppermute | solution.py:147
  42.4 5.2 %collective-permute-start.8 = (bf16[2,8,1152]{2,1,0:T(8,128)(2,1)S(1)}, bf16[2,8,1152]{2,1,0:T(8,128)(2,1)S(1)}, u32[]{:S(2)}, u32[]{:S(2)}) collective-permute-start(bf16[2,8,1152]{2,1,0:T(8,128)(2,1)S(1)} %get-tuple-element.29), channel_id=1, source_target_pairs={{0,6},{1,7},{2,0},{3,1},{4,2},{5,3},{6,4},{7,5},{8,14},{9,15},{10,... | collective-permute-start | bytes 110600 | tf_op jit(solution)/shard_map/ppermute | solution.py:147
  45.0 4.0 %collective-permute-start.9 = (bf16[2,8,1152]{2,1,0:T(8,128)(2,1)S(1)}, bf16[2,8,1152]{2,1,0:T(8,128)(2,1)S(1)}, u32[]{:S(2)}, u32[]{:S(2)}) collective-permute-start(bf16[2,8,1152]{2,1,0:T(8,128)(2,1)S(1)} %get-tuple-element.30), channel_id=1, source_target_pairs={{0,7},{1,0},{2,1},{3,2},{4,3},{5,4},{6,5},{7,6},{8,15},{9,8},{10,9... | collective-permute-start | bytes 110600 | tf_op jit(solution)/shard_map/ppermute | solution.py:147
  76.5 11.1 %collective-permute-start.16 = (bf16[2,8,1024]{2,1,0:T(8,128)(2,1)S(1)}, bf16[2,8,1024]{2,1,0:T(8,128)(2,1)S(1)}, u32[]{:S(2)}, u32[]{:S(2)}) collective-permute-start(bf16[2,8,1024]{2,1,0:T(8,128)(2,1)S(1)} %total.1.refs_0_), channel_id=1, source_target_pairs={{0,1},{1,2},{2,3},{3,4},{4,5},{5,6},{6,7},{7,0},{8,9},{9,10},{10,1... | collective-permute-start | bytes 98312 | tf_op jit(solution)/shard_map/ppermute | solution.py:147
  76.8 13.3 %collective-permute-start.15 = (bf16[2,8,1024]{2,1,0:T(8,128)(2,1)S(1)}, bf16[2,8,1024]{2,1,0:T(8,128)(2,1)S(1)}, u32[]{:S(2)}, u32[]{:S(2)}) collective-permute-start(bf16[2,8,1024]{2,1,0:T(8,128)(2,1)S(1)} %total.1.refs_0_), channel_id=1, source_target_pairs={{0,2},{1,3},{2,4},{3,5},{4,6},{5,7},{6,0},{7,1},{8,10},{9,11},{10,... | collective-permute-start | bytes 98312 | tf_op jit(solution)/shard_map/ppermute | solution.py:147
  78.6 13.4 %collective-permute-start.14 = (bf16[2,8,1024]{2,1,0:T(8,128)(2,1)S(1)}, bf16[2,8,1024]{2,1,0:T(8,128)(2,1)S(1)}, u32[]{:S(2)}, u32[]{:S(2)}) collective-permute-start(bf16[2,8,1024]{2,1,0:T(8,128)(2,1)S(1)} %total.1.refs_0_), channel_id=1, source_target_pairs={{0,3},{1,4},{2,5},{3,6},{4,7},{5,0},{6,1},{7,2},{8,11},{9,12},{10,... | collective-permute-start | bytes 98312 | tf_op jit(solution)/shard_map/ppermute | solution.py:147
  81.7 10.3 %collective-permute-start.13 = (bf16[2,8,1024]{2,1,0:T(8,128)(2,1)S(1)}, bf16[2,8,1024]{2,1,0:T(8,128)(2,1)S(1)}, u32[]{:S(2)}, u32[]{:S(2)}) collective-permute-start(bf16[2,8,1024]{2,1,0:T(8,128)(2,1)S(1)} %total.1.refs_0_), channel_id=1, source_target_pairs={{0,4},{1,5},{2,6},{3,7},{4,0},{5,1},{6,2},{7,3},{8,12},{9,13},{10,... | collective-permute-start | bytes 98312 | tf_op jit(solution)/shard_map/ppermute | solution.py:147
  83.6 8.4 %collective-permute-start.12 = (bf16[2,8,1024]{2,1,0:T(8,128)(2,1)S(1)}, bf16[2,8,1024]{2,1,0:T(8,128)(2,1)S(1)}, u32[]{:S(2)}, u32[]{:S(2)}) collective-permute-start(bf16[2,8,1024]{2,1,0:T(8,128)(2,1)S(1)} %total.1.refs_0_), channel_id=1, source_target_pairs={{0,5},{1,6},{2,7},{3,0},{4,1},{5,2},{6,3},{7,4},{8,13},{9,14},{10,... | collective-permute-start | bytes 98312 | tf_op jit(solution)/shard_map/ppermute | solution.py:147
  87.7 5.0 %collective-permute-start.11 = (bf16[2,8,1024]{2,1,0:T(8,128)(2,1)S(1)}, bf16[2,8,1024]{2,1,0:T(8,128)(2,1)S(1)}, u32[]{:S(2)}, u32[]{:S(2)}) collective-permute-start(bf16[2,8,1024]{2,1,0:T(8,128)(2,1)S(1)} %total.1.refs_0_), channel_id=1, source_target_pairs={{0,6},{1,7},{2,0},{3,1},{4,2},{5,3},{6,4},{7,5},{8,14},{9,15},{10,... | collective-permute-start | bytes 98312 | tf_op jit(solution)/shard_map/ppermute | solution.py:147
  90.1 3.9 %collective-permute-start.10 = (bf16[2,8,1024]{2,1,0:T(8,128)(2,1)S(1)}, bf16[2,8,1024]{2,1,0:T(8,128)(2,1)S(1)}, u32[]{:S(2)}, u32[]{:S(2)}) collective-permute-start(bf16[2,8,1024]{2,1,0:T(8,128)(2,1)S(1)} %total.1.refs_0_), channel_id=1, source_target_pairs={{0,7},{1,0},{2,1},{3,2},{4,3},{5,4},{6,5},{7,6},{8,15},{9,8},{10,9... | collective-permute-start | bytes 98312 | tf_op jit(solution)/shard_map/ppermute | solution.py:147
  94.0 10.4 %collective-permute-start.19 = (bf16[8,2,8,1024]{3,2,1,0:T(8,128)(2,1)S(1)}, bf16[8,2,8,1024]{3,2,1,0:T(8,128)(2,1)S(1)}, u32[]{:S(2)}, u32[]{:S(2)}) collective-permute-start(bf16[8,2,8,1024]{3,2,1,0:T(8,128)(2,1)S(1)} %stack.1.refs_0_), channel_id=1, source_target_pairs={{0,8},{8,16},{16,24},{24,0},{1,9},{9,17},{17,25},{25,1},{2,10},{10... | collective-permute-start | bytes 786440 | tf_op jit(solution)/shard_map/ppermute | solution.py:147
  95.3 11.9 %collective-permute-start.18 = (bf16[8,2,8,1024]{3,2,1,0:T(8,128)(2,1)S(1)}, bf16[8,2,8,1024]{3,2,1,0:T(8,128)(2,1)S(1)}, u32[]{:S(2)}, u32[]{:S(2)}) collective-permute-start(bf16[8,2,8,1024]{3,2,1,0:T(8,128)(2,1)S(1)} %stack.1.refs_0_), channel_id=1, source_target_pairs={{0,16},{8,24},{16,0},{24,8},{1,17},{9,25},{17,1},{25,9},{2,18},{10... | collective-permute-start | bytes 786440 | tf_op jit(solution)/shard_map/ppermute | solution.py:147
  97.7 9.7 %collective-permute-start.17 = (bf16[8,2,8,1024]{3,2,1,0:T(8,128)(2,1)S(1)}, bf16[8,2,8,1024]{3,2,1,0:T(8,128)(2,1)S(1)}, u32[]{:S(2)}, u32[]{:S(2)}) collective-permute-start(bf16[8,2,8,1024]{3,2,1,0:T(8,128)(2,1)S(1)} %stack.1.refs_0_), channel_id=1, source_target_pairs={{0,24},{8,0},{16,8},{24,16},{1,25},{9,1},{17,9},{25,17},{2,26},{10... | collective-permute-start | bytes 786440 | tf_op jit(solution)/shard_map/ppermute | solution.py:147
  107.4 1.2 %copy-start = (bf16[2,1024,256]{2,1,0:T(8,128)(2,1)S(1)}, bf16[2,1024,256]{2,1,0:T(8,128)(2,1)}, u32[]{:S(2)}) copy-start(bf16[2,1024,256]{2,1,0:T(8,128)(2,1)} %combine.1.comb_ref) | copy-start | bytes 3145732

commit v2 on v0

v2 whole, which is shorter than its diff:
```python
import functools

import jax
import jax.numpy as jnp
from jax import lax
from jax.experimental import pallas as pl
from jax.experimental.pallas import tpu as pltpu
from jax.sharding import Mesh
from jax.sharding import PartitionSpec as P

F32 = jnp.float32
BF16 = jnp.bfloat16
SLOT_P = 4
STAT = 128
STEPS = 4
MIB = 1 << 20
BIG = 52
ROWS = (((1,), (1,)), ((), ()))


def vmem():
    return pl.BlockSpec(memory_space=pltpu.VMEM)


def params(mib=48):
    return pltpu.CompilerParams(vmem_limit_bytes=mib * MIB)


def name(f, *a):
    def body(*refs):
        f(*a, *refs)

    return body


def first_member(group, nz):
    return group % 2 * (nz // 2)


def device_order(slot_params, groups, ny, nz):
    slots = slot_params.shape[1]
    row = lax.broadcasted_iota(jnp.int32, (slots, 1), 0)
    at_y = (row // (nz * groups) + lax.axis_index("y")) % ny
    at_z = (row // groups + first_member(lax.axis_index("group"), nz)) % nz
    slot = (row % groups * ny + at_y) * nz + at_z
    perm = (lax.broadcasted_iota(jnp.int32, (slots, slots), 1) == slot).astype(F32).astype(BF16)
    return lax.dot_general(perm, slot_params, ROWS, preferred_element_type=F32).astype(BF16)


def pack(lse):
    hi = lse.astype(BF16).astype(F32)
    mid = (lse - hi).astype(BF16).astype(F32)
    low = lse - hi - mid
    lane = lax.broadcasted_iota(jnp.int32, lse.shape[:-1] + (STAT,), lse.ndim - 1)
    return jnp.where(lane == 0, hi, jnp.where(lane == 1, mid, jnp.where(lane == 2, low, 0.0)))


def gather_kernel(clip, groups, ny, nz, tok_hbm, sp_ref, *refs):
    out_refs, refs = refs[:ny], refs[ny:]
    tok_ref, logit_ref, sems = refs[-3:]
    rows = tok_ref.shape[0] // STEPS
    copies = []
    for i in range(STEPS):
        part = pl.ds(i * rows, rows)
        copies.append(pltpu.make_async_copy(tok_hbm.at[clip, part], tok_ref.at[part], sems.at[i]))
        copies[-1].start()
    if len(refs) == 4:
        refs[0][...] = device_order(sp_ref[...], groups, ny, nz)
        sp_ref = refs[0]
    for i in range(STEPS):
        copies[i].wait()
        part = slice(i * rows, (i + 1) * rows)
        logit_ref[:, part] = lax.dot_general(sp_ref[...], tok_ref[part], ROWS, preferred_element_type=F32)
    logits = logit_ref[...]
    peak = jnp.max(logits, axis=1, keepdims=True)
    spread = jnp.exp(logits - peak)
    total = jnp.sum(spread, axis=1, keepdims=True)
    summed = jnp.dot(spread.astype(BF16), tok_ref[...], preferred_element_type=F32)
    wide = jnp.concatenate([summed * (1.0 / total), pack(peak + jnp.log(total))], axis=1)
    wide = wide.reshape(ny, nz, groups, wide.shape[1]).astype(BF16)
    for i in range(ny):
        out_refs[i][...] = wide[i]


def combine_kernel(tok_ref, sp_ref, after_ref, out_ref, tick_ref):
    logits = lax.dot_general(tok_ref[0], sp_ref[...], ROWS, preferred_element_type=F32)
    spread = jnp.exp(logits - jnp.max(logits, axis=1, keepdims=True))
    out_ref[0] = (spread * (1.0 / jnp.sum(spread, axis=1, keepdims=True))).astype(BF16)
    tick_ref[...] = jnp.zeros_like(tick_ref)


def merged(width, wides):
    lses = []
    for wide in wides:
        stat = wide[..., width:].astype(F32)
        lses.append(stat[..., 0:1] + stat[..., 1:2] + stat[..., 2:3])
    peak = functools.reduce(jnp.maximum, lses)
    weights = [jnp.exp(lse - peak) for lse in lses]
    total = sum(weights)
    mean = sum(wide[..., :width].astype(F32) * (w / total) for wide, w in zip(wides, weights))
    return mean, peak + jnp.log(total)


def halfway_kernel(width, ny, *refs):
    in_refs, out_ref = refs[:-1], refs[-1]
    for k in range(out_ref.shape[0]):
        for c in range(out_ref.shape[1]):
            mean, lse = merged(width, [r[k] for r in in_refs[c * ny : (c + 1) * ny]])
            out_ref[k, c] = jnp.concatenate([mean, pack(lse)], axis=-1).astype(BF16)


def merge_kernel(width, in_ref, after_ref, out_ref):
    nz, clips, groups = in_ref.shape[:3]
    acc, _ = merged(width, [in_ref[k] for k in range(nz)])
    for g in range(groups):
        rows = jnp.concatenate([acc[c, g : g + 1] for c in range(clips)], axis=0).astype(BF16)
        for q in range(SLOT_P):
            out_ref[g * SLOT_P + q] = rows


def expert_kernel(x_ref, up_ref, down_ref, out_ref):
    parts, clips, width = x_ref.shape
    x = x_ref[...].astype(F32).reshape(parts * clips, width).astype(BF16)
    hidden = jax.nn.gelu(jnp.dot(x, up_ref[...], preferred_element_type=F32)).astype(BF16)
    out = jnp.dot(hidden, down_ref[...], preferred_element_type=F32)
    out_ref[...] = out.reshape(parts, clips, width).astype(BF16)


def total_kernel(x_ref, out_ref):
    parts, clips, width = x_ref.shape
    x = x_ref[...].astype(F32).reshape(parts // SLOT_P, SLOT_P, clips, width)
    total = jnp.sum(x, axis=1)
    for c in range(clips):
        rows = jnp.concatenate([total[g, c : c + 1] for g in range(parts // SLOT_P)], axis=0).astype(BF16)
        for k in range(out_ref.shape[0]):
            out_ref[k, c] = rows


def split_kernel(in_ref, *out_refs):
    nz, _, groups, width = in_ref.shape
    for c, ref in enumerate(out_refs):
        ref[...] = in_ref[:, c].astype(F32).reshape(nz * groups, width).astype(BF16)


def mix_kernel(ny, *refs):
    comb_ref, slot_refs, (out_ref, held) = refs[0], refs[1 : 1 + ny], refs[-2:]
    rows = slot_refs[0].shape[0]

    @pl.when(pl.program_id(0) == 0)
    def _():
        for i, r in enumerate(slot_refs):
            held[i * rows : (i + 1) * rows] = r[...]

    out_ref[0] = jnp.dot(comb_ref[0], held[...], preferred_element_type=F32).astype(BF16)


def shards(tokens, slot_params, w_up, w_down):
    clips, length, width = tokens.shape
    slots = slot_params.shape[1]
    groups = lax.axis_size("group")
    around = ("zh", "quarter")
    ny, nz = lax.axis_size("y"), lax.axis_size(around)
    sharers = ("group", "quarter")
    wide = width + STAT

    def shift(x, k):
        return lax.ppermute(x, "y", [(i, (i + k) % ny) for i in range(ny)])

    everyone = ("group", "y") + around
    starts = [g * ny * nz + y * nz for g in range(groups) for y in range(ny)]
    order = [[first_member(s // (ny * nz), nz) + j for j in range(nz)] for s in starts]
    circles = [[s + j % nz for j in o] for s, o in zip(starts, order)]

    def exchange_z(x):
        return lax.all_to_all(x, everyone, 0, 0, axis_index_groups=circles, tiled=True)

    def small(kernel, out, label, *operands):
        return pl.pallas_call(
            kernel,
            in_specs=[vmem()] * len(operands),
            out_specs=jax.tree.map(lambda _: vmem(), out),
            out_shape=out,
            compiler_params=params(),
            name=label,
        )(*operands)

    def gather(clip, sp):
        extra = [jax.ShapeDtypeStruct((slots, width), BF16)] if clip == 0 else []
        return pl.pallas_call(
            name(gather_kernel, clip, groups, ny, nz),
            in_specs=[pl.BlockSpec(memory_space=pl.ANY), vmem()],
            out_specs=[vmem()] * (ny + len(extra)),
            out_shape=[jax.ShapeDtypeStruct((nz, groups, wide), BF16)] * ny + extra,
            scratch_shapes=[
                pltpu.VMEM((length, width), BF16),
                pltpu.VMEM((slots, length), F32),
                pltpu.SemaphoreType.DMA((STEPS,)),
            ],
            compiler_params=params(BIG + 1 if clip == 0 else BIG),
            cost_estimate=pl.CostEstimate(
                flops=4 * length * width * slots,
                bytes_accessed=2 * length * width,
                transcendentals=length * slots,
            ),
            name=f"gather{clip}",
        )(tokens, sp)

    arrived = []
    ordered = slot_params
    for clip in range(clips):
        means = gather(clip, ordered)
        if clip == 0:
            ordered = means[ny]
        arrived += [means[0]] + [shift(means[k], k) for k in range(1, ny)]
    halfway = small(
        name(halfway_kernel, width, ny),
        jax.ShapeDtypeStruct((nz, clips, groups, wide), BF16),
        "halfway",
        *arrived,
    )
    arrived = exchange_z(halfway)
    half = length // 2
    combine, tick = pl.pallas_call(
        combine_kernel,
        grid=(clips, 2),
        in_specs=[
            pl.BlockSpec((1, half, width), lambda c, t: (c, t, 0)),
            pl.BlockSpec((slots, width), lambda c, t: (0, 0)),
            pl.BlockSpec((1, 1, groups, STAT), lambda c, t: (0, 0, 0, 0)),
        ],
        out_specs=[
            pl.BlockSpec((1, half, slots), lambda c, t: (c, t, 0)),
            pl.BlockSpec((8, STAT), lambda c, t: (0, 0)),
        ],
        out_shape=[
            jax.ShapeDtypeStruct((clips, length, slots), BF16),
            jax.ShapeDtypeStruct((8, STAT), F32),
        ],
        compiler_params=params(BIG),
        cost_estimate=pl.CostEstimate(
            flops=2 * clips * length * width * slots,
            bytes_accessed=2 * clips * length * (width + slots),
            transcendentals=clips * length * slots,
        ),
        name="combine",
    )(tokens, ordered, halfway)
    rows = jax.ShapeDtypeStruct((groups * SLOT_P, clips, width), BF16)
    slot_in = small(name(merge_kernel, width), rows, "merge", arrived, tick)
    own = lax.all_to_all(slot_in, sharers, 0, 0, tiled=True)
    partial = small(expert_kernel, rows, "expert", own, w_up, w_down)
    back = lax.all_to_all(partial, sharers, 0, 0, tiled=True)
    slot_out = small(
        total_kernel, jax.ShapeDtypeStruct((nz, clips, groups, width), BF16), "total", back
    )
    ring = exchange_z(slot_out)
    own = small(
        split_kernel, [jax.ShapeDtypeStruct((nz * groups, width), BF16)] * clips, "split", ring
    )
    above0, below1 = shift(own[0], -1), shift(own[1], 1)
    below0, above1 = shift(own[0], 1), shift(own[1], -1)
    far0, far1 = shift(above0, -1), shift(below1, 1)
    rings = [[own[0], above0, far0, below0], [own[1], above1, far1, below1]]
    steps = 2
    mixed = None
    for clip in range(clips):
        before = [] if mixed is None else [mixed]
        mixed = pl.pallas_call(
            name(mix_kernel, ny),
            grid=(steps,),
            in_specs=[pl.BlockSpec((1, length // steps, slots), lambda t, c=clip: (c, t, 0))]
            + [pl.BlockSpec((nz * groups, width), lambda t: (0, 0))] * ny
            + [pl.BlockSpec(memory_space=pl.ANY) for _ in before],
            out_specs=pl.BlockSpec((1, length // steps, width), lambda t, c=clip: (c, t, 0)),
            out_shape=jax.ShapeDtypeStruct((clips, length, width), BF16),
            scratch_shapes=[pltpu.VMEM((slots, width), BF16)],
            input_output_aliases={1 + ny: 0} if before else {},
            compiler_params=params(),
            cost_estimate=pl.CostEstimate(
                flops=2 * length * width * slots,
                bytes_accessed=2 * length * (width + slots),
                transcendentals=0,
            ),
            name=f"mix{clip}",
        )(combine, *rings[clip], *before)
    return mixed


def solution(mesh):
    groups, n = mesh.devices.shape
    split = Mesh(mesh.devices.reshape(groups, 4, n // (4 * SLOT_P), SLOT_P), ("group", "y", "zh", "quarter"))
    seq = ("y", "zh", "quarter")
    everyone = ("group",) + seq
    placed = (P("group", seq, None), P(), P(None, everyone), P(everyone, None))
    return jax.shard_map(
        shards, mesh=split, in_specs=placed, out_specs=P("group", seq, None), check_vma=False
    )
```

time: 477 us -> 110 us (0.23)
  blocking collectives: 312 us -> 38.8 us
  waiting for transfers between devices: 103 us -> 18.7 us
  matrix products: 21.3 us -> 0 us
  Pallas kernels: 0 us -> 19.6 us
  starting transfers between devices: 9.73 us -> 28.2 us
  between operations: 13.5 us -> 0.07 us
  other arithmetic: 8.52 us -> 0 us
    psum x2 -> x0, blocking collectives: 235 us -> none  [the longest x1 165 us: shards(): expert_out = lax.psum(partial_out, 'seq').astype(jnp.bfloat16)]
    pmax x1 -> x0, blocking collectives: 77.9 us -> none  [shards(): col_peak = lax.pmax(jnp.max(logits, axis=1), 'seq')]
    psum x1 -> x0, waiting for transfers between devices: 76.7 us -> none  [shards(): total_in, col_total = lax.psum((partial_in, col_local), 'seq')]
    all_to_all x0 -> x3, blocking collectives: none -> 38.8 us  [the longest x1 13.6 us: exchange_z(): lax.all_to_all(x, everyone, 0, 0, axis_index_groups=circles, tiled=True)]
    dot_general x4 -> x0, matrix products: 21.3 us -> none  [the longest x1 8.36 us: shards(): jnp.einsum('cts,csd->ctd', combine, returned, preferred_element_type=jnp....]
    all_to_all x2 -> x1, waiting for transfers between devices: 26.2 us -> 6.28 us  [exchange_z(): lax.all_to_all(x, everyone, 0, 0, axis_index_groups=circles, tiled=True)]
    ppermute x0 -> x12, starting transfers between devices: none -> 19.8 us  [shift(): return lax.ppermute(x, 'y', [(i, (i + k) % ny) for i in range(ny)])]
    pallas_call x0 -> x10, Pallas kernels: none -> 19.6 us  [the longest x2 8.42 us: gather(): pl.pallas_call(name(gather_kernel, clip, groups, ny, nz), in_specs=[pl.Bl...]
  transfers between devices with their start and end apart: 3 -> 13, of which waited for: 3 -> 7; matrix products, arithmetic and copies ran while one was open for 1% -> 0% of each run, Pallas kernels for 0% -> 9%
where the time goes in v2:
time: 110 us
  blocking collectives  38.8 us (35%)
  starting transfers between devices  28.2 us (26%)
  Pallas kernels  19.6 us (18%)
  waiting for transfers between devices  18.7 us (17%)
  local copies, waits for them, and re-layouts  4.23 us (4%)
    ppermute x12, starting transfers between devices, shift(): return lax.ppermute(x, 'y', [(i, (i + k) % ny) for i in range(ny)])  19.8 us
    all_to_all x1, blocking collectives, exchange_z(): lax.all_to_all(x, everyone, 0, 0, axis_index_groups=circles, tiled=True)  13.6 us
    all_to_all x1, blocking collectives, shards(): own = lax.all_to_all(slot_in, sharers, 0, 0, tiled=True)  12.7 us
    all_to_all x1, blocking collectives, shards(): back = lax.all_to_all(partial, sharers, 0, 0, tiled=True)  12.5 us
    ppermute x12, waiting for transfers between devices, shift(): return lax.ppermute(x, 'y', [(i, (i + k) % ny) for i in range(ny)])  12.5 us
    all_to_all x1, starting transfers between devices, exchange_z(): lax.all_to_all(x, everyone, 0, 0, axis_index_groups=circles, tiled=True)  8.46 us
    pallas_call x2, Pallas kernels, gather(): pl.pallas_call(name(gather_kernel, clip, groups, ny, nz), in_specs=[pl.Bl...  8.42 us
    all_to_all x1, waiting for transfers between devices, exchange_z(): lax.all_to_all(x, everyone, 0, 0, axis_index_groups=circles, tiled=True)  6.28 us
  transfers between devices with their start and end apart: 13, of which 7 were waited for; matrix products, arithmetic and copies ran while one was open for 0% of the time, Pallas kernels for 9%

profile of v2, /device:TPU:2, one launch (start us, length us, event | category | flops | bytes accessed | tf_op | source)
XLA Modules:
  0.0 109.7 jit_solution(6676030230251864918)
XLA Ops:
  0.0 4.7 %gather0.1 = (bf16[8,8,1152]{2,1,0:T(8,128)(2,1)S(1)}, bf16[8,8,1152]{2,1,0:T(8,128)(2,1)S(1)}, bf16[8,8,1152]{2,1,0:T(8,128)(2,1)S(1)}, bf16[8,8,1152]{2,1,0:T(8,128)(2,1)S(1)}, bf16[256,1024]{1,0:T(8,128)(2,1)}) custom-call(bf16[2,1024,1024]{2,1,0:T(8,128)(2,1)} %tok_ref.1, bf16[1024,256]{1,0:T(8,128)(2,1)} %refs_1_.1), custom_call_target="tpu_custom_call" | custom-call | flops 1073741824 | bytes 2097152 | tf_op jit(solution)/shard_map/gather0/pallas_call | solution.py:189
  4.7 1.7 %collective-permute-start = (bf16[8,8,1152]{2,1,0:T(8,128)(2,1)S(1)}, bf16[8,8,1152]{2,1,0:T(8,128)(2,1)S(1)}, u32[]{:S(2)}, u32[]{:S(2)}) collective-permute-start(bf16[8,8,1152]{2,1,0:T(8,128)(2,1)S(1)} %get-tuple-element.20), channel_id=1, source_target_pairs={{0,8},{8,16},{16,24},{24,0},{1,9},{9,17},{17,25},{25,1},{2,10},{10... | collective-permute-start | bytes 442376 | tf_op jit(solution)/shard_map/ppermute | solution.py:167
  6.4 2.9 %collective-permute-start.1 = (bf16[8,8,1152]{2,1,0:T(8,128)(2,1)S(1)}, bf16[8,8,1152]{2,1,0:T(8,128)(2,1)S(1)}, u32[]{:S(2)}, u32[]{:S(2)}) collective-permute-start(bf16[8,8,1152]{2,1,0:T(8,128)(2,1)S(1)} %get-tuple-element.21), channel_id=1, source_target_pairs={{0,16},{8,24},{16,0},{24,8},{1,17},{9,25},{17,1},{25,9},{2,18},{10... | collective-permute-start | bytes 442376 | tf_op jit(solution)/shard_map/ppermute | solution.py:167
  9.3 1.3 %collective-permute-start.2 = (bf16[8,8,1152]{2,1,0:T(8,128)(2,1)S(1)}, bf16[8,8,1152]{2,1,0:T(8,128)(2,1)S(1)}, u32[]{:S(2)}, u32[]{:S(2)}) collective-permute-start(bf16[8,8,1152]{2,1,0:T(8,128)(2,1)S(1)} %get-tuple-element.22), channel_id=1, source_target_pairs={{0,24},{8,0},{16,8},{24,16},{1,25},{9,1},{17,9},{25,17},{2,26},{10... | collective-permute-start | bytes 442376 | tf_op jit(solution)/shard_map/ppermute | solution.py:167
  10.6 1.0 copy-done
  11.7 3.7 %gather1.1 = (bf16[8,8,1152]{2,1,0:T(8,128)(2,1)S(1)}, bf16[8,8,1152]{2,1,0:T(8,128)(2,1)S(1)}, bf16[8,8,1152]{2,1,0:T(8,128)(2,1)S(1)}, bf16[8,8,1152]{2,1,0:T(8,128)(2,1)S(1)}) custom-call(bf16[2,1024,1024]{2,1,0:T(8,128)(2,1)} %tok_ref.1, bf16[256,1024]{1,0:T(8,128)(2,1)S(1)} %copy-done), custom_call_target="tpu_custom_call" | custom-call | flops 1073741824 | bytes 2097152 | tf_op jit(solution)/shard_map/gather1/pallas_call | solution.py:189
  15.4 0.8 collective-permute-start.3
  16.1 0.8 collective-permute-start.4
  16.9 2.0 %collective-permute-start.5 = (bf16[8,8,1152]{2,1,0:T(8,128)(2,1)S(1)}, bf16[8,8,1152]{2,1,0:T(8,128)(2,1)S(1)}, u32[]{:S(2)}, u32[]{:S(2)}) collective-permute-start(bf16[8,8,1152]{2,1,0:T(8,128)(2,1)S(1)} %get-tuple-element.26), channel_id=1, source_target_pairs={{0,24},{8,0},{16,8},{24,16},{1,25},{9,1},{17,9},{25,17},{2,26},{10... | collective-permute-start | bytes 442376 | tf_op jit(solution)/shard_map/ppermute | solution.py:167
  18.9 5.7 %collective-permute-done.3.refs_5_ = bf16[8,8,1152]{2,1,0:T(8,128)(2,1)S(1)} collective-permute-done((bf16[8,8,1152]{2,1,0:T(8,128)(2,1)S(1)}, bf16[8,8,1152]{2,1,0:T(8,128)(2,1)S(1)}, u32[]{:S(2)}, u32[]{:S(2)}) %collective-permute-start.3) | collective-permute-done | bytes 147488 | tf_op jit(solution)/shard_map/ppermute | solution.py:167
  24.6 0.6 collective-permute-done.5.refs_7_
  25.2 1.5 %halfway.1.after_ref = bf16[8,2,8,1152]{3,2,1,0:T(8,128)(2,1)} custom-call(bf16[8,8,1152]{2,1,0:T(8,128)(2,1)S(1)} %get-tuple-element.19.refs_0_, bf16[8,8,1152]{2,1,0:T(8,128)(2,1)S(1)} %collective-permute-done.refs_1_, bf16[8,8,1152]{2,1,0:T(8,128)(2,1)S(1)} %collective-permute-done.1.refs_2_, bf16[8,8,1152]{2,1,0:T(8,128)(2,1)S(1)} %collective-permute-done.2.refs_3_, ...), custom_call_target="tpu_custom_call" | custom-call | tf_op jit(solution)/shard_map/halfway/pallas_call | solution.py:178
  26.7 8.5 %all-to-all-start = ((bf16[8,2,8,1152]{3,2,1,0:T(8,128)(2,1)}), bf16[8,2,8,1152]{3,2,1,0:T(8,128)(2,1)S(1)}, u32[]{:S(2)}, u32[]{:S(2)}) async-start(bf16[8,2,8,1152]{3,2,1,0:T(8,128)(2,1)} %halfway.1.after_ref), calls=%async_computation | async-start | bytes 589824 | tf_op jit(solution)/shard_map/all_to_all | solution.py:175
  35.2 4.5 %combine.1 = (bf16[2,1024,256]{2,1,0:T(8,128)(2,1)S(1)}, f32[8,128]{1,0:T(8,128)S(1)}) custom-call(bf16[2,1024,1024]{2,1,0:T(8,128)(2,1)} %tok_ref.1, bf16[256,1024]{1,0:T(8,128)(2,1)S(1)} %copy-done.1, bf16[8,2,8,1152]{3,2,1,0:T(8,128)(2,1)} %halfway.1.after_ref), custom_call_target="tpu_custom_call" | custom-call | flops 1073741824 | bytes 5242880 | tf_op jit(solution)/shard_map/combine/pallas_call | solution.py:223
  39.7 6.3 %all-to-all-done.refs_0_ = bf16[8,2,8,1152]{3,2,1,0:T(8,128)(2,1)S(1)} async-done(((bf16[8,2,8,1152]{3,2,1,0:T(8,128)(2,1)}), bf16[8,2,8,1152]{3,2,1,0:T(8,128)(2,1)S(1)}, u32[]{:S(2)}, u32[]{:S(2)}) %all-to-all-start) | async-done | bytes 294944 | tf_op jit(solution)/shard_map/all_to_all | solution.py:175
  46.0 0.3 merge.1
  46.3 12.7 %all_to_all.20.x_ref = bf16[32,2,1024]{2,1,0:T(2,128)(2,1)S(1)} all-to-all(bf16[32,2,1024]{2,1,0:T(2,128)(2,1)S(1)} %merge.1), channel_id=1, replica_groups=mesh['group'=8,'y'=4,'zh'=2,'quarter'=4] {'group','quarter'}, dimensions={0} | all-to-all | bytes 262144 | tf_op jit(solution)/shard_map/all_to_all | solution.py:249
  59.0 1.6 %copy-done.2 = bf16[1024,1024]{1,0:T(8,128)(2,1)S(1)} copy-done((bf16[1024,1024]{1,0:T(8,128)(2,1)S(1)}, bf16[1024,1024]{1,0:T(8,128)(2,1)}, u32[]{:S(2)}) %copy-start.2) | copy-done | bytes 2097176
  60.6 1.6 %copy-done.3 = bf16[1024,1024]{1,0:T(8,128)(2,1)S(1)} copy-done((bf16[1024,1024]{1,0:T(8,128)(2,1)S(1)}, bf16[1024,1024]{1,0:T(8,128)(2,1)}, u32[]{:S(2)}) %copy-start.3) | copy-done | bytes 2097176
  62.1 1.0 expert.1
  63.1 12.5 %all_to_all.21.x_ref = bf16[32,2,1024]{2,1,0:T(2,128)(2,1)S(1)} all-to-all(bf16[32,2,1024]{2,1,0:T(2,128)(2,1)S(1)} %expert.1), channel_id=1, replica_groups=mesh['group'=8,'y'=4,'zh'=2,'quarter'=4] {'group','quarter'}, dimensions={0} | all-to-all | bytes 262144 | tf_op jit(solution)/shard_map/all_to_all | solution.py:251
  75.7 0.1 total.1
  75.8 13.6 %all_to_all.22.in_ref = bf16[8,2,8,1024]{3,2,1,0:T(8,128)(2,1)S(1)} all-to-all(bf16[8,2,8,1024]{3,2,1,0:T(8,128)(2,1)S(1)} %total.1), channel_id=1, replica_groups={{0,1,2,3,4,5,6,7},{8,9,10,11,12,13,14,15},{16,17,18,19,20,21,22,23},{24..., dimensions={0} | all-to-all | bytes 524288 | tf_op jit(solution)/shard_map/all_to_all | solution.py:175
  89.4 4.6 %collective-permute-start.9 = (bf16[64,1024]{1,0:T(8,128)(2,1)S(1)}, bf16[64,1024]{1,0:T(8,128)(2,1)S(1)}, u32[]{:S(2)}, u32[]{:S(2)}) collective-permute-start(bf16[64,1024]{1,0:T(8,128)(2,1)S(1)} %get-tuple-element.30.refs_1_), channel_id=1, source_target_pairs={{0,24},{8,0},{16,8},{24,16},{1,25},{9,1},{17,9},{25,17},{2,26},{10... | collective-permute-start | bytes 393224 | tf_op jit(solution)/shard_map/ppermute | solution.py:167
  94.0 3.9 %collective-permute-done.9.refs_2_ = bf16[64,1024]{1,0:T(8,128)(2,1)S(1)} collective-permute-done((bf16[64,1024]{1,0:T(8,128)(2,1)S(1)}, bf16[64,1024]{1,0:T(8,128)(2,1)S(1)}, u32[]{:S(2)}, u32[]{:S(2)}) %collective-permute-start.9) | collective-permute-done | bytes 131104 | tf_op jit(solution)/shard_map/ppermute | solution.py:167
  97.9 3.7 %collective-permute-start.10 = (bf16[64,1024]{1,0:T(8,128)(2,1)S(1)}, bf16[64,1024]{1,0:T(8,128)(2,1)S(1)}, u32[]{:S(2)}, u32[]{:S(2)}) collective-permute-start(bf16[64,1024]{1,0:T(8,128)(2,1)S(1)} %collective-permute-done.9.refs_2_), channel_id=1, source_target_pairs={{0,24},{8,0},{16,8},{24,16},{1,25},{9,1},{17,9},{25,17},{2,26},{10... | collective-permute-start | bytes 393224 | tf_op jit(solution)/shard_map/ppermute | solution.py:167
  101.6 2.0 %collective-permute-start.8 = (bf16[64,1024]{1,0:T(8,128)(2,1)S(1)}, bf16[64,1024]{1,0:T(8,128)(2,1)S(1)}, u32[]{:S(2)}, u32[]{:S(2)}) collective-permute-start(bf16[64,1024]{1,0:T(8,128)(2,1)S(1)} %collective-permute-done.7.refs_4_), channel_id=1, source_target_pairs={{0,8},{8,16},{16,24},{24,0},{1,9},{9,17},{17,25},{25,1},{2,10},{10... | collective-permute-start | bytes 393224 | tf_op jit(solution)/shard_map/ppermute | solution.py:167
  103.6 0.5 collective-permute-done.10.refs_3_
  104.1 1.9 %mix0.1.refs_5_ = bf16[2,1024,1024]{2,1,0:T(8,128)(2,1)} custom-call(bf16[2,1024,256]{2,1,0:T(8,128)(2,1)S(1)} %get-tuple-element.27.refs_0_, bf16[64,1024]{1,0:T(8,128)(2,1)S(1)} %get-tuple-element.30.refs_1_, bf16[64,1024]{1,0:T(8,128)(2,1)S(1)} %collective-permute-done.9.refs_2_, bf16[64,1024]{1,0:T(8,128)(2,1)S(1)} %collective-permute-done.10.refs_3_, ...), custom_call_target="tpu_custom_call" | custom-call | flops 536870912 | bytes 2621440 | tf_op jit(solution)/shard_map/mix0/pallas_call | solution.py:267
  106.0 0.5 collective-permute-done.6.refs_2_
  106.5 1.2 %collective-permute-done.8.refs_3_ = bf16[64,1024]{1,0:T(8,128)(2,1)S(1)} collective-permute-done((bf16[64,1024]{1,0:T(8,128)(2,1)S(1)}, bf16[64,1024]{1,0:T(8,128)(2,1)S(1)}, u32[]{:S(2)}, u32[]{:S(2)}) %collective-permute-start.8) | collective-permute-done | bytes 131104 | tf_op jit(solution)/shard_map/ppermute | solution.py:167
  107.8 1.9 %mix1.1 = bf16[2,1024,1024]{2,1,0:T(8,128)(2,1)} custom-call(bf16[2,1024,256]{2,1,0:T(8,128)(2,1)S(1)} %get-tuple-element.27.refs_0_, bf16[64,1024]{1,0:T(8,128)(2,1)S(1)} %get-tuple-element.29.refs_1_, bf16[64,1024]{1,0:T(8,128)(2,1)S(1)} %collective-permute-done.6.refs_2_, ...), custom_call_target="tpu_custom_call", output_to_operand_aliasing={{}: (5, {})} | custom-call | flops 536870912 | bytes 2621440 | tf_op jit(solution)/shard_map/mix1/pallas_call | solution.py:267
  (15 shorter events, 0.1 us)
Async XLA Ops:
  4.7 12.2 %collective-permute-start = (bf16[8,8,1152]{2,1,0:T(8,128)(2,1)S(1)}, bf16[8,8,1152]{2,1,0:T(8,128)(2,1)S(1)}, u32[]{:S(2)}, u32[]{:S(2)}) collective-permute-start(bf16[8,8,1152]{2,1,0:T(8,128)(2,1)S(1)} %get-tuple-element.20), channel_id=1, source_target_pairs={{0,8},{8,16},{16,24},{24,0},{1,9},{9,17},{17,25},{25,1},{2,10},{10... | collective-permute-start | bytes 442376 | tf_op jit(solution)/shard_map/ppermute | solution.py:167
  6.4 12.6 %collective-permute-start.1 = (bf16[8,8,1152]{2,1,0:T(8,128)(2,1)S(1)}, bf16[8,8,1152]{2,1,0:T(8,128)(2,1)S(1)}, u32[]{:S(2)}, u32[]{:S(2)}) collective-permute-start(bf16[8,8,1152]{2,1,0:T(8,128)(2,1)S(1)} %get-tuple-element.21), channel_id=1, source_target_pairs={{0,16},{8,24},{16,0},{24,8},{1,17},{9,25},{17,1},{25,9},{2,18},{10... | collective-permute-start | bytes 442376 | tf_op jit(solution)/shard_map/ppermute | solution.py:167
  9.3 9.7 %collective-permute-start.2 = (bf16[8,8,1152]{2,1,0:T(8,128)(2,1)S(1)}, bf16[8,8,1152]{2,1,0:T(8,128)(2,1)S(1)}, u32[]{:S(2)}, u32[]{:S(2)}) collective-permute-start(bf16[8,8,1152]{2,1,0:T(8,128)(2,1)S(1)} %get-tuple-element.22), channel_id=1, source_target_pairs={{0,24},{8,0},{16,8},{24,16},{1,25},{9,1},{17,9},{25,17},{2,26},{10... | collective-permute-start | bytes 442376 | tf_op jit(solution)/shard_map/ppermute | solution.py:167
  10.6 1.0 copy-start
  11.7 23.5 %copy-start.1 = (bf16[256,1024]{1,0:T(8,128)(2,1)S(1)}, bf16[256,1024]{1,0:T(8,128)(2,1)}, u32[]{:S(2)}) copy-start(bf16[256,1024]{1,0:T(8,128)(2,1)} %get-tuple-element.18.refs_1_.sp_ref) | copy-start | bytes 1572868
  15.4 9.2 %collective-permute-start.3 = (bf16[8,8,1152]{2,1,0:T(8,128)(2,1)S(1)}, bf16[8,8,1152]{2,1,0:T(8,128)(2,1)S(1)}, u32[]{:S(2)}, u32[]{:S(2)}) collective-permute-start(bf16[8,8,1152]{2,1,0:T(8,128)(2,1)S(1)} %get-tuple-element.24), channel_id=1, source_target_pairs={{0,8},{8,16},{16,24},{24,0},{1,9},{9,17},{17,25},{25,1},{2,10},{10... | collective-permute-start | bytes 442376 | tf_op jit(solution)/shard_map/ppermute | solution.py:167
  16.1 8.4 %collective-permute-start.4 = (bf16[8,8,1152]{2,1,0:T(8,128)(2,1)S(1)}, bf16[8,8,1152]{2,1,0:T(8,128)(2,1)S(1)}, u32[]{:S(2)}, u32[]{:S(2)}) collective-permute-start(bf16[8,8,1152]{2,1,0:T(8,128)(2,1)S(1)} %get-tuple-element.25), channel_id=1, source_target_pairs={{0,16},{8,24},{16,0},{24,8},{1,17},{9,25},{17,1},{25,9},{2,18},{10... | collective-permute-start | bytes 442376 | tf_op jit(solution)/shard_map/ppermute | solution.py:167
  16.9 8.3 %collective-permute-start.5 = (bf16[8,8,1152]{2,1,0:T(8,128)(2,1)S(1)}, bf16[8,8,1152]{2,1,0:T(8,128)(2,1)S(1)}, u32[]{:S(2)}, u32[]{:S(2)}) collective-permute-start(bf16[8,8,1152]{2,1,0:T(8,128)(2,1)S(1)} %get-tuple-element.26), channel_id=1, source_target_pairs={{0,24},{8,0},{16,8},{24,16},{1,25},{9,1},{17,9},{25,17},{2,26},{10... | collective-permute-start | bytes 442376 | tf_op jit(solution)/shard_map/ppermute | solution.py:167
  26.7 19.3 %all-to-all-start = ((bf16[8,2,8,1152]{3,2,1,0:T(8,128)(2,1)}), bf16[8,2,8,1152]{3,2,1,0:T(8,128)(2,1)S(1)}, u32[]{:S(2)}, u32[]{:S(2)}) async-start(bf16[8,2,8,1152]{3,2,1,0:T(8,128)(2,1)} %halfway.1.after_ref), calls=%async_computation | async-start | bytes 589824 | tf_op jit(solution)/shard_map/all_to_all | solution.py:175
  59.0 1.6 %copy-start.2 = (bf16[1024,1024]{1,0:T(8,128)(2,1)S(1)}, bf16[1024,1024]{1,0:T(8,128)(2,1)}, u32[]{:S(2)}) copy-start(bf16[1024,1024]{1,0:T(8,128)(2,1)} %up_ref.1) | copy-start | bytes 6291460
  60.5 1.6 %copy-start.3 = (bf16[1024,1024]{1,0:T(8,128)(2,1)S(1)}, bf16[1024,1024]{1,0:T(8,128)(2,1)}, u32[]{:S(2)}) copy-start(bf16[1024,1024]{1,0:T(8,128)(2,1)} %down_ref.1) | copy-start | bytes 6291460
  89.4 8.5 %collective-permute-start.9 = (bf16[64,1024]{1,0:T(8,128)(2,1)S(1)}, bf16[64,1024]{1,0:T(8,128)(2,1)S(1)}, u32[]{:S(2)}, u32[]{:S(2)}) collective-permute-start(bf16[64,1024]{1,0:T(8,128)(2,1)S(1)} %get-tuple-element.30.refs_1_), channel_id=1, source_target_pairs={{0,24},{8,0},{16,8},{24,16},{1,25},{9,1},{17,9},{25,17},{2,26},{10... | collective-permute-start | bytes 393224 | tf_op jit(solution)/shard_map/ppermute | solution.py:167
  94.0 7.6 %collective-permute-start.7 = (bf16[64,1024]{1,0:T(8,128)(2,1)S(1)}, bf16[64,1024]{1,0:T(8,128)(2,1)S(1)}, u32[]{:S(2)}, u32[]{:S(2)}) collective-permute-start(bf16[64,1024]{1,0:T(8,128)(2,1)S(1)} %get-tuple-element.29.refs_1_), channel_id=1, source_target_pairs={{0,8},{8,16},{16,24},{24,0},{1,9},{9,17},{17,25},{25,1},{2,10},{10... | collective-permute-start | bytes 393224 | tf_op jit(solution)/shard_map/ppermute | solution.py:167
  94.0 9.6 %collective-permute-start.11 = (bf16[64,1024]{1,0:T(8,128)(2,1)S(1)}, bf16[64,1024]{1,0:T(8,128)(2,1)S(1)}, u32[]{:S(2)}, u32[]{:S(2)}) collective-permute-start(bf16[64,1024]{1,0:T(8,128)(2,1)S(1)} %get-tuple-element.30.refs_1_), channel_id=1, source_target_pairs={{0,8},{8,16},{16,24},{24,0},{1,9},{9,17},{17,25},{25,1},{2,10},{10... | collective-permute-start | bytes 393224 | tf_op jit(solution)/shard_map/ppermute | solution.py:167
  97.9 6.2 %collective-permute-start.10 = (bf16[64,1024]{1,0:T(8,128)(2,1)S(1)}, bf16[64,1024]{1,0:T(8,128)(2,1)S(1)}, u32[]{:S(2)}, u32[]{:S(2)}) collective-permute-start(bf16[64,1024]{1,0:T(8,128)(2,1)S(1)} %collective-permute-done.9.refs_2_), channel_id=1, source_target_pairs={{0,24},{8,0},{16,8},{24,16},{1,25},{9,1},{17,9},{25,17},{2,26},{10... | collective-permute-start | bytes 393224 | tf_op jit(solution)/shard_map/ppermute | solution.py:167
  101.6 5.0 %collective-permute-start.6 = (bf16[64,1024]{1,0:T(8,128)(2,1)S(1)}, bf16[64,1024]{1,0:T(8,128)(2,1)S(1)}, u32[]{:S(2)}, u32[]{:S(2)}) collective-permute-start(bf16[64,1024]{1,0:T(8,128)(2,1)S(1)} %get-tuple-element.29.refs_1_), channel_id=1, source_target_pairs={{0,24},{8,0},{16,8},{24,16},{1,25},{9,1},{17,9},{25,17},{2,26},{10... | collective-permute-start | bytes 393224 | tf_op jit(solution)/shard_map/ppermute | solution.py:167
  101.6 6.2 %collective-permute-start.8 = (bf16[64,1024]{1,0:T(8,128)(2,1)S(1)}, bf16[64,1024]{1,0:T(8,128)(2,1)S(1)}, u32[]{:S(2)}, u32[]{:S(2)}) collective-permute-start(bf16[64,1024]{1,0:T(8,128)(2,1)S(1)} %collective-permute-done.7.refs_4_), channel_id=1, source_target_pairs={{0,8},{8,16},{16,24},{24,0},{1,9},{9,17},{17,25},{25,1},{2,10},{10... | collective-permute-start | bytes 393224 | tf_op jit(solution)/shard_map/ppermute | solution.py:167

commit v3 on v2

v3 whole, which is shorter than its diff:
```python
import functools

import jax
import jax.numpy as jnp
from jax import lax
from jax.experimental import pallas as pl
from jax.experimental.pallas import tpu as pltpu
from jax.sharding import Mesh
from jax.sharding import PartitionSpec as P

F32 = jnp.float32
BF16 = jnp.bfloat16
SLOT_P = 4
STAT = 128
STEPS = 4
MIB = 1 << 20
BIG = 52


def vmem():
    return pl.BlockSpec(memory_space=pltpu.VMEM)


def anywhere():
    return pl.BlockSpec(memory_space=pl.ANY)


def params(mib=48):
    return pltpu.CompilerParams(vmem_limit_bytes=mib * MIB)


def name(f, *a):
    def body(*refs):
        f(*a, *refs)

    return body


def device_order(slot_params, groups, ny, nz):
    slots = slot_params.shape[1]
    col = lax.broadcasted_iota(jnp.int32, (1, slots), 1)
    at_y = (col // (nz * groups) + lax.axis_index("y")) % ny
    slot = (col % groups * ny + at_y) * nz + col // groups % nz
    perm = (lax.broadcasted_iota(jnp.int32, (slots, slots), 0) == slot).astype(F32).astype(BF16)
    return jnp.dot(slot_params, perm, preferred_element_type=F32).astype(BF16)


def pack(lse):
    hi = lse.astype(BF16).astype(F32)
    mid = (lse - hi).astype(BF16).astype(F32)
    low = lse - hi - mid
    lane = lax.broadcasted_iota(jnp.int32, lse.shape[:-1] + (STAT,), lse.ndim - 1)
    return jnp.where(lane == 0, hi, jnp.where(lane == 1, mid, jnp.where(lane == 2, low, 0.0)))


def gather_kernel(clip, groups, ny, nz, tok_hbm, sp_ref, *refs):
    out_refs, refs = refs[:ny], refs[ny:]
    ordered_ref, tok_ref, logit_ref, sems = refs[-4:]
    rows = tok_ref.shape[0] // STEPS
    copies = []
    first = pltpu.make_async_copy(sp_ref, ordered_ref, sems.at[STEPS])
    first.start()
    for i in range(STEPS):
        part = pl.ds(i * rows, rows)
        copies.append(pltpu.make_async_copy(tok_hbm.at[clip, part], tok_ref.at[part], sems.at[i]))
        copies[-1].start()
    first.wait()
    if clip == 0:
        refs[0][...] = device_order(ordered_ref[...], groups, ny, nz)
        ordered_ref = refs[0]
    peak = None
    for i in range(STEPS):
        copies[i].wait()
        part = slice(i * rows, (i + 1) * rows)
        logits = jnp.dot(tok_ref[part], ordered_ref[...], preferred_element_type=F32)
        logit_ref[part] = logits
        top = jnp.max(logits, axis=0, keepdims=True)
        peak = top if peak is None else jnp.maximum(peak, top)
    spread = jnp.exp(logit_ref[...] - peak)
    total = jnp.sum(spread, axis=0, keepdims=True)
    summed = lax.dot_general(
        spread.astype(BF16), tok_ref[...], (((0,), (0,)), ((), ())), preferred_element_type=F32
    )
    slots = total.shape[1]
    cols = jnp.concatenate([1.0 / total, peak + jnp.log(total), jnp.zeros((6, slots), F32)], axis=0).T
    wide = jnp.concatenate([summed * cols[:, 0:1], pack(cols[:, 1:2])], axis=1)
    wide = wide.reshape(ny, nz, groups, wide.shape[1]).astype(BF16)
    for i in range(ny):
        out_refs[i][...] = wide[i]


def combine_kernel(tok_ref, sp_ref, after_ref, out_ref, tick_ref):
    logits = jnp.dot(tok_ref[0], sp_ref[...], preferred_element_type=F32)
    spread = jnp.exp(logits - jnp.max(logits, axis=1, keepdims=True))
    out_ref[0] = (spread * (1.0 / jnp.sum(spread, axis=1, keepdims=True))).astype(BF16)
    tick_ref[...] = jnp.zeros_like(tick_ref)


def merged(width, wides):
    lses = []
    for wide in wides:
        stat = wide[..., width:].astype(F32)
        lses.append(stat[..., 0:1] + stat[..., 1:2] + stat[..., 2:3])
    peak = functools.reduce(jnp.maximum, lses)
    weights = [jnp.exp(lse - peak) for lse in lses]
    total = sum(weights)
    mean = sum(wide[..., :width].astype(F32) * (w / total) for wide, w in zip(wides, weights))
    return mean, peak + jnp.log(total)


def halfway_kernel(width, *refs):
    in_refs, out_ref = refs[:-2], refs[-1]
    for k in range(out_ref.shape[0]):
        mean, lse = merged(width, [r[k] for r in in_refs])
        out_ref[k] = jnp.concatenate([mean, pack(lse)], axis=-1).astype(BF16)


def both_kernel(width, *refs):
    in_refs, first_ref, out_ref = refs[:-2], refs[-2], refs[-1]
    for k in range(out_ref.shape[0]):
        out_ref[k, 0] = first_ref[k]
        mean, lse = merged(width, [r[k] for r in in_refs])
        out_ref[k, 1] = jnp.concatenate([mean, pack(lse)], axis=-1).astype(BF16)


def merge_kernel(width, in_ref, out_ref):
    nz, clips, groups = in_ref.shape[:3]
    acc, _ = merged(width, [in_ref[k] for k in range(nz)])
    for g in range(groups):
        rows = jnp.concatenate([acc[c, g : g + 1] for c in range(clips)], axis=0).astype(BF16)
        for q in range(SLOT_P):
            out_ref[g * SLOT_P + q] = rows


def expert_kernel(x_ref, up_ref, down_ref, out_ref):
    parts, clips, width = x_ref.shape
    x = x_ref[...].astype(F32).reshape(parts * clips, width).astype(BF16)
    hidden = jax.nn.gelu(jnp.dot(x, up_ref[...], preferred_element_type=F32)).astype(BF16)
    out = jnp.dot(hidden, down_ref[...], preferred_element_type=F32)
    out_ref[...] = out.reshape(parts, clips, width).astype(BF16)


def total_kernel(x_ref, out_ref):
    parts, clips, width = x_ref.shape
    x = x_ref[...].astype(F32).reshape(parts // SLOT_P, SLOT_P, clips, width)
    total = jnp.sum(x, axis=1)
    for c in range(clips):
        rows = jnp.concatenate([total[g, c : c + 1] for g in range(parts // SLOT_P)], axis=0).astype(BF16)
        for k in range(out_ref.shape[0]):
            out_ref[k, c] = rows


def split_kernel(in_ref, *out_refs):
    nz, _, groups, width = in_ref.shape
    for c, ref in enumerate(out_refs):
        ref[...] = in_ref[:, c].astype(F32).reshape(nz * groups, width).astype(BF16)


def mix_kernel(clip, ny, comb_ref, *refs):
    slot_refs, (out_hbm, held, buf, sems) = refs[:ny], refs[-4:]
    rows = slot_refs[0].shape[0]
    for i, r in enumerate(slot_refs):
        held[i * rows : (i + 1) * rows] = r[...]
    step = buf.shape[0] // STEPS
    copies = []
    for i in range(STEPS):
        part = pl.ds(i * step, step)
        buf[part] = jnp.dot(comb_ref[clip, part], held[...], preferred_element_type=F32).astype(BF16)
        copies.append(pltpu.make_async_copy(buf.at[part], out_hbm.at[clip, part], sems.at[i]))
        copies[-1].start()
    for copy in copies:
        copy.wait()


def shards(tokens, slot_params, w_up, w_down):
    clips, length, width = tokens.shape
    slots = slot_params.shape[1]
    groups = lax.axis_size("group")
    around = ("zh", "quarter")
    ny, nz = lax.axis_size("y"), lax.axis_size(around)
    sharers = ("group", "quarter")
    wide = width + STAT

    def shift(x, k):
        return lax.ppermute(x, "y", [(i, (i + k) % ny) for i in range(ny)])

    def small(kernel, out, label, *operands):
        return pl.pallas_call(
            kernel,
            in_specs=[vmem()] * len(operands),
            out_specs=jax.tree.map(lambda _: vmem(), out),
            out_shape=out,
            compiler_params=params(),
            name=label,
        )(*operands)

    def gather(clip, sp):
        extra = [jax.ShapeDtypeStruct((width, slots), BF16)] if clip == 0 else []
        return pl.pallas_call(
            name(gather_kernel, clip, groups, ny, nz),
            in_specs=[anywhere(), anywhere()],
            out_specs=[vmem()] * (ny + len(extra)),
            out_shape=[jax.ShapeDtypeStruct((nz, groups, wide), BF16)] * ny + extra,
            scratch_shapes=[
                pltpu.VMEM((width, slots), BF16),
                pltpu.VMEM((length, width), BF16),
                pltpu.VMEM((length, slots), F32),
                pltpu.SemaphoreType.DMA((STEPS + 1,)),
            ],
            compiler_params=params(BIG + 1),
            cost_estimate=pl.CostEstimate(
                flops=4 * length * width * slots,
                bytes_accessed=2 * length * width,
                transcendentals=length * slots,
            ),
            name=f"gather{clip}",
        )(tokens, sp)

    arrived = []
    ordered = slot_params
    for clip in range(clips):
        means = gather(clip, ordered)
        if clip == 0:
            ordered = means[ny]
        arrived += [means[0]] + [shift(means[k], k) for k in range(1, ny)]
    half = length // 2
    combine, tick = pl.pallas_call(
        combine_kernel,
        grid=(clips, 2),
        in_specs=[
            pl.BlockSpec((1, half, width), lambda c, t: (c, t, 0)),
            pl.BlockSpec((width, slots), lambda c, t: (0, 0)),
            pl.BlockSpec((1, groups, STAT), lambda c, t: (0, 0, 0)),
        ],
        out_specs=[
            pl.BlockSpec((1, half, slots), lambda c, t: (c, t, 0)),
            pl.BlockSpec((8, STAT), lambda c, t: (0, 0)),
        ],
        out_shape=[
            jax.ShapeDtypeStruct((clips, length, slots), BF16),
            jax.ShapeDtypeStruct((8, STAT), F32),
        ],
        compiler_params=params(BIG),
        cost_estimate=pl.CostEstimate(
            flops=2 * clips * length * width * slots,
            bytes_accessed=2 * clips * length * (width + slots),
            transcendentals=clips * length * slots,
        ),
        name="combine",
    )(tokens, ordered, arrived[-ny])
    assert clips == 2
    halfway = small(
        name(halfway_kernel, width),
        jax.ShapeDtypeStruct((nz, groups, wide), BF16),
        "halfway",
        *arrived[:ny],
        tick,
    )
    halfway = small(
        name(both_kernel, width),
        jax.ShapeDtypeStruct((nz, clips, groups, wide), BF16),
        "both",
        *arrived[ny:],
        halfway,
    )
    arrived = lax.all_to_all(halfway, around, 0, 0, tiled=True)
    rows = jax.ShapeDtypeStruct((groups * SLOT_P, clips, width), BF16)
    slot_in = small(name(merge_kernel, width), rows, "merge", arrived)
    own = lax.all_to_all(slot_in, sharers, 0, 0, tiled=True)
    partial = small(expert_kernel, rows, "expert", own, w_up, w_down)
    back = lax.all_to_all(partial, sharers, 0, 0, tiled=True)
    slot_out = small(
        total_kernel, jax.ShapeDtypeStruct((nz, clips, groups, width), BF16), "total", back
    )
    ring = lax.all_to_all(slot_out, around, 0, 0, tiled=True)
    rings = small(
        split_kernel, [jax.ShapeDtypeStruct((nz * groups, width), BF16)] * clips, "split", ring
    )
    rings = [[ring] + [shift(ring, -k) for k in range(1, ny)] for ring in rings]
    mixed = None
    for clip in range(clips):
        before = [] if mixed is None else [mixed]
        mixed = pl.pallas_call(
            name(mix_kernel, clip, ny),
            in_specs=[vmem()] * (1 + ny) + [anywhere() for _ in before],
            out_specs=anywhere(),
            out_shape=jax.ShapeDtypeStruct((clips, length, width), BF16),
            scratch_shapes=[
                pltpu.VMEM((slots, width), BF16),
                pltpu.VMEM((length, width), BF16),
                pltpu.SemaphoreType.DMA((STEPS,)),
            ],
            input_output_aliases={1 + ny: 0} if before else {},
            compiler_params=params(),
            cost_estimate=pl.CostEstimate(
                flops=2 * length * width * slots,
                bytes_accessed=2 * length * (width + slots),
                transcendentals=0,
            ),
            name=f"mix{clip}",
        )(combine, *rings[clip], *before)
    return mixed


def solution(mesh):
    groups, n = mesh.devices.shape
    split = Mesh(mesh.devices.reshape(groups, 4, n // (4 * SLOT_P), SLOT_P), ("group", "y", "zh", "quarter"))
    seq = ("y", "zh", "quarter")
    everyone = ("group",) + seq
    placed = (P("group", seq, None), P(), P(None, everyone), P(everyone, None))
    return jax.shard_map(
        shards, mesh=split, in_specs=placed, out_specs=P("group", seq, None), check_vma=False
    )
```

time: 110 us -> 103 us (0.936)
  blocking collectives: 38.8 us -> 59.9 us
  waiting for transfers between devices: 18.7 us -> 6.63 us
  starting transfers between devices: 28.2 us -> 17.3 us
  local copies, waits for them, and re-layouts: 4.23 us -> 0.02 us
  Pallas kernels: 19.6 us -> 17.5 us
    all_to_all x1 -> x2, blocking collectives: 13.6 us -> 34.7 us  [the longest x1 19.1 us: shards(): arrived = lax.all_to_all(halfway, around, 0, 0, tiled=True)]
    all_to_all x1 -> x0, starting transfers between devices: 8.46 us -> none  [exchange_z(): lax.all_to_all(x, everyone, 0, 0, axis_index_groups=circles, tiled=True)]
    all_to_all x1 -> x0, waiting for transfers between devices: 6.28 us -> none  [exchange_z(): lax.all_to_all(x, everyone, 0, 0, axis_index_groups=circles, tiled=True)]
    ppermute x12, waiting for transfers between devices: 12.5 us -> 6.63 us  [shift(): return lax.ppermute(x, 'y', [(i, (i + k) % ny) for i in range(ny)])]
    unnamed x8 -> x6, local copies, waits for them, and re-layouts: 4.23 us -> 0.02 us
    ppermute x12, starting transfers between devices: 19.8 us -> 17.3 us  [shift(): return lax.ppermute(x, 'y', [(i, (i + k) % ny) for i in range(ny)])]
    pallas_call x4, Pallas kernels: 12.2 us -> 11.1 us  [the longest x2 7.8 us: gather(): pl.pallas_call(name(gather_kernel, clip, groups, ny, nz), in_specs=[anywh...]
    pallas_call x5 -> x6, Pallas kernels: 2.86 us -> 1.95 us  [small(): pl.pallas_call(kernel, in_specs=[vmem()] * len(operands), out_specs=jax.t...]
  transfers between devices with their start and end apart: 13 -> 12, of which waited for: 7 -> 6; matrix products, arithmetic and copies ran while one was open for 0% -> 0% of each run, Pallas kernels for 9% -> 10%
where the time goes in v3:
time: 103 us; the launch traced here: 102 us
  blocking collectives  59.9 us (58%)
  Pallas kernels  17.5 us (17%)
  starting transfers between devices  17.3 us (17%)
  waiting for transfers between devices  6.63 us (6%)
    all_to_all x1, blocking collectives, shards(): arrived = lax.all_to_all(halfway, around, 0, 0, tiled=True)  19.1 us
    ppermute x12, starting transfers between devices, shift(): return lax.ppermute(x, 'y', [(i, (i + k) % ny) for i in range(ny)])  17.3 us
    all_to_all x1, blocking collectives, shards(): ring = lax.all_to_all(slot_out, around, 0, 0, tiled=True)  15.6 us
    all_to_all x1, blocking collectives, shards(): own = lax.all_to_all(slot_in, sharers, 0, 0, tiled=True)  12.7 us
    all_to_all x1, blocking collectives, shards(): back = lax.all_to_all(partial, sharers, 0, 0, tiled=True)  12.5 us
    pallas_call x2, Pallas kernels, gather(): pl.pallas_call(name(gather_kernel, clip, groups, ny, nz), in_specs=[anywh...  7.8 us
    ppermute x12, waiting for transfers between devices, shift(): return lax.ppermute(x, 'y', [(i, (i + k) % ny) for i in range(ny)])  6.63 us
    pallas_call x1, Pallas kernels, shards(): pl.pallas_call(combine_kernel, grid=(clips, 2), in_specs=[pl.BlockSpec((1...  4.41 us
  transfers between devices with their start and end apart: 12, of which 6 were waited for; matrix products, arithmetic and copies ran while one was open for 0% of the time, Pallas kernels for 10%

profile of v3, /device:TPU:2, one launch (start us, length us, event | category | flops | bytes accessed | tf_op | source)
XLA Modules:
  0.0 101.7 jit_solution(3611749207610737667)
XLA Ops:
  0.0 4.0 %gather0.1 = (bf16[8,8,1152]{2,1,0:T(8,128)(2,1)S(1)}, bf16[8,8,1152]{2,1,0:T(8,128)(2,1)S(1)}, bf16[8,8,1152]{2,1,0:T(8,128)(2,1)S(1)}, bf16[8,8,1152]{2,1,0:T(8,128)(2,1)S(1)}, bf16[1024,256]{1,0:T(8,128)(2,1)}) custom-call(bf16[2,1024,1024]{2,1,0:T(8,128)(2,1)} %tok_ref.1, bf16[1024,256]{1,0:T(8,128)(2,1)} %refs_1_.1), custom_call_target="tpu_custom_call" | custom-call | flops 1073741824 | bytes 2097152 | tf_op jit(solution)/shard_map/gather0/pallas_call | solution.py:199
  4.0 0.0 copy-start
  4.0 1.7 %collective-permute-start.3 = (bf16[8,8,1152]{2,1,0:T(8,128)(2,1)S(1)}, bf16[8,8,1152]{2,1,0:T(8,128)(2,1)S(1)}, u32[]{:S(2)}, u32[]{:S(2)}) collective-permute-start(bf16[8,8,1152]{2,1,0:T(8,128)(2,1)S(1)} %get-tuple-element.25), channel_id=1, source_target_pairs={{0,8},{8,16},{16,24},{24,0},{1,9},{9,17},{17,25},{25,1},{2,10},{10... | collective-permute-start | bytes 442376 | tf_op jit(solution)/shard_map/ppermute | solution.py:185
  5.7 2.9 %collective-permute-start.4 = (bf16[8,8,1152]{2,1,0:T(8,128)(2,1)S(1)}, bf16[8,8,1152]{2,1,0:T(8,128)(2,1)S(1)}, u32[]{:S(2)}, u32[]{:S(2)}) collective-permute-start(bf16[8,8,1152]{2,1,0:T(8,128)(2,1)S(1)} %get-tuple-element.26), channel_id=1, source_target_pairs={{0,16},{8,24},{16,0},{24,8},{1,17},{9,25},{17,1},{25,9},{2,18},{10... | collective-permute-start | bytes 442376 | tf_op jit(solution)/shard_map/ppermute | solution.py:185
  8.6 1.3 %collective-permute-start.5 = (bf16[8,8,1152]{2,1,0:T(8,128)(2,1)S(1)}, bf16[8,8,1152]{2,1,0:T(8,128)(2,1)S(1)}, u32[]{:S(2)}, u32[]{:S(2)}) collective-permute-start(bf16[8,8,1152]{2,1,0:T(8,128)(2,1)S(1)} %get-tuple-element.27), channel_id=1, source_target_pairs={{0,24},{8,0},{16,8},{24,16},{1,25},{9,1},{17,9},{25,17},{2,26},{10... | collective-permute-start | bytes 442376 | tf_op jit(solution)/shard_map/ppermute | solution.py:185
  9.9 3.8 %gather1.1 = (bf16[8,8,1152]{2,1,0:T(8,128)(2,1)S(1)}, bf16[8,8,1152]{2,1,0:T(8,128)(2,1)S(1)}, bf16[8,8,1152]{2,1,0:T(8,128)(2,1)S(1)}, bf16[8,8,1152]{2,1,0:T(8,128)(2,1)S(1)}) custom-call(bf16[2,1024,1024]{2,1,0:T(8,128)(2,1)} %tok_ref.1, bf16[1024,256]{1,0:T(8,128)(2,1)} %get-tuple-element.18.refs_1_.sp_ref), custom_call_target="tpu_custom_call" | custom-call | flops 1073741824 | bytes 2097152 | tf_op jit(solution)/shard_map/gather1/pallas_call | solution.py:199
  13.8 0.0 copy-start.2
  13.8 0.8 collective-permute-start
  14.5 0.8 collective-permute-start.1
  15.3 2.0 %collective-permute-start.2 = (bf16[8,8,1152]{2,1,0:T(8,128)(2,1)S(1)}, bf16[8,8,1152]{2,1,0:T(8,128)(2,1)S(1)}, u32[]{:S(2)}, u32[]{:S(2)}) collective-permute-start(bf16[8,8,1152]{2,1,0:T(8,128)(2,1)S(1)} %get-tuple-element.23), channel_id=1, source_target_pairs={{0,24},{8,0},{16,8},{24,16},{1,25},{9,1},{17,9},{25,17},{2,26},{10... | collective-permute-start | bytes 442376 | tf_op jit(solution)/shard_map/ppermute | solution.py:185
  17.3 4.4 %combine.1 = (bf16[2,1024,256]{2,1,0:T(8,128)(2,1)S(1)}, f32[8,128]{1,0:T(8,128)S(1)}) custom-call(bf16[2,1024,1024]{2,1,0:T(8,128)(2,1)} %tok_ref.1, bf16[1024,256]{1,0:T(8,128)(2,1)S(1)} %copy-done, bf16[8,8,1152]{2,1,0:T(8,128)(2,1)S(1)} %get-tuple-element.19.after_ref.refs_0_), custom_call_target="tpu_custom_call" | custom-call | flops 1073741824 | bytes 5242880 | tf_op jit(solution)/shard_map/combine/pallas_call | solution.py:227
  21.8 0.3 halfway.1.refs_4_
  22.0 0.9 collective-permute-done.refs_1_
  23.0 0.6 collective-permute-done.2.refs_3_
  23.6 0.3 both.1
  23.9 19.1 %all_to_all.20.refs_0_ = bf16[8,2,8,1152]{3,2,1,0:T(8,128)(2,1)S(1)} all-to-all(bf16[8,2,8,1152]{3,2,1,0:T(8,128)(2,1)S(1)} %both.1), channel_id=1, replica_groups=mesh['group'=8,'y'=4,'zh'=2,'quarter'=4] {'zh','quarter'}, dimensions={0} | all-to-all | bytes 589824 | tf_op jit(solution)/shard_map/all_to_all | solution.py:266
  43.0 0.3 merge.1
  43.3 12.7 %all_to_all.21.x_ref = bf16[32,2,1024]{2,1,0:T(2,128)(2,1)S(1)} all-to-all(bf16[32,2,1024]{2,1,0:T(2,128)(2,1)S(1)} %merge.1), channel_id=1, replica_groups=mesh['group'=8,'y'=4,'zh'=2,'quarter'=4] {'group','quarter'}, dimensions={0} | all-to-all | bytes 262144 | tf_op jit(solution)/shard_map/all_to_all | solution.py:269
  55.9 1.0 expert.1
  56.9 12.5 %all_to_all.22.x_ref = bf16[32,2,1024]{2,1,0:T(2,128)(2,1)S(1)} all-to-all(bf16[32,2,1024]{2,1,0:T(2,128)(2,1)S(1)} %expert.1), channel_id=1, replica_groups=mesh['group'=8,'y'=4,'zh'=2,'quarter'=4] {'group','quarter'}, dimensions={0} | all-to-all | bytes 262144 | tf_op jit(solution)/shard_map/all_to_all | solution.py:271
  69.5 0.1 total.1
  69.6 15.6 %all_to_all.23.in_ref = bf16[8,2,8,1024]{3,2,1,0:T(8,128)(2,1)S(1)} all-to-all(bf16[8,2,8,1024]{3,2,1,0:T(8,128)(2,1)S(1)} %total.1), channel_id=1, replica_groups=mesh['group'=8,'y'=4,'zh'=2,'quarter'=4] {'zh','quarter'}, dimensions={0} | all-to-all | bytes 524288 | tf_op jit(solution)/shard_map/all_to_all | solution.py:275
  85.2 0.9 collective-permute-start.11
  86.2 4.2 %collective-permute-start.10 = (bf16[64,1024]{1,0:T(8,128)(2,1)S(1)}, bf16[64,1024]{1,0:T(8,128)(2,1)S(1)}, u32[]{:S(2)}, u32[]{:S(2)}) collective-permute-start(bf16[64,1024]{1,0:T(8,128)(2,1)S(1)} %get-tuple-element.30.refs_1_), channel_id=1, source_target_pairs={{0,16},{8,24},{16,0},{24,8},{1,17},{9,25},{17,1},{25,9},{2,18},{10... | collective-permute-start | bytes 393224 | tf_op jit(solution)/shard_map/ppermute | solution.py:185
  90.4 2.0 %collective-permute-start.8 = (bf16[64,1024]{1,0:T(8,128)(2,1)S(1)}, bf16[64,1024]{1,0:T(8,128)(2,1)S(1)}, u32[]{:S(2)}, u32[]{:S(2)}) collective-permute-start(bf16[64,1024]{1,0:T(8,128)(2,1)S(1)} %get-tuple-element.29.refs_1_), channel_id=1, source_target_pairs={{0,8},{8,16},{16,24},{24,0},{1,9},{9,17},{17,25},{25,1},{2,10},{10... | collective-permute-start | bytes 393224 | tf_op jit(solution)/shard_map/ppermute | solution.py:185
  92.4 2.2 %collective-permute-done.11.refs_4_ = bf16[64,1024]{1,0:T(8,128)(2,1)S(1)} collective-permute-done((bf16[64,1024]{1,0:T(8,128)(2,1)S(1)}, bf16[64,1024]{1,0:T(8,128)(2,1)S(1)}, u32[]{:S(2)}, u32[]{:S(2)}) %collective-permute-start.11) | collective-permute-done | bytes 131104 | tf_op jit(solution)/shard_map/ppermute | solution.py:185
  94.7 0.7 collective-permute-start.6
  95.4 1.7 %collective-permute-done.10.refs_3_ = bf16[64,1024]{1,0:T(8,128)(2,1)S(1)} collective-permute-done((bf16[64,1024]{1,0:T(8,128)(2,1)S(1)}, bf16[64,1024]{1,0:T(8,128)(2,1)S(1)}, u32[]{:S(2)}, u32[]{:S(2)}) %collective-permute-start.10) | collective-permute-done | bytes 131104 | tf_op jit(solution)/shard_map/ppermute | solution.py:185
  97.0 1.6 %mix0.1.refs_5_ = bf16[2,1024,1024]{2,1,0:T(8,128)(2,1)} custom-call(bf16[2,1024,256]{2,1,0:T(8,128)(2,1)S(1)} %get-tuple-element.20.refs_0_, bf16[64,1024]{1,0:T(8,128)(2,1)S(1)} %get-tuple-element.30.refs_1_, bf16[64,1024]{1,0:T(8,128)(2,1)S(1)} %collective-permute-done.9.refs_2_, bf16[64,1024]{1,0:T(8,128)(2,1)S(1)} %collective-permute-done.10.refs_3_, ...), custom_call_target="tpu_custom_call" | custom-call | flops 536870912 | bytes 2621440 | tf_op jit(solution)/shard_map/mix0/pallas_call | solution.py:283
  98.7 1.1 %collective-permute-done.7.refs_3_ = bf16[64,1024]{1,0:T(8,128)(2,1)S(1)} collective-permute-done((bf16[64,1024]{1,0:T(8,128)(2,1)S(1)}, bf16[64,1024]{1,0:T(8,128)(2,1)S(1)}, u32[]{:S(2)}, u32[]{:S(2)}) %collective-permute-start.7) | collective-permute-done | bytes 131104 | tf_op jit(solution)/shard_map/ppermute | solution.py:185
  99.8 0.1 collective-permute-done.6.refs_2_
  99.9 1.6 %mix1.1 = bf16[2,1024,1024]{2,1,0:T(8,128)(2,1)} custom-call(bf16[2,1024,256]{2,1,0:T(8,128)(2,1)S(1)} %get-tuple-element.20.refs_0_, bf16[64,1024]{1,0:T(8,128)(2,1)S(1)} %get-tuple-element.29.refs_1_, bf16[64,1024]{1,0:T(8,128)(2,1)S(1)} %collective-permute-done.6.refs_2_, ...), custom_call_target="tpu_custom_call", output_to_operand_aliasing={{}: (5, {})} | custom-call | flops 536870912 | bytes 2621440 | tf_op jit(solution)/shard_map/mix1/pallas_call | solution.py:283
  (13 shorter events, 0.0 us)
Async XLA Ops:
  4.0 13.3 %copy-start = (bf16[1024,256]{1,0:T(8,128)(2,1)S(1)}, bf16[1024,256]{1,0:T(8,128)(2,1)}, u32[]{:S(2)}) copy-start(bf16[1024,256]{1,0:T(8,128)(2,1)} %get-tuple-element.18.refs_1_.sp_ref) | copy-start | bytes 1572868
  4.0 11.3 %collective-permute-start.3 = (bf16[8,8,1152]{2,1,0:T(8,128)(2,1)S(1)}, bf16[8,8,1152]{2,1,0:T(8,128)(2,1)S(1)}, u32[]{:S(2)}, u32[]{:S(2)}) collective-permute-start(bf16[8,8,1152]{2,1,0:T(8,128)(2,1)S(1)} %get-tuple-element.25), channel_id=1, source_target_pairs={{0,8},{8,16},{16,24},{24,0},{1,9},{9,17},{17,25},{25,1},{2,10},{10... | collective-permute-start | bytes 442376 | tf_op jit(solution)/shard_map/ppermute | solution.py:185
  5.7 16.1 %collective-permute-start.4 = (bf16[8,8,1152]{2,1,0:T(8,128)(2,1)S(1)}, bf16[8,8,1152]{2,1,0:T(8,128)(2,1)S(1)}, u32[]{:S(2)}, u32[]{:S(2)}) collective-permute-start(bf16[8,8,1152]{2,1,0:T(8,128)(2,1)S(1)} %get-tuple-element.26), channel_id=1, source_target_pairs={{0,16},{8,24},{16,0},{24,8},{1,17},{9,25},{17,1},{25,9},{2,18},{10... | collective-permute-start | bytes 442376 | tf_op jit(solution)/shard_map/ppermute | solution.py:185
  8.6 13.2 %collective-permute-start.5 = (bf16[8,8,1152]{2,1,0:T(8,128)(2,1)S(1)}, bf16[8,8,1152]{2,1,0:T(8,128)(2,1)S(1)}, u32[]{:S(2)}, u32[]{:S(2)}) collective-permute-start(bf16[8,8,1152]{2,1,0:T(8,128)(2,1)S(1)} %get-tuple-element.27), channel_id=1, source_target_pairs={{0,24},{8,0},{16,8},{24,16},{1,25},{9,1},{17,9},{25,17},{2,26},{10... | collective-permute-start | bytes 442376 | tf_op jit(solution)/shard_map/ppermute | solution.py:185
  13.8 42.2 %copy-start.1 = (bf16[1024,1024]{1,0:T(8,128)(2,1)S(1)}, bf16[1024,1024]{1,0:T(8,128)(2,1)}, u32[]{:S(2)}) copy-start(bf16[1024,1024]{1,0:T(8,128)(2,1)} %up_ref.1) | copy-start | bytes 6291460
  13.8 42.2 %copy-start.2 = (bf16[1024,1024]{1,0:T(8,128)(2,1)S(1)}, bf16[1024,1024]{1,0:T(8,128)(2,1)}, u32[]{:S(2)}) copy-start(bf16[1024,1024]{1,0:T(8,128)(2,1)} %down_ref.1) | copy-start | bytes 6291460
  13.8 9.2 %collective-permute-start = (bf16[8,8,1152]{2,1,0:T(8,128)(2,1)S(1)}, bf16[8,8,1152]{2,1,0:T(8,128)(2,1)S(1)}, u32[]{:S(2)}, u32[]{:S(2)}) collective-permute-start(bf16[8,8,1152]{2,1,0:T(8,128)(2,1)S(1)} %get-tuple-element.21), channel_id=1, source_target_pairs={{0,8},{8,16},{16,24},{24,0},{1,9},{9,17},{17,25},{25,1},{2,10},{10... | collective-permute-start | bytes 442376 | tf_op jit(solution)/shard_map/ppermute | solution.py:185
  14.5 8.4 %collective-permute-start.1 = (bf16[8,8,1152]{2,1,0:T(8,128)(2,1)S(1)}, bf16[8,8,1152]{2,1,0:T(8,128)(2,1)S(1)}, u32[]{:S(2)}, u32[]{:S(2)}) collective-permute-start(bf16[8,8,1152]{2,1,0:T(8,128)(2,1)S(1)} %get-tuple-element.22), channel_id=1, source_target_pairs={{0,16},{8,24},{16,0},{24,8},{1,17},{9,25},{17,1},{25,9},{2,18},{10... | collective-permute-start | bytes 442376 | tf_op jit(solution)/shard_map/ppermute | solution.py:185
  15.3 8.2 %collective-permute-start.2 = (bf16[8,8,1152]{2,1,0:T(8,128)(2,1)S(1)}, bf16[8,8,1152]{2,1,0:T(8,128)(2,1)S(1)}, u32[]{:S(2)}, u32[]{:S(2)}) collective-permute-start(bf16[8,8,1152]{2,1,0:T(8,128)(2,1)S(1)} %get-tuple-element.23), channel_id=1, source_target_pairs={{0,24},{8,0},{16,8},{24,16},{1,25},{9,1},{17,9},{25,17},{2,26},{10... | collective-permute-start | bytes 442376 | tf_op jit(solution)/shard_map/ppermute | solution.py:185
  85.2 9.4 %collective-permute-start.11 = (bf16[64,1024]{1,0:T(8,128)(2,1)S(1)}, bf16[64,1024]{1,0:T(8,128)(2,1)S(1)}, u32[]{:S(2)}, u32[]{:S(2)}) collective-permute-start(bf16[64,1024]{1,0:T(8,128)(2,1)S(1)} %get-tuple-element.30.refs_1_), channel_id=1, source_target_pairs={{0,8},{8,16},{16,24},{24,0},{1,9},{9,17},{17,25},{25,1},{2,10},{10... | collective-permute-start | bytes 393224 | tf_op jit(solution)/shard_map/ppermute | solution.py:185
  86.2 10.9 %collective-permute-start.10 = (bf16[64,1024]{1,0:T(8,128)(2,1)S(1)}, bf16[64,1024]{1,0:T(8,128)(2,1)S(1)}, u32[]{:S(2)}, u32[]{:S(2)}) collective-permute-start(bf16[64,1024]{1,0:T(8,128)(2,1)S(1)} %get-tuple-element.30.refs_1_), channel_id=1, source_target_pairs={{0,16},{8,24},{16,0},{24,8},{1,17},{9,25},{17,1},{25,9},{2,18},{10... | collective-permute-start | bytes 393224 | tf_op jit(solution)/shard_map/ppermute | solution.py:185
  90.4 6.6 %collective-permute-start.9 = (bf16[64,1024]{1,0:T(8,128)(2,1)S(1)}, bf16[64,1024]{1,0:T(8,128)(2,1)S(1)}, u32[]{:S(2)}, u32[]{:S(2)}) collective-permute-start(bf16[64,1024]{1,0:T(8,128)(2,1)S(1)} %get-tuple-element.30.refs_1_), channel_id=1, source_target_pairs={{0,24},{8,0},{16,8},{24,16},{1,25},{9,1},{17,9},{25,17},{2,26},{10... | collective-permute-start | bytes 393224 | tf_op jit(solution)/shard_map/ppermute | solution.py:185
  90.4 8.3 %collective-permute-start.8 = (bf16[64,1024]{1,0:T(8,128)(2,1)S(1)}, bf16[64,1024]{1,0:T(8,128)(2,1)S(1)}, u32[]{:S(2)}, u32[]{:S(2)}) collective-permute-start(bf16[64,1024]{1,0:T(8,128)(2,1)S(1)} %get-tuple-element.29.refs_1_), channel_id=1, source_target_pairs={{0,8},{8,16},{16,24},{24,0},{1,9},{9,17},{17,25},{25,1},{2,10},{10... | collective-permute-start | bytes 393224 | tf_op jit(solution)/shard_map/ppermute | solution.py:185
  92.4 7.3 %collective-permute-start.7 = (bf16[64,1024]{1,0:T(8,128)(2,1)S(1)}, bf16[64,1024]{1,0:T(8,128)(2,1)S(1)}, u32[]{:S(2)}, u32[]{:S(2)}) collective-permute-start(bf16[64,1024]{1,0:T(8,128)(2,1)S(1)} %get-tuple-element.29.refs_1_), channel_id=1, source_target_pairs={{0,16},{8,24},{16,0},{24,8},{1,17},{9,25},{17,1},{25,9},{2,18},{10... | collective-permute-start | bytes 393224 | tf_op jit(solution)/shard_map/ppermute | solution.py:185
  94.7 5.2 %collective-permute-start.6 = (bf16[64,1024]{1,0:T(8,128)(2,1)S(1)}, bf16[64,1024]{1,0:T(8,128)(2,1)S(1)}, u32[]{:S(2)}, u32[]{:S(2)}) collective-permute-start(bf16[64,1024]{1,0:T(8,128)(2,1)S(1)} %get-tuple-element.29.refs_1_), channel_id=1, source_target_pairs={{0,24},{8,0},{16,8},{24,16},{1,25},{9,1},{17,9},{25,17},{2,26},{10... | collective-permute-start | bytes 393224 | tf_op jit(solution)/shard_map/ppermute | solution.py:185

commit v4 on v3

--- a/solution.py
+++ b/solution.py
@@ -15,6 +15,8 @@
 STEPS = 4
 MIB = 1 << 20
 BIG = 52
+FAR_FIRST = (2, 1, 3)
+FAR_LAST = (0, 1, 3, 2)
 
 
 def vmem():
@@ -92,7 +94,7 @@
 def combine_kernel(tok_ref, sp_ref, after_ref, out_ref, tick_ref):
     logits = jnp.dot(tok_ref[0], sp_ref[...], preferred_element_type=F32)
     spread = jnp.exp(logits - jnp.max(logits, axis=1, keepdims=True))
-    out_ref[0] = (spread * (1.0 / jnp.sum(spread, axis=1, keepdims=True))).astype(BF16)
+    out_ref[...] = (spread * (1.0 / jnp.sum(spread, axis=1, keepdims=True))).astype(BF16)
     tick_ref[...] = jnp.zeros_like(tick_ref)
 
 
@@ -159,13 +161,13 @@
 def mix_kernel(clip, ny, comb_ref, *refs):
     slot_refs, (out_hbm, held, buf, sems) = refs[:ny], refs[-4:]
     rows = slot_refs[0].shape[0]
-    for i, r in enumerate(slot_refs):
+    for i, r in zip(FAR_LAST, slot_refs):
         held[i * rows : (i + 1) * rows] = r[...]
     step = buf.shape[0] // STEPS
     copies = []
     for i in range(STEPS):
         part = pl.ds(i * step, step)
-        buf[part] = jnp.dot(comb_ref[clip, part], held[...], preferred_element_type=F32).astype(BF16)
+        buf[part] = jnp.dot(comb_ref[part], held[...], preferred_element_type=F32).astype(BF16)
         copies.append(pltpu.make_async_copy(buf.at[part], out_hbm.at[clip, part], sems.at[i]))
         copies[-1].start()
     for copy in copies:
@@ -216,39 +218,40 @@
             name=f"gather{clip}",
         )(tokens, sp)
 
-    arrived = []
-    ordered = slot_params
-    for clip in range(clips):
-        means = gather(clip, ordered)
-        if clip == 0:
-            ordered = means[ny]
-        arrived += [means[0]] + [shift(means[k], k) for k in range(1, ny)]
-    half = length // 2
-    combine, tick = pl.pallas_call(
-        combine_kernel,
-        grid=(clips, 2),
-        in_specs=[
-            pl.BlockSpec((1, half, width), lambda c, t: (c, t, 0)),
-            pl.BlockSpec((width, slots), lambda c, t: (0, 0)),
-            pl.BlockSpec((1, groups, STAT), lambda c, t: (0, 0, 0)),
-        ],
-        out_specs=[
-            pl.BlockSpec((1, half, slots), lambda c, t: (c, t, 0)),
-            pl.BlockSpec((8, STAT), lambda c, t: (0, 0)),
-        ],
-        out_shape=[
-            jax.ShapeDtypeStruct((clips, length, slots), BF16),
-            jax.ShapeDtypeStruct((8, STAT), F32),
-        ],
-        compiler_params=params(BIG),
-        cost_estimate=pl.CostEstimate(
-            flops=2 * clips * length * width * slots,
-            bytes_accessed=2 * clips * length * (width + slots),
-            transcendentals=clips * length * slots,
-        ),
-        name="combine",
-    )(tokens, ordered, arrived[-ny])
-    assert clips == 2
+    def combine(clip, after):
+        half = length // 2
+        return pl.pallas_call(
+            combine_kernel,
+            grid=(2,),
+            in_specs=[
+                pl.BlockSpec((1, half, width), lambda t: (clip, t, 0)),
+                pl.BlockSpec((width, slots), lambda t: (0, 0)),
+                pl.BlockSpec((1,) * (after.ndim - 2) + (8, STAT), lambda t: (0,) * after.ndim),
+            ],
+            out_specs=[
+                pl.BlockSpec((half, slots), lambda t: (t, 0)),
+                pl.BlockSpec((8, STAT), lambda t: (0, 0)),
+            ],
+            out_shape=[
+                jax.ShapeDtypeStruct((length, slots), BF16),
+                jax.ShapeDtypeStruct((8, STAT), F32),
+            ],
+            compiler_params=params(BIG),
+            cost_estimate=pl.CostEstimate(
+                flops=2 * length * width * slots,
+                bytes_accessed=2 * length * (width + slots),
+                transcendentals=length * slots,
+            ),
+            name=f"combine{clip}",
+        )(tokens, ordered, after)
+
+    assert clips == 2 and ny == 4
+    *means0, ordered = gather(0, slot_params)
+    sent0 = {k: shift(means0[k], k) for k in FAR_FIRST}
+    means1 = gather(1, ordered)
+    sent1 = {k: shift(means1[k], k) for k in FAR_FIRST}
+    arrived = [means0[0], *sent0.values(), means1[0], *sent1.values()]
+    combine0, tick = combine(0, means1[0])
     halfway = small(
         name(halfway_kernel, width),
         jax.ShapeDtypeStruct((nz, groups, wide), BF16),
@@ -276,7 +279,8 @@
     rings = small(
         split_kernel, [jax.ShapeDtypeStruct((nz * groups, width), BF16)] * clips, "split", ring
     )
-    rings = [[ring] + [shift(ring, -k) for k in range(1, ny)] for ring in rings]
+    combines = [combine0, combine(1, rings[0])[0]]
+    rings = [[shift(ring, -k) if k else ring for k in FAR_LAST] for ring in rings]
     mixed = None
     for clip in range(clips):
         before = [] if mixed is None else [mixed]
@@ -298,7 +302,7 @@
                 transcendentals=0,
             ),
             name=f"mix{clip}",
-        )(combine, *rings[clip], *before)
+        )(combines[clip], *rings[clip], *before)
     return mixed
 
 

time: 103 us -> 103 us (level)
  blocking collectives: 59.9 us -> 61.3 us
  waiting for transfers between devices: 6.63 us -> 5.53 us
    all_to_all x1, blocking collectives: 19.1 us -> 20.7 us  [shards(): arrived = lax.all_to_all(halfway, around, 0, 0, tiled=True)]
    ppermute x12, waiting for transfers between devices: 6.63 us -> 5.53 us  [shift(): return lax.ppermute(x, 'y', [(i, (i + k) % ny) for i in range(ny)])]
    pallas_call x1 -> x2, Pallas kernels: 4.41 us -> 5.43 us  [combine(): pl.pallas_call(combine_kernel, grid=(2,), in_specs=[pl.BlockSpec((1, half...]
  transfers between devices with their start and end apart: 12 -> 12, of which waited for: 6 -> 3; matrix products, arithmetic and copies ran while one was open for 0% -> 0% of each run, Pallas kernels for 10% -> 11%
where the time goes in v4:
time: 103 us; the launch traced here: 102 us
  blocking collectives  61.3 us (60%)
  Pallas kernels  18.5 us (18%)
  starting transfers between devices  16.4 us (16%)
  waiting for transfers between devices  5.53 us (5%)
    all_to_all x1, blocking collectives, shards(): arrived = lax.all_to_all(halfway, around, 0, 0, tiled=True)  20.7 us
    ppermute x12, starting transfers between devices, shift(): return lax.ppermute(x, 'y', [(i, (i + k) % ny) for i in range(ny)])  16.4 us
    all_to_all x1, blocking collectives, shards(): ring = lax.all_to_all(slot_out, around, 0, 0, tiled=True)  15.4 us
    all_to_all x1, blocking collectives, shards(): own = lax.all_to_all(slot_in, sharers, 0, 0, tiled=True)  12.7 us
    all_to_all x1, blocking collectives, shards(): back = lax.all_to_all(partial, sharers, 0, 0, tiled=True)  12.5 us
    pallas_call x2, Pallas kernels, gather(): pl.pallas_call(name(gather_kernel, clip, groups, ny, nz), in_specs=[anywh...  7.8 us
    ppermute x12, waiting for transfers between devices, shift(): return lax.ppermute(x, 'y', [(i, (i + k) % ny) for i in range(ny)])  5.53 us
    pallas_call x2, Pallas kernels, combine(): pl.pallas_call(combine_kernel, grid=(2,), in_specs=[pl.BlockSpec((1, half...  5.43 us
  transfers between devices with their start and end apart: 12, of which 3 were waited for; matrix products, arithmetic and copies ran while one was open for 0% of the time, Pallas kernels for 11%

profile of v4, /device:TPU:2, one launch (start us, length us, event | category | flops | bytes accessed | tf_op | source)
XLA Modules:
  0.0 102.0 jit_solution(12765142280187399730)
XLA Ops:
  0.0 4.0 %gather0.1 = (bf16[8,8,1152]{2,1,0:T(8,128)(2,1)S(1)}, bf16[8,8,1152]{2,1,0:T(8,128)(2,1)S(1)}, bf16[8,8,1152]{2,1,0:T(8,128)(2,1)S(1)}, bf16[8,8,1152]{2,1,0:T(8,128)(2,1)S(1)}, bf16[1024,256]{1,0:T(8,128)(2,1)}) custom-call(bf16[2,1024,1024]{2,1,0:T(8,128)(2,1)} %tok_ref.3, bf16[1024,256]{1,0:T(8,128)(2,1)} %refs_1_.1), custom_call_target="tpu_custom_call" | custom-call | flops 1073741824 | bytes 2097152 | tf_op jit(solution)/shard_map/gather0/pallas_call | solution.py:201
  4.0 0.0 copy-start
  4.0 3.3 %collective-permute-start.3 = (bf16[8,8,1152]{2,1,0:T(8,128)(2,1)S(1)}, bf16[8,8,1152]{2,1,0:T(8,128)(2,1)S(1)}, u32[]{:S(2)}, u32[]{:S(2)}) collective-permute-start(bf16[8,8,1152]{2,1,0:T(8,128)(2,1)S(1)} %get-tuple-element.25), channel_id=1, source_target_pairs={{0,16},{8,24},{16,0},{24,8},{1,17},{9,25},{17,1},{25,9},{2,18},{10... | collective-permute-start | bytes 442376 | tf_op jit(solution)/shard_map/ppermute | solution.py:187
  7.3 0.7 collective-permute-start.4
  8.0 2.6 %collective-permute-start.5 = (bf16[8,8,1152]{2,1,0:T(8,128)(2,1)S(1)}, bf16[8,8,1152]{2,1,0:T(8,128)(2,1)S(1)}, u32[]{:S(2)}, u32[]{:S(2)}) collective-permute-start(bf16[8,8,1152]{2,1,0:T(8,128)(2,1)S(1)} %get-tuple-element.27), channel_id=1, source_target_pairs={{0,24},{8,0},{16,8},{24,16},{1,25},{9,1},{17,9},{25,17},{2,26},{10... | collective-permute-start | bytes 442376 | tf_op jit(solution)/shard_map/ppermute | solution.py:187
  10.5 3.8 %gather1.1 = (bf16[8,8,1152]{2,1,0:T(8,128)(2,1)S(1)}, bf16[8,8,1152]{2,1,0:T(8,128)(2,1)S(1)}, bf16[8,8,1152]{2,1,0:T(8,128)(2,1)S(1)}, bf16[8,8,1152]{2,1,0:T(8,128)(2,1)S(1)}) custom-call(bf16[2,1024,1024]{2,1,0:T(8,128)(2,1)} %tok_ref.3, bf16[1024,256]{1,0:T(8,128)(2,1)} %get-tuple-element.19.refs_1_.sp_ref), custom_call_target="tpu_custom_call" | custom-call | flops 1073741824 | bytes 2097152 | tf_op jit(solution)/shard_map/gather1/pallas_call | solution.py:201
  14.4 0.0 copy-start.1
  14.4 0.0 copy-start.2
  14.4 0.1 collective-permute-start
  14.5 0.9 collective-permute-start.1
  15.4 2.5 %collective-permute-start.2 = (bf16[8,8,1152]{2,1,0:T(8,128)(2,1)S(1)}, bf16[8,8,1152]{2,1,0:T(8,128)(2,1)S(1)}, u32[]{:S(2)}, u32[]{:S(2)}) collective-permute-start(bf16[8,8,1152]{2,1,0:T(8,128)(2,1)S(1)} %get-tuple-element.23), channel_id=1, source_target_pairs={{0,24},{8,0},{16,8},{24,16},{1,25},{9,1},{17,9},{25,17},{2,26},{10... | collective-permute-start | bytes 442376 | tf_op jit(solution)/shard_map/ppermute | solution.py:187
  17.8 2.5 %combine0.1 = (bf16[1024,256]{1,0:T(8,128)(2,1)S(1)}, f32[8,128]{1,0:T(8,128)S(1)}) custom-call(bf16[2,1024,1024]{2,1,0:T(8,128)(2,1)} %tok_ref.3, bf16[1024,256]{1,0:T(8,128)(2,1)S(1)} %copy-done, bf16[8,8,1152]{2,1,0:T(8,128)(2,1)S(1)} %get-tuple-element.20.after_ref.refs_0_), custom_call_target="tpu_custom_call" | custom-call | flops 536870912 | bytes 2621440 | tf_op jit(solution)/shard_map/combine0/pallas_call | solution.py:223
  20.3 0.3 halfway.1.refs_4_
  20.6 1.8 %collective-permute-done.refs_1_ = bf16[8,8,1152]{2,1,0:T(8,128)(2,1)S(1)} collective-permute-done((bf16[8,8,1152]{2,1,0:T(8,128)(2,1)S(1)}, bf16[8,8,1152]{2,1,0:T(8,128)(2,1)S(1)}, u32[]{:S(2)}, u32[]{:S(2)}) %collective-permute-start) | collective-permute-done | bytes 147488 | tf_op jit(solution)/shard_map/ppermute | solution.py:187
  22.4 1.3 %collective-permute-done.1.refs_2_ = bf16[8,8,1152]{2,1,0:T(8,128)(2,1)S(1)} collective-permute-done((bf16[8,8,1152]{2,1,0:T(8,128)(2,1)S(1)}, bf16[8,8,1152]{2,1,0:T(8,128)(2,1)S(1)}, u32[]{:S(2)}, u32[]{:S(2)}) %collective-permute-start.1) | collective-permute-done | bytes 147488 | tf_op jit(solution)/shard_map/ppermute | solution.py:187
  23.7 0.3 both.1
  24.0 20.7 %all_to_all.20.refs_0_ = bf16[8,2,8,1152]{3,2,1,0:T(8,128)(2,1)S(1)} all-to-all(bf16[8,2,8,1152]{3,2,1,0:T(8,128)(2,1)S(1)} %both.1), channel_id=1, replica_groups=mesh['group'=8,'y'=4,'zh'=2,'quarter'=4] {'zh','quarter'}, dimensions={0} | all-to-all | bytes 589824 | tf_op jit(solution)/shard_map/all_to_all | solution.py:269
  44.6 0.3 merge.1
  44.9 12.7 %all_to_all.21.x_ref = bf16[32,2,1024]{2,1,0:T(2,128)(2,1)S(1)} all-to-all(bf16[32,2,1024]{2,1,0:T(2,128)(2,1)S(1)} %merge.1), channel_id=1, replica_groups=mesh['group'=8,'y'=4,'zh'=2,'quarter'=4] {'group','quarter'}, dimensions={0} | all-to-all | bytes 262144 | tf_op jit(solution)/shard_map/all_to_all | solution.py:272
  57.6 1.0 expert.1
  58.6 12.5 %all_to_all.22.x_ref = bf16[32,2,1024]{2,1,0:T(2,128)(2,1)S(1)} all-to-all(bf16[32,2,1024]{2,1,0:T(2,128)(2,1)S(1)} %expert.1), channel_id=1, replica_groups=mesh['group'=8,'y'=4,'zh'=2,'quarter'=4] {'group','quarter'}, dimensions={0} | all-to-all | bytes 262144 | tf_op jit(solution)/shard_map/all_to_all | solution.py:274
  71.1 0.1 total.1
  71.3 15.4 %all_to_all.23.in_ref = bf16[8,2,8,1024]{3,2,1,0:T(8,128)(2,1)S(1)} all-to-all(bf16[8,2,8,1024]{3,2,1,0:T(8,128)(2,1)S(1)} %total.1), channel_id=1, replica_groups=mesh['group'=8,'y'=4,'zh'=2,'quarter'=4] {'zh','quarter'}, dimensions={0} | all-to-all | bytes 524288 | tf_op jit(solution)/shard_map/all_to_all | solution.py:278
  86.7 0.1 collective-permute-start.11
  86.8 0.9 collective-permute-start.10
  87.6 2.4 %collective-permute-start.9 = (bf16[64,1024]{1,0:T(8,128)(2,1)S(1)}, bf16[64,1024]{1,0:T(8,128)(2,1)S(1)}, u32[]{:S(2)}, u32[]{:S(2)}) collective-permute-start(bf16[64,1024]{1,0:T(8,128)(2,1)S(1)} %get-tuple-element.29.after_ref.refs_1_), channel_id=1, source_target_pairs={{0,24},{8,0},{16,8},{24,16},{1,25},{9,1},{17,9},{25,17},{2,26},{10... | collective-permute-start | bytes 393224 | tf_op jit(solution)/shard_map/ppermute | solution.py:187
  90.1 2.2 %collective-permute-start.8 = (bf16[64,1024]{1,0:T(8,128)(2,1)S(1)}, bf16[64,1024]{1,0:T(8,128)(2,1)S(1)}, u32[]{:S(2)}, u32[]{:S(2)}) collective-permute-start(bf16[64,1024]{1,0:T(8,128)(2,1)S(1)} %get-tuple-element.31.refs_1_), channel_id=1, source_target_pairs={{0,16},{8,24},{16,0},{24,8},{1,17},{9,25},{17,1},{25,9},{2,18},{10... | collective-permute-start | bytes 393224 | tf_op jit(solution)/shard_map/ppermute | solution.py:187
  92.3 2.4 %collective-permute-done.11.refs_4_ = bf16[64,1024]{1,0:T(8,128)(2,1)S(1)} collective-permute-done((bf16[64,1024]{1,0:T(8,128)(2,1)S(1)}, bf16[64,1024]{1,0:T(8,128)(2,1)S(1)}, u32[]{:S(2)}, u32[]{:S(2)}) %collective-permute-start.11) | collective-permute-done | bytes 131104 | tf_op jit(solution)/shard_map/ppermute | solution.py:187
  94.7 0.8 collective-permute-start.6
  95.6 3.0 %combine1.1 = (bf16[1024,256]{1,0:T(8,128)(2,1)S(1)}, f32[8,128]{1,0:T(8,128)}) custom-call(bf16[2,1024,1024]{2,1,0:T(8,128)(2,1)} %tok_ref.3, bf16[1024,256]{1,0:T(8,128)(2,1)S(1)} %copy-done, bf16[64,1024]{1,0:T(8,128)(2,1)S(1)} %get-tuple-element.29.after_ref.refs_1_), custom_call_target="tpu_custom_call" | custom-call | flops 536870912 | bytes 2621440 | tf_op jit(solution)/shard_map/combine1/pallas_call | solution.py:223
  98.5 1.6 %mix0.1.refs_5_ = bf16[2,1024,1024]{2,1,0:T(8,128)(2,1)} custom-call(bf16[1024,256]{1,0:T(8,128)(2,1)S(1)} %get-tuple-element.32.refs_0_, bf16[64,1024]{1,0:T(8,128)(2,1)S(1)} %get-tuple-element.29.after_ref.refs_1_, bf16[64,1024]{1,0:T(8,128)(2,1)S(1)} %collective-permute-done.9.refs_2_, bf16[64,1024]{1,0:T(8,128)(2,1)S(1)} %collective-permute-done.10.refs_3_, ...), custom_call_target="tpu_custom_call" | custom-call | flops 536870912 | bytes 2621440 | tf_op jit(solution)/shard_map/mix0/pallas_call | solution.py:287
  100.2 1.7 %mix1.1 = bf16[2,1024,1024]{2,1,0:T(8,128)(2,1)} custom-call(bf16[1024,256]{1,0:T(8,128)(2,1)S(1)} %get-tuple-element.30.refs_0_, bf16[64,1024]{1,0:T(8,128)(2,1)S(1)} %get-tuple-element.31.refs_1_, bf16[64,1024]{1,0:T(8,128)(2,1)S(1)} %collective-permute-done.6.refs_2_, ...), custom_call_target="tpu_custom_call", output_to_operand_aliasing={{}: (5, {})} | custom-call | flops 536870912 | bytes 2621440 | tf_op jit(solution)/shard_map/mix1/pallas_call | solution.py:287
  (14 shorter events, 0.1 us)
Async XLA Ops:
  4.0 13.8 %copy-start = (bf16[1024,256]{1,0:T(8,128)(2,1)S(1)}, bf16[1024,256]{1,0:T(8,128)(2,1)}, u32[]{:S(2)}) copy-start(bf16[1024,256]{1,0:T(8,128)(2,1)} %get-tuple-element.19.refs_1_.sp_ref) | copy-start | bytes 1572868
  4.0 11.4 %collective-permute-start.3 = (bf16[8,8,1152]{2,1,0:T(8,128)(2,1)S(1)}, bf16[8,8,1152]{2,1,0:T(8,128)(2,1)S(1)}, u32[]{:S(2)}, u32[]{:S(2)}) collective-permute-start(bf16[8,8,1152]{2,1,0:T(8,128)(2,1)S(1)} %get-tuple-element.25), channel_id=1, source_target_pairs={{0,16},{8,24},{16,0},{24,8},{1,17},{9,25},{17,1},{25,9},{2,18},{10... | collective-permute-start | bytes 442376 | tf_op jit(solution)/shard_map/ppermute | solution.py:187
  7.3 13.0 %collective-permute-start.4 = (bf16[8,8,1152]{2,1,0:T(8,128)(2,1)S(1)}, bf16[8,8,1152]{2,1,0:T(8,128)(2,1)S(1)}, u32[]{:S(2)}, u32[]{:S(2)}) collective-permute-start(bf16[8,8,1152]{2,1,0:T(8,128)(2,1)S(1)} %get-tuple-element.26), channel_id=1, source_target_pairs={{0,8},{8,16},{16,24},{24,0},{1,9},{9,17},{17,25},{25,1},{2,10},{10... | collective-permute-start | bytes 442376 | tf_op jit(solution)/shard_map/ppermute | solution.py:187
  8.0 12.3 %collective-permute-start.5 = (bf16[8,8,1152]{2,1,0:T(8,128)(2,1)S(1)}, bf16[8,8,1152]{2,1,0:T(8,128)(2,1)S(1)}, u32[]{:S(2)}, u32[]{:S(2)}) collective-permute-start(bf16[8,8,1152]{2,1,0:T(8,128)(2,1)S(1)} %get-tuple-element.27), channel_id=1, source_target_pairs={{0,24},{8,0},{16,8},{24,16},{1,25},{9,1},{17,9},{25,17},{2,26},{10... | collective-permute-start | bytes 442376 | tf_op jit(solution)/shard_map/ppermute | solution.py:187
  14.4 43.2 %copy-start.1 = (bf16[1024,1024]{1,0:T(8,128)(2,1)S(1)}, bf16[1024,1024]{1,0:T(8,128)(2,1)}, u32[]{:S(2)}) copy-start(bf16[1024,1024]{1,0:T(8,128)(2,1)} %up_ref.1) | copy-start | bytes 6291460
  14.4 43.2 %copy-start.2 = (bf16[1024,1024]{1,0:T(8,128)(2,1)S(1)}, bf16[1024,1024]{1,0:T(8,128)(2,1)}, u32[]{:S(2)}) copy-start(bf16[1024,1024]{1,0:T(8,128)(2,1)} %down_ref.1) | copy-start | bytes 6291460
  14.4 8.0 %collective-permute-start = (bf16[8,8,1152]{2,1,0:T(8,128)(2,1)S(1)}, bf16[8,8,1152]{2,1,0:T(8,128)(2,1)S(1)}, u32[]{:S(2)}, u32[]{:S(2)}) collective-permute-start(bf16[8,8,1152]{2,1,0:T(8,128)(2,1)S(1)} %get-tuple-element.21), channel_id=1, source_target_pairs={{0,16},{8,24},{16,0},{24,8},{1,17},{9,25},{17,1},{25,9},{2,18},{10... | collective-permute-start | bytes 442376 | tf_op jit(solution)/shard_map/ppermute | solution.py:187
  14.5 9.2 %collective-permute-start.1 = (bf16[8,8,1152]{2,1,0:T(8,128)(2,1)S(1)}, bf16[8,8,1152]{2,1,0:T(8,128)(2,1)S(1)}, u32[]{:S(2)}, u32[]{:S(2)}) collective-permute-start(bf16[8,8,1152]{2,1,0:T(8,128)(2,1)S(1)} %get-tuple-element.22), channel_id=1, source_target_pairs={{0,8},{8,16},{16,24},{24,0},{1,9},{9,17},{17,25},{25,1},{2,10},{10... | collective-permute-start | bytes 442376 | tf_op jit(solution)/shard_map/ppermute | solution.py:187
  15.4 8.3 %collective-permute-start.2 = (bf16[8,8,1152]{2,1,0:T(8,128)(2,1)S(1)}, bf16[8,8,1152]{2,1,0:T(8,128)(2,1)S(1)}, u32[]{:S(2)}, u32[]{:S(2)}) collective-permute-start(bf16[8,8,1152]{2,1,0:T(8,128)(2,1)S(1)} %get-tuple-element.23), channel_id=1, source_target_pairs={{0,24},{8,0},{16,8},{24,16},{1,25},{9,1},{17,9},{25,17},{2,26},{10... | collective-permute-start | bytes 442376 | tf_op jit(solution)/shard_map/ppermute | solution.py:187
  86.7 8.1 %collective-permute-start.11 = (bf16[64,1024]{1,0:T(8,128)(2,1)S(1)}, bf16[64,1024]{1,0:T(8,128)(2,1)S(1)}, u32[]{:S(2)}, u32[]{:S(2)}) collective-permute-start(bf16[64,1024]{1,0:T(8,128)(2,1)S(1)} %get-tuple-element.29.after_ref.refs_1_), channel_id=1, source_target_pairs={{0,16},{8,24},{16,0},{24,8},{1,17},{9,25},{17,1},{25,9},{2,18},{10... | collective-permute-start | bytes 393224 | tf_op jit(solution)/shard_map/ppermute | solution.py:187
  86.8 11.8 %collective-permute-start.10 = (bf16[64,1024]{1,0:T(8,128)(2,1)S(1)}, bf16[64,1024]{1,0:T(8,128)(2,1)S(1)}, u32[]{:S(2)}, u32[]{:S(2)}) collective-permute-start(bf16[64,1024]{1,0:T(8,128)(2,1)S(1)} %get-tuple-element.29.after_ref.refs_1_), channel_id=1, source_target_pairs={{0,8},{8,16},{16,24},{24,0},{1,9},{9,17},{17,25},{25,1},{2,10},{10... | collective-permute-start | bytes 393224 | tf_op jit(solution)/shard_map/ppermute | solution.py:187
  87.6 10.9 %collective-permute-start.9 = (bf16[64,1024]{1,0:T(8,128)(2,1)S(1)}, bf16[64,1024]{1,0:T(8,128)(2,1)S(1)}, u32[]{:S(2)}, u32[]{:S(2)}) collective-permute-start(bf16[64,1024]{1,0:T(8,128)(2,1)S(1)} %get-tuple-element.29.after_ref.refs_1_), channel_id=1, source_target_pairs={{0,24},{8,0},{16,8},{24,16},{1,25},{9,1},{17,9},{25,17},{2,26},{10... | collective-permute-start | bytes 393224 | tf_op jit(solution)/shard_map/ppermute | solution.py:187
  90.1 10.1 %collective-permute-start.8 = (bf16[64,1024]{1,0:T(8,128)(2,1)S(1)}, bf16[64,1024]{1,0:T(8,128)(2,1)S(1)}, u32[]{:S(2)}, u32[]{:S(2)}) collective-permute-start(bf16[64,1024]{1,0:T(8,128)(2,1)S(1)} %get-tuple-element.31.refs_1_), channel_id=1, source_target_pairs={{0,16},{8,24},{16,0},{24,8},{1,17},{9,25},{17,1},{25,9},{2,18},{10... | collective-permute-start | bytes 393224 | tf_op jit(solution)/shard_map/ppermute | solution.py:187
  92.3 7.9 %collective-permute-start.7 = (bf16[64,1024]{1,0:T(8,128)(2,1)S(1)}, bf16[64,1024]{1,0:T(8,128)(2,1)S(1)}, u32[]{:S(2)}, u32[]{:S(2)}) collective-permute-start(bf16[64,1024]{1,0:T(8,128)(2,1)S(1)} %get-tuple-element.31.refs_1_), channel_id=1, source_target_pairs={{0,8},{8,16},{16,24},{24,0},{1,9},{9,17},{17,25},{25,1},{2,10},{10... | collective-permute-start | bytes 393224 | tf_op jit(solution)/shard_map/ppermute | solution.py:187
  94.7 5.5 %collective-permute-start.6 = (bf16[64,1024]{1,0:T(8,128)(2,1)S(1)}, bf16[64,1024]{1,0:T(8,128)(2,1)S(1)}, u32[]{:S(2)}, u32[]{:S(2)}) collective-permute-start(bf16[64,1024]{1,0:T(8,128)(2,1)S(1)} %get-tuple-element.31.refs_1_), channel_id=1, source_target_pairs={{0,24},{8,0},{16,8},{24,16},{1,25},{9,1},{17,9},{25,17},{2,26},{10... | collective-permute-start | bytes 393224 | tf_op jit(solution)/shard_map/ppermute | solution.py:187

commit v5 on v4

--- a/solution.py
+++ b/solution.py
@@ -11,7 +11,9 @@
 F32 = jnp.float32
 BF16 = jnp.bfloat16
 SLOT_P = 4
-STAT = 128
+LANES = 128
+STAT = LANES
+STAT_ROWS = 16
 STEPS = 4
 MIB = 1 << 20
 BIG = 52
@@ -47,10 +49,14 @@
     return jnp.dot(slot_params, perm, preferred_element_type=F32).astype(BF16)
 
 
-def pack(lse):
+def thirds(lse):
     hi = lse.astype(BF16).astype(F32)
     mid = (lse - hi).astype(BF16).astype(F32)
-    low = lse - hi - mid
+    return hi, mid, lse - hi - mid
+
+
+def pack(lse):
+    hi, mid, low = thirds(lse)
     lane = lax.broadcasted_iota(jnp.int32, lse.shape[:-1] + (STAT,), lse.ndim - 1)
     return jnp.where(lane == 0, hi, jnp.where(lane == 1, mid, jnp.where(lane == 2, low, 0.0)))
 
@@ -84,11 +90,17 @@
         spread.astype(BF16), tok_ref[...], (((0,), (0,)), ((), ())), preferred_element_type=F32
     )
     slots = total.shape[1]
-    cols = jnp.concatenate([1.0 / total, peak + jnp.log(total), jnp.zeros((6, slots), F32)], axis=0).T
-    wide = jnp.concatenate([summed * cols[:, 0:1], pack(cols[:, 1:2])], axis=1)
-    wide = wide.reshape(ny, nz, groups, wide.shape[1]).astype(BF16)
+    cols = jnp.concatenate([1.0 / total, jnp.zeros((7, slots), F32)], axis=0).T
+    mean = (summed * cols[:, 0:1]).astype(BF16)
+    stat = jnp.concatenate([*thirds(peak + jnp.log(total)), jnp.zeros((13, slots), F32)], axis=0).astype(BF16)
+    rows = nz * groups
     for i in range(ny):
-        out_refs[i][...] = wide[i]
+        block = mean[i * rows : (i + 1) * rows]
+        tiles = block.shape[1] // LANES
+        for t in range(tiles):
+            out_refs[i][t * rows : (t + 1) * rows] = block[:, t * LANES : (t + 1) * LANES]
+        at = i * rows // LANES * LANES
+        out_refs[i][tiles * rows :] = stat[:, at : at + LANES]
 
 
 def combine_kernel(tok_ref, sp_ref, after_ref, out_ref, tick_ref):
@@ -110,19 +122,42 @@
     return mean, peak + jnp.log(total)
 
 
-def halfway_kernel(width, *refs):
+def along_y(rows, in_refs, store):
+    tiles = (in_refs[0].shape[0] - STAT_ROWS) // rows
+    lses = []
+    for k, ref in zip((0,) + FAR_FIRST, in_refs):
+        at = k * rows % LANES
+        stat = ref[tiles * rows :].astype(F32).T[at : at + rows]
+        lses.append(stat[:, 0:1] + stat[:, 1:2] + stat[:, 2:3])
+    peak = functools.reduce(jnp.maximum, lses)
+    weights = [jnp.exp(lse - peak) for lse in lses]
+    total = sum(weights)
+    weights = [w / total for w in weights]
+    for t in range(tiles):
+        part = slice(t * rows, (t + 1) * rows)
+        store(t, sum(ref[part].astype(F32) * w for ref, w in zip(in_refs, weights)))
+    store(tiles, pack(peak + jnp.log(total)))
+
+
+def halfway_kernel(*refs):
     in_refs, out_ref = refs[:-2], refs[-1]
-    for k in range(out_ref.shape[0]):
-        mean, lse = merged(width, [r[k] for r in in_refs])
-        out_ref[k] = jnp.concatenate([mean, pack(lse)], axis=-1).astype(BF16)
-
-
-def both_kernel(width, *refs):
+    nz, groups = out_ref.shape[:2]
+
+    def store(t, x):
+        out_ref[:, :, t * LANES : (t + 1) * LANES] = x.reshape(nz, groups, LANES).astype(BF16)
+
+    along_y(nz * groups, in_refs, store)
+
+
+def both_kernel(*refs):
     in_refs, first_ref, out_ref = refs[:-2], refs[-2], refs[-1]
-    for k in range(out_ref.shape[0]):
-        out_ref[k, 0] = first_ref[k]
-        mean, lse = merged(width, [r[k] for r in in_refs])
-        out_ref[k, 1] = jnp.concatenate([mean, pack(lse)], axis=-1).astype(BF16)
+    nz, _, groups = out_ref.shape[:3]
+
+    def store(t, x):
+        out_ref[:, 1, :, t * LANES : (t + 1) * LANES] = x.reshape(nz, groups, LANES).astype(BF16)
+
+    out_ref[:, 0] = first_ref[...]
+    along_y(nz * groups, in_refs, store)
 
 
 def merge_kernel(width, in_ref, out_ref):
@@ -202,7 +237,7 @@
             name(gather_kernel, clip, groups, ny, nz),
             in_specs=[anywhere(), anywhere()],
             out_specs=[vmem()] * (ny + len(extra)),
-            out_shape=[jax.ShapeDtypeStruct((nz, groups, wide), BF16)] * ny + extra,
+            out_shape=[jax.ShapeDtypeStruct((nz * groups * (width // LANES) + STAT_ROWS, LANES), BF16)] * ny + extra,
             scratch_shapes=[
                 pltpu.VMEM((width, slots), BF16),
                 pltpu.VMEM((length, width), BF16),
@@ -252,15 +287,16 @@
     sent1 = {k: shift(means1[k], k) for k in FAR_FIRST}
     arrived = [means0[0], *sent0.values(), means1[0], *sent1.values()]
     combine0, tick = combine(0, means1[0])
+    combine1, tick = combine(1, tick)
     halfway = small(
-        name(halfway_kernel, width),
+        halfway_kernel,
         jax.ShapeDtypeStruct((nz, groups, wide), BF16),
         "halfway",
         *arrived[:ny],
         tick,
     )
     halfway = small(
-        name(both_kernel, width),
+        both_kernel,
         jax.ShapeDtypeStruct((nz, clips, groups, wide), BF16),
         "both",
         *arrived[ny:],
@@ -279,7 +315,7 @@
     rings = small(
         split_kernel, [jax.ShapeDtypeStruct((nz * groups, width), BF16)] * clips, "split", ring
     )
-    combines = [combine0, combine(1, rings[0])[0]]
+    combines = [combine0, combine1]
     rings = [[shift(ring, -k) if k else ring for k in FAR_LAST] for ring in rings]
     mixed = None
     for clip in range(clips):

time: 103 us -> 102 us (level)
  no operation moved by 1% of the time
where the time goes in v5:
time: 102 us; the launch traced here: 101 us
  blocking collectives  60.9 us (60%)
  Pallas kernels  18.2 us (18%)
  starting transfers between devices  16.7 us (16%)
  waiting for transfers between devices  5.21 us (5%)
    all_to_all x1, blocking collectives, shards(): arrived = lax.all_to_all(halfway, around, 0, 0, tiled=True)  20.3 us
    ppermute x12, starting transfers between devices, shift(): return lax.ppermute(x, 'y', [(i, (i + k) % ny) for i in range(ny)])  16.7 us
    all_to_all x1, blocking collectives, shards(): ring = lax.all_to_all(slot_out, around, 0, 0, tiled=True)  15.4 us
    all_to_all x1, blocking collectives, shards(): own = lax.all_to_all(slot_in, sharers, 0, 0, tiled=True)  12.7 us
    all_to_all x1, blocking collectives, shards(): back = lax.all_to_all(partial, sharers, 0, 0, tiled=True)  12.5 us
    pallas_call x2, Pallas kernels, gather(): pl.pallas_call(name(gather_kernel, clip, groups, ny, nz), in_specs=[anywh...  7.66 us
    ppermute x12, waiting for transfers between devices, shift(): return lax.ppermute(x, 'y', [(i, (i + k) % ny) for i in range(ny)])  5.21 us
    pallas_call x2, Pallas kernels, combine(): pl.pallas_call(combine_kernel, grid=(2,), in_specs=[pl.BlockSpec((1, half...  5.08 us
  transfers between devices with their start and end apart: 12, of which 3 were waited for; matrix products, arithmetic and copies ran while one was open for 0% of the time, Pallas kernels for 11%

profile of v5, /device:TPU:2, one launch (start us, length us, event | category | flops | bytes accessed | tf_op | source)
XLA Modules:
  0.0 101.3 jit_solution(15663864857409295721)
XLA Ops:
  0.0 3.9 %gather0.1 = (bf16[528,128]{1,0:T(8,128)(2,1)S(1)}, bf16[528,128]{1,0:T(8,128)(2,1)S(1)}, bf16[528,128]{1,0:T(8,128)(2,1)S(1)}, bf16[528,128]{1,0:T(8,128)(2,1)S(1)}, bf16[1024,256]{1,0:T(8,128)(2,1)}) custom-call(bf16[2,1024,1024]{2,1,0:T(8,128)(2,1)} %tok_ref.3, bf16[1024,256]{1,0:T(8,128)(2,1)} %refs_1_.1), custom_call_target="tpu_custom_call" | custom-call | flops 1073741824 | bytes 2097152 | tf_op jit(solution)/shard_map/gather0/pallas_call | solution.py:236
  3.9 0.0 copy-start
  3.9 3.3 %collective-permute-start.3 = (bf16[528,128]{1,0:T(8,128)(2,1)S(1)}, bf16[528,128]{1,0:T(8,128)(2,1)S(1)}, u32[]{:S(2)}, u32[]{:S(2)}) collective-permute-start(bf16[528,128]{1,0:T(8,128)(2,1)S(1)} %get-tuple-element.28), channel_id=1, source_target_pairs={{0,16},{8,24},{16,0},{24,8},{1,17},{9,25},{17,1},{25,9},{2,18},{10... | collective-permute-start | bytes 405512 | tf_op jit(solution)/shard_map/ppermute | solution.py:222
  7.2 0.7 collective-permute-start.4
  7.9 2.6 %collective-permute-start.5 = (bf16[528,128]{1,0:T(8,128)(2,1)S(1)}, bf16[528,128]{1,0:T(8,128)(2,1)S(1)}, u32[]{:S(2)}, u32[]{:S(2)}) collective-permute-start(bf16[528,128]{1,0:T(8,128)(2,1)S(1)} %get-tuple-element.30), channel_id=1, source_target_pairs={{0,24},{8,0},{16,8},{24,16},{1,25},{9,1},{17,9},{25,17},{2,26},{10... | collective-permute-start | bytes 405512 | tf_op jit(solution)/shard_map/ppermute | solution.py:222
  10.5 3.7 %gather1.1 = (bf16[528,128]{1,0:T(8,128)(2,1)S(1)}, bf16[528,128]{1,0:T(8,128)(2,1)S(1)}, bf16[528,128]{1,0:T(8,128)(2,1)S(1)}, bf16[528,128]{1,0:T(8,128)(2,1)S(1)}) custom-call(bf16[2,1024,1024]{2,1,0:T(8,128)(2,1)} %tok_ref.3, bf16[1024,256]{1,0:T(8,128)(2,1)} %get-tuple-element.20.refs_1_.sp_ref), custom_call_target="tpu_custom_call" | custom-call | flops 1073741824 | bytes 2097152 | tf_op jit(solution)/shard_map/gather1/pallas_call | solution.py:236
  14.2 0.1 collective-permute-start
  14.3 0.8 collective-permute-start.1
  15.2 2.5 %collective-permute-start.2 = (bf16[528,128]{1,0:T(8,128)(2,1)S(1)}, bf16[528,128]{1,0:T(8,128)(2,1)S(1)}, u32[]{:S(2)}, u32[]{:S(2)}) collective-permute-start(bf16[528,128]{1,0:T(8,128)(2,1)S(1)} %get-tuple-element.26), channel_id=1, source_target_pairs={{0,24},{8,0},{16,8},{24,16},{1,25},{9,1},{17,9},{25,17},{2,26},{10... | collective-permute-start | bytes 405512 | tf_op jit(solution)/shard_map/ppermute | solution.py:222
  17.6 2.5 %combine0.1 = (bf16[1024,256]{1,0:T(8,128)(2,1)S(1)}, f32[8,128]{1,0:T(8,128)S(1)}) custom-call(bf16[2,1024,1024]{2,1,0:T(8,128)(2,1)} %tok_ref.3, bf16[1024,256]{1,0:T(8,128)(2,1)S(1)} %copy-done, bf16[528,128]{1,0:T(8,128)(2,1)S(1)} %get-tuple-element.21.after_ref.refs_0_), custom_call_target="tpu_custom_call" | custom-call | flops 536870912 | bytes 2621440 | tf_op jit(solution)/shard_map/combine0/pallas_call | solution.py:258
  20.1 0.0 copy-start.1
  20.1 0.0 copy-start.2
  20.1 2.6 %combine1.1 = (bf16[1024,256]{1,0:T(8,128)(2,1)S(1)}, f32[8,128]{1,0:T(8,128)S(1)}) custom-call(bf16[2,1024,1024]{2,1,0:T(8,128)(2,1)} %tok_ref.3, bf16[1024,256]{1,0:T(8,128)(2,1)S(1)} %copy-done, f32[8,128]{1,0:T(8,128)S(1)} %get-tuple-element.22.after_ref), custom_call_target="tpu_custom_call" | custom-call | flops 536870912 | bytes 2621440 | tf_op jit(solution)/shard_map/combine1/pallas_call | solution.py:258
  22.8 0.4 halfway.1.refs_4_
  23.2 0.4 both.1
  23.6 20.3 %all_to_all.20.refs_0_ = bf16[8,2,8,1152]{3,2,1,0:T(8,128)(2,1)S(1)} all-to-all(bf16[8,2,8,1152]{3,2,1,0:T(8,128)(2,1)S(1)} %both.1), channel_id=1, replica_groups=mesh['group'=8,'y'=4,'zh'=2,'quarter'=4] {'zh','quarter'}, dimensions={0} | all-to-all | bytes 589824 | tf_op jit(solution)/shard_map/all_to_all | solution.py:305
  43.9 0.3 merge.1
  44.2 12.7 %all_to_all.21.x_ref = bf16[32,2,1024]{2,1,0:T(2,128)(2,1)S(1)} all-to-all(bf16[32,2,1024]{2,1,0:T(2,128)(2,1)S(1)} %merge.1), channel_id=1, replica_groups=mesh['group'=8,'y'=4,'zh'=2,'quarter'=4] {'group','quarter'}, dimensions={0} | all-to-all | bytes 262144 | tf_op jit(solution)/shard_map/all_to_all | solution.py:308
  56.9 1.0 expert.1
  57.8 12.5 %all_to_all.22.x_ref = bf16[32,2,1024]{2,1,0:T(2,128)(2,1)S(1)} all-to-all(bf16[32,2,1024]{2,1,0:T(2,128)(2,1)S(1)} %expert.1), channel_id=1, replica_groups=mesh['group'=8,'y'=4,'zh'=2,'quarter'=4] {'group','quarter'}, dimensions={0} | all-to-all | bytes 262144 | tf_op jit(solution)/shard_map/all_to_all | solution.py:310
  70.4 0.1 total.1
  70.5 15.4 %all_to_all.23.in_ref = bf16[8,2,8,1024]{3,2,1,0:T(8,128)(2,1)S(1)} all-to-all(bf16[8,2,8,1024]{3,2,1,0:T(8,128)(2,1)S(1)} %total.1), channel_id=1, replica_groups=mesh['group'=8,'y'=4,'zh'=2,'quarter'=4] {'zh','quarter'}, dimensions={0} | all-to-all | bytes 524288 | tf_op jit(solution)/shard_map/all_to_all | solution.py:314
  85.9 1.4 %collective-permute-start.11 = (bf16[64,1024]{1,0:T(8,128)(2,1)S(1)}, bf16[64,1024]{1,0:T(8,128)(2,1)S(1)}, u32[]{:S(2)}, u32[]{:S(2)}) collective-permute-start(bf16[64,1024]{1,0:T(8,128)(2,1)S(1)} %get-tuple-element.34.refs_1_), channel_id=1, source_target_pairs={{0,16},{8,24},{16,0},{24,8},{1,17},{9,25},{17,1},{25,9},{2,18},{10... | collective-permute-start | bytes 393224 | tf_op jit(solution)/shard_map/ppermute | solution.py:222
  87.3 0.0 collective-permute-start.10
  87.3 3.2 %collective-permute-start.9 = (bf16[64,1024]{1,0:T(8,128)(2,1)S(1)}, bf16[64,1024]{1,0:T(8,128)(2,1)S(1)}, u32[]{:S(2)}, u32[]{:S(2)}) collective-permute-start(bf16[64,1024]{1,0:T(8,128)(2,1)S(1)} %get-tuple-element.34.refs_1_), channel_id=1, source_target_pairs={{0,24},{8,0},{16,8},{24,16},{1,25},{9,1},{17,9},{25,17},{2,26},{10... | collective-permute-start | bytes 393224 | tf_op jit(solution)/shard_map/ppermute | solution.py:222
  90.6 1.0 %collective-permute-start.8 = (bf16[64,1024]{1,0:T(8,128)(2,1)S(1)}, bf16[64,1024]{1,0:T(8,128)(2,1)S(1)}, u32[]{:S(2)}, u32[]{:S(2)}) collective-permute-start(bf16[64,1024]{1,0:T(8,128)(2,1)S(1)} %get-tuple-element.32.refs_1_), channel_id=1, source_target_pairs={{0,16},{8,24},{16,0},{24,8},{1,17},{9,25},{17,1},{25,9},{2,18},{10... | collective-permute-start | bytes 393224 | tf_op jit(solution)/shard_map/ppermute | solution.py:222
  91.6 2.2 %collective-permute-done.11.refs_4_ = bf16[64,1024]{1,0:T(8,128)(2,1)S(1)} collective-permute-done((bf16[64,1024]{1,0:T(8,128)(2,1)S(1)}, bf16[64,1024]{1,0:T(8,128)(2,1)S(1)}, u32[]{:S(2)}, u32[]{:S(2)}) %collective-permute-start.11) | collective-permute-done | bytes 131104 | tf_op jit(solution)/shard_map/ppermute | solution.py:222
  93.7 1.1 %collective-permute-start.6 = (bf16[64,1024]{1,0:T(8,128)(2,1)S(1)}, bf16[64,1024]{1,0:T(8,128)(2,1)S(1)}, u32[]{:S(2)}, u32[]{:S(2)}) collective-permute-start(bf16[64,1024]{1,0:T(8,128)(2,1)S(1)} %get-tuple-element.32.refs_1_), channel_id=1, source_target_pairs={{0,24},{8,0},{16,8},{24,16},{1,25},{9,1},{17,9},{25,17},{2,26},{10... | collective-permute-start | bytes 393224 | tf_op jit(solution)/shard_map/ppermute | solution.py:222
  94.8 2.1 %collective-permute-done.10.refs_3_ = bf16[64,1024]{1,0:T(8,128)(2,1)S(1)} collective-permute-done((bf16[64,1024]{1,0:T(8,128)(2,1)S(1)}, bf16[64,1024]{1,0:T(8,128)(2,1)S(1)}, u32[]{:S(2)}, u32[]{:S(2)}) %collective-permute-start.10) | collective-permute-done | bytes 131104 | tf_op jit(solution)/shard_map/ppermute | solution.py:222
  96.9 1.6 %mix0.1.refs_5_ = bf16[2,1024,1024]{2,1,0:T(8,128)(2,1)} custom-call(bf16[1024,256]{1,0:T(8,128)(2,1)S(1)} %get-tuple-element.33.refs_0_, bf16[64,1024]{1,0:T(8,128)(2,1)S(1)} %get-tuple-element.34.refs_1_, bf16[64,1024]{1,0:T(8,128)(2,1)S(1)} %collective-permute-done.9.refs_2_, bf16[64,1024]{1,0:T(8,128)(2,1)S(1)} %collective-permute-done.10.refs_3_, ...), custom_call_target="tpu_custom_call" | custom-call | flops 536870912 | bytes 2621440 | tf_op jit(solution)/shard_map/mix0/pallas_call | solution.py:323
  98.6 0.9 collective-permute-done.7.refs_3_
  99.5 1.6 %mix1.1 = bf16[2,1024,1024]{2,1,0:T(8,128)(2,1)} custom-call(bf16[1024,256]{1,0:T(8,128)(2,1)S(1)} %get-tuple-element.23.refs_0_, bf16[64,1024]{1,0:T(8,128)(2,1)S(1)} %get-tuple-element.32.refs_1_, bf16[64,1024]{1,0:T(8,128)(2,1)S(1)} %collective-permute-done.6.refs_2_, ...), custom_call_target="tpu_custom_call", output_to_operand_aliasing={{}: (5, {})} | custom-call | flops 536870912 | bytes 2621440 | tf_op jit(solution)/shard_map/mix1/pallas_call | solution.py:323
  (14 shorter events, 0.1 us)
Async XLA Ops:
  3.9 13.7 %copy-start = (bf16[1024,256]{1,0:T(8,128)(2,1)S(1)}, bf16[1024,256]{1,0:T(8,128)(2,1)}, u32[]{:S(2)}) copy-start(bf16[1024,256]{1,0:T(8,128)(2,1)} %get-tuple-element.20.refs_1_.sp_ref) | copy-start | bytes 1572868
  3.9 11.2 %collective-permute-start.3 = (bf16[528,128]{1,0:T(8,128)(2,1)S(1)}, bf16[528,128]{1,0:T(8,128)(2,1)S(1)}, u32[]{:S(2)}, u32[]{:S(2)}) collective-permute-start(bf16[528,128]{1,0:T(8,128)(2,1)S(1)} %get-tuple-element.28), channel_id=1, source_target_pairs={{0,16},{8,24},{16,0},{24,8},{1,17},{9,25},{17,1},{25,9},{2,18},{10... | collective-permute-start | bytes 405512 | tf_op jit(solution)/shard_map/ppermute | solution.py:222
  7.2 15.5 %collective-permute-start.4 = (bf16[528,128]{1,0:T(8,128)(2,1)S(1)}, bf16[528,128]{1,0:T(8,128)(2,1)S(1)}, u32[]{:S(2)}, u32[]{:S(2)}) collective-permute-start(bf16[528,128]{1,0:T(8,128)(2,1)S(1)} %get-tuple-element.29), channel_id=1, source_target_pairs={{0,8},{8,16},{16,24},{24,0},{1,9},{9,17},{17,25},{25,1},{2,10},{10... | collective-permute-start | bytes 405512 | tf_op jit(solution)/shard_map/ppermute | solution.py:222
  7.9 14.9 %collective-permute-start.5 = (bf16[528,128]{1,0:T(8,128)(2,1)S(1)}, bf16[528,128]{1,0:T(8,128)(2,1)S(1)}, u32[]{:S(2)}, u32[]{:S(2)}) collective-permute-start(bf16[528,128]{1,0:T(8,128)(2,1)S(1)} %get-tuple-element.30), channel_id=1, source_target_pairs={{0,24},{8,0},{16,8},{24,16},{1,25},{9,1},{17,9},{25,17},{2,26},{10... | collective-permute-start | bytes 405512 | tf_op jit(solution)/shard_map/ppermute | solution.py:222
  14.2 8.9 %collective-permute-start = (bf16[528,128]{1,0:T(8,128)(2,1)S(1)}, bf16[528,128]{1,0:T(8,128)(2,1)S(1)}, u32[]{:S(2)}, u32[]{:S(2)}) collective-permute-start(bf16[528,128]{1,0:T(8,128)(2,1)S(1)} %get-tuple-element.24), channel_id=1, source_target_pairs={{0,16},{8,24},{16,0},{24,8},{1,17},{9,25},{17,1},{25,9},{2,18},{10... | collective-permute-start | bytes 405512 | tf_op jit(solution)/shard_map/ppermute | solution.py:222
  14.3 8.9 %collective-permute-start.1 = (bf16[528,128]{1,0:T(8,128)(2,1)S(1)}, bf16[528,128]{1,0:T(8,128)(2,1)S(1)}, u32[]{:S(2)}, u32[]{:S(2)}) collective-permute-start(bf16[528,128]{1,0:T(8,128)(2,1)S(1)} %get-tuple-element.25), channel_id=1, source_target_pairs={{0,8},{8,16},{16,24},{24,0},{1,9},{9,17},{17,25},{25,1},{2,10},{10... | collective-permute-start | bytes 405512 | tf_op jit(solution)/shard_map/ppermute | solution.py:222
  15.2 8.0 %collective-permute-start.2 = (bf16[528,128]{1,0:T(8,128)(2,1)S(1)}, bf16[528,128]{1,0:T(8,128)(2,1)S(1)}, u32[]{:S(2)}, u32[]{:S(2)}) collective-permute-start(bf16[528,128]{1,0:T(8,128)(2,1)S(1)} %get-tuple-element.26), channel_id=1, source_target_pairs={{0,24},{8,0},{16,8},{24,16},{1,25},{9,1},{17,9},{25,17},{2,26},{10... | collective-permute-start | bytes 405512 | tf_op jit(solution)/shard_map/ppermute | solution.py:222
  20.1 36.8 %copy-start.1 = (bf16[1024,1024]{1,0:T(8,128)(2,1)S(1)}, bf16[1024,1024]{1,0:T(8,128)(2,1)}, u32[]{:S(2)}) copy-start(bf16[1024,1024]{1,0:T(8,128)(2,1)} %up_ref.1) | copy-start | bytes 6291460
  20.1 36.7 %copy-start.2 = (bf16[1024,1024]{1,0:T(8,128)(2,1)S(1)}, bf16[1024,1024]{1,0:T(8,128)(2,1)}, u32[]{:S(2)}) copy-start(bf16[1024,1024]{1,0:T(8,128)(2,1)} %down_ref.1) | copy-start | bytes 6291460
  85.9 7.8 %collective-permute-start.11 = (bf16[64,1024]{1,0:T(8,128)(2,1)S(1)}, bf16[64,1024]{1,0:T(8,128)(2,1)S(1)}, u32[]{:S(2)}, u32[]{:S(2)}) collective-permute-start(bf16[64,1024]{1,0:T(8,128)(2,1)S(1)} %get-tuple-element.34.refs_1_), channel_id=1, source_target_pairs={{0,16},{8,24},{16,0},{24,8},{1,17},{9,25},{17,1},{25,9},{2,18},{10... | collective-permute-start | bytes 393224 | tf_op jit(solution)/shard_map/ppermute | solution.py:222
  87.3 9.6 %collective-permute-start.10 = (bf16[64,1024]{1,0:T(8,128)(2,1)S(1)}, bf16[64,1024]{1,0:T(8,128)(2,1)S(1)}, u32[]{:S(2)}, u32[]{:S(2)}) collective-permute-start(bf16[64,1024]{1,0:T(8,128)(2,1)S(1)} %get-tuple-element.34.refs_1_), channel_id=1, source_target_pairs={{0,8},{8,16},{16,24},{24,0},{1,9},{9,17},{17,25},{25,1},{2,10},{10... | collective-permute-start | bytes 393224 | tf_op jit(solution)/shard_map/ppermute | solution.py:222
  87.3 9.6 %collective-permute-start.9 = (bf16[64,1024]{1,0:T(8,128)(2,1)S(1)}, bf16[64,1024]{1,0:T(8,128)(2,1)S(1)}, u32[]{:S(2)}, u32[]{:S(2)}) collective-permute-start(bf16[64,1024]{1,0:T(8,128)(2,1)S(1)} %get-tuple-element.34.refs_1_), channel_id=1, source_target_pairs={{0,24},{8,0},{16,8},{24,16},{1,25},{9,1},{17,9},{25,17},{2,26},{10... | collective-permute-start | bytes 393224 | tf_op jit(solution)/shard_map/ppermute | solution.py:222
  90.6 8.0 %collective-permute-start.8 = (bf16[64,1024]{1,0:T(8,128)(2,1)S(1)}, bf16[64,1024]{1,0:T(8,128)(2,1)S(1)}, u32[]{:S(2)}, u32[]{:S(2)}) collective-permute-start(bf16[64,1024]{1,0:T(8,128)(2,1)S(1)} %get-tuple-element.32.refs_1_), channel_id=1, source_target_pairs={{0,16},{8,24},{16,0},{24,8},{1,17},{9,25},{17,1},{25,9},{2,18},{10... | collective-permute-start | bytes 393224 | tf_op jit(solution)/shard_map/ppermute | solution.py:222
  91.6 7.9 %collective-permute-start.7 = (bf16[64,1024]{1,0:T(8,128)(2,1)S(1)}, bf16[64,1024]{1,0:T(8,128)(2,1)S(1)}, u32[]{:S(2)}, u32[]{:S(2)}) collective-permute-start(bf16[64,1024]{1,0:T(8,128)(2,1)S(1)} %get-tuple-element.32.refs_1_), channel_id=1, source_target_pairs={{0,8},{8,16},{16,24},{24,0},{1,9},{9,17},{17,25},{25,1},{2,10},{10... | collective-permute-start | bytes 393224 | tf_op jit(solution)/shard_map/ppermute | solution.py:222
  93.7 5.8 %collective-permute-start.6 = (bf16[64,1024]{1,0:T(8,128)(2,1)S(1)}, bf16[64,1024]{1,0:T(8,128)(2,1)S(1)}, u32[]{:S(2)}, u32[]{:S(2)}) collective-permute-start(bf16[64,1024]{1,0:T(8,128)(2,1)S(1)} %get-tuple-element.32.refs_1_), channel_id=1, source_target_pairs={{0,24},{8,0},{16,8},{24,16},{1,25},{9,1},{17,9},{25,17},{2,26},{10... | collective-permute-start | bytes 393224 | tf_op jit(solution)/shard_map/ppermute | solution.py:222

commit v6 on v5

--- a/solution.py
+++ b/solution.py
@@ -17,6 +17,7 @@
 STEPS = 4
 MIB = 1 << 20
 BIG = 52
+LATE = 48
 FAR_FIRST = (2, 1, 3)
 FAR_LAST = (0, 1, 3, 2)
 
@@ -160,7 +161,7 @@
     along_y(nz * groups, in_refs, store)
 
 
-def merge_kernel(width, in_ref, out_ref):
+def merge_kernel(width, in_ref, after_ref, out_ref):
     nz, clips, groups = in_ref.shape[:3]
     acc, _ = merged(width, [in_ref[k] for k in range(nz)])
     for g in range(groups):
@@ -271,7 +272,7 @@
                 jax.ShapeDtypeStruct((length, slots), BF16),
                 jax.ShapeDtypeStruct((8, STAT), F32),
             ],
-            compiler_params=params(BIG),
+            compiler_params=params(BIG if clip == 0 else LATE),
             cost_estimate=pl.CostEstimate(
                 flops=2 * length * width * slots,
                 bytes_accessed=2 * length * (width + slots),
@@ -287,7 +288,6 @@
     sent1 = {k: shift(means1[k], k) for k in FAR_FIRST}
     arrived = [means0[0], *sent0.values(), means1[0], *sent1.values()]
     combine0, tick = combine(0, means1[0])
-    combine1, tick = combine(1, tick)
     halfway = small(
         halfway_kernel,
         jax.ShapeDtypeStruct((nz, groups, wide), BF16),
@@ -303,8 +303,9 @@
         halfway,
     )
     arrived = lax.all_to_all(halfway, around, 0, 0, tiled=True)
+    combine1, tick = combine(1, halfway)
     rows = jax.ShapeDtypeStruct((groups * SLOT_P, clips, width), BF16)
-    slot_in = small(name(merge_kernel, width), rows, "merge", arrived)
+    slot_in = small(name(merge_kernel, width), rows, "merge", arrived, tick)
     own = lax.all_to_all(slot_in, sharers, 0, 0, tiled=True)
     partial = small(expert_kernel, rows, "expert", own, w_up, w_down)
     back = lax.all_to_all(partial, sharers, 0, 0, tiled=True)

time: 102 us -> 103 us (level)
  blocking collectives: 60.9 us -> 39.8 us
  waiting for transfers between devices: 5.21 us -> 14.4 us
  starting transfers between devices: 16.7 us -> 25.3 us
  local copies, waits for them, and re-layouts: 0.02 us -> 4.59 us
    all_to_all x1 -> x0, blocking collectives: 20.3 us -> none  [shards(): arrived = lax.all_to_all(halfway, around, 0, 0, tiled=True)]
    all_to_all x0 -> x1, starting transfers between devices: none -> 8.46 us  [shards(): arrived = lax.all_to_all(halfway, around, 0, 0, tiled=True)]
    all_to_all x0 -> x1, waiting for transfers between devices: none -> 7.36 us  [shards(): arrived = lax.all_to_all(halfway, around, 0, 0, tiled=True)]
    unnamed x6 -> x12, local copies, waits for them, and re-layouts: 0.02 us -> 4.59 us
    ppermute x12, waiting for transfers between devices: 5.21 us -> 7.02 us  [shift(): return lax.ppermute(x, 'y', [(i, (i + k) % ny) for i in range(ny)])]
  transfers between devices with their start and end apart: 12 -> 13, of which waited for: 3 -> 6; matrix products, arithmetic and copies ran while one was open for 0% -> 0% of each run, Pallas kernels for 11% -> 10%
where the time goes in v6:
time: 103 us
  blocking collectives  39.8 us (39%)
  starting transfers between devices  25.3 us (25%)
  Pallas kernels  18.2 us (18%)
  waiting for transfers between devices  14.4 us (14%)
  local copies, waits for them, and re-layouts  4.59 us (4%)
    ppermute x12, starting transfers between devices, shift(): return lax.ppermute(x, 'y', [(i, (i + k) % ny) for i in range(ny)])  16.8 us
    all_to_all x1, blocking collectives, shards(): ring = lax.all_to_all(slot_out, around, 0, 0, tiled=True)  14.5 us
    all_to_all x1, blocking collectives, shards(): own = lax.all_to_all(slot_in, sharers, 0, 0, tiled=True)  12.7 us
    all_to_all x1, blocking collectives, shards(): back = lax.all_to_all(partial, sharers, 0, 0, tiled=True)  12.7 us
    all_to_all x1, starting transfers between devices, shards(): arrived = lax.all_to_all(halfway, around, 0, 0, tiled=True)  8.46 us
    pallas_call x2, Pallas kernels, gather(): pl.pallas_call(name(gather_kernel, clip, groups, ny, nz), in_specs=[anywh...  7.66 us
    all_to_all x1, waiting for transfers between devices, shards(): arrived = lax.all_to_all(halfway, around, 0, 0, tiled=True)  7.36 us
    ppermute x12, waiting for transfers between devices, shift(): return lax.ppermute(x, 'y', [(i, (i + k) % ny) for i in range(ny)])  7.02 us
  transfers between devices with their start and end apart: 13, of which 6 were waited for; matrix products, arithmetic and copies ran while one was open for 0% of the time, Pallas kernels for 10%

profile of v6, /device:TPU:2, one launch (start us, length us, event | category | flops | bytes accessed | tf_op | source)
XLA Modules:
  0.0 102.6 jit_solution(3839052195346311660)
XLA Ops:
  0.0 3.9 %gather0.1 = (bf16[528,128]{1,0:T(8,128)(2,1)S(1)}, bf16[528,128]{1,0:T(8,128)(2,1)S(1)}, bf16[528,128]{1,0:T(8,128)(2,1)S(1)}, bf16[528,128]{1,0:T(8,128)(2,1)S(1)}, bf16[1024,256]{1,0:T(8,128)(2,1)}) custom-call(bf16[2,1024,1024]{2,1,0:T(8,128)(2,1)} %tok_ref.3, bf16[1024,256]{1,0:T(8,128)(2,1)} %refs_1_.1), custom_call_target="tpu_custom_call" | custom-call | flops 1073741824 | bytes 2097152 | tf_op jit(solution)/shard_map/gather0/pallas_call | solution.py:237
  3.9 3.3 %collective-permute-start.3 = (bf16[528,128]{1,0:T(8,128)(2,1)S(1)}, bf16[528,128]{1,0:T(8,128)(2,1)S(1)}, u32[]{:S(2)}, u32[]{:S(2)}) collective-permute-start(bf16[528,128]{1,0:T(8,128)(2,1)S(1)} %get-tuple-element.26), channel_id=1, source_target_pairs={{0,16},{8,24},{16,0},{24,8},{1,17},{9,25},{17,1},{25,9},{2,18},{10... | collective-permute-start | bytes 405512 | tf_op jit(solution)/shard_map/ppermute | solution.py:223
  7.2 0.7 collective-permute-start.4
  7.9 2.6 %collective-permute-start.5 = (bf16[528,128]{1,0:T(8,128)(2,1)S(1)}, bf16[528,128]{1,0:T(8,128)(2,1)S(1)}, u32[]{:S(2)}, u32[]{:S(2)}) collective-permute-start(bf16[528,128]{1,0:T(8,128)(2,1)S(1)} %get-tuple-element.28), channel_id=1, source_target_pairs={{0,24},{8,0},{16,8},{24,16},{1,25},{9,1},{17,9},{25,17},{2,26},{10... | collective-permute-start | bytes 405512 | tf_op jit(solution)/shard_map/ppermute | solution.py:223
  10.5 3.7 %gather1.1 = (bf16[528,128]{1,0:T(8,128)(2,1)S(1)}, bf16[528,128]{1,0:T(8,128)(2,1)S(1)}, bf16[528,128]{1,0:T(8,128)(2,1)S(1)}, bf16[528,128]{1,0:T(8,128)(2,1)S(1)}) custom-call(bf16[2,1024,1024]{2,1,0:T(8,128)(2,1)} %tok_ref.3, bf16[1024,256]{1,0:T(8,128)(2,1)} %get-tuple-element.20.refs_1_.sp_ref), custom_call_target="tpu_custom_call" | custom-call | flops 1073741824 | bytes 2097152 | tf_op jit(solution)/shard_map/gather1/pallas_call | solution.py:237
  14.3 0.8 collective-permute-start.1
  15.2 2.5 %collective-permute-start.2 = (bf16[528,128]{1,0:T(8,128)(2,1)S(1)}, bf16[528,128]{1,0:T(8,128)(2,1)S(1)}, u32[]{:S(2)}, u32[]{:S(2)}) collective-permute-start(bf16[528,128]{1,0:T(8,128)(2,1)S(1)} %get-tuple-element.24), channel_id=1, source_target_pairs={{0,24},{8,0},{16,8},{24,16},{1,25},{9,1},{17,9},{25,17},{2,26},{10... | collective-permute-start | bytes 405512 | tf_op jit(solution)/shard_map/ppermute | solution.py:223
  17.6 2.5 %combine0.1 = (bf16[1024,256]{1,0:T(8,128)(2,1)S(1)}, f32[8,128]{1,0:T(8,128)S(1)}) custom-call(bf16[2,1024,1024]{2,1,0:T(8,128)(2,1)} %tok_ref.3, bf16[1024,256]{1,0:T(8,128)(2,1)S(1)} %copy-done.1, bf16[528,128]{1,0:T(8,128)(2,1)S(1)} %get-tuple-element.21.after_ref.refs_0_), custom_call_target="tpu_custom_call" | custom-call | flops 536870912 | bytes 2621440 | tf_op jit(solution)/shard_map/combine0/pallas_call | solution.py:259
  20.1 0.4 halfway.1.refs_4_
  20.5 1.3 %collective-permute-done.refs_1_ = bf16[528,128]{1,0:T(8,128)(2,1)S(1)} collective-permute-done((bf16[528,128]{1,0:T(8,128)(2,1)S(1)}, bf16[528,128]{1,0:T(8,128)(2,1)S(1)}, u32[]{:S(2)}, u32[]{:S(2)}) %collective-permute-start) | collective-permute-done | bytes 135200 | tf_op jit(solution)/shard_map/ppermute | solution.py:223
  21.8 1.1 %collective-permute-done.1.refs_2_ = bf16[528,128]{1,0:T(8,128)(2,1)S(1)} collective-permute-done((bf16[528,128]{1,0:T(8,128)(2,1)S(1)}, bf16[528,128]{1,0:T(8,128)(2,1)S(1)}, u32[]{:S(2)}, u32[]{:S(2)}) %collective-permute-start.1) | collective-permute-done | bytes 135200 | tf_op jit(solution)/shard_map/ppermute | solution.py:223
  23.0 1.1 %both.1.after_ref = bf16[8,2,8,1152]{3,2,1,0:T(8,128)(2,1)} custom-call(bf16[528,128]{1,0:T(8,128)(2,1)S(1)} %get-tuple-element.21.after_ref.refs_0_, bf16[528,128]{1,0:T(8,128)(2,1)S(1)} %collective-permute-done.refs_1_, bf16[528,128]{1,0:T(8,128)(2,1)S(1)} %collective-permute-done.1.refs_2_, bf16[528,128]{1,0:T(8,128)(2,1)S(1)} %collective-permute-done.2.refs_3_, ...), custom_call_target="tpu_custom_call" | custom-call | tf_op jit(solution)/shard_map/both/pallas_call | solution.py:226
  24.1 8.5 %all-to-all-start = ((bf16[8,2,8,1152]{3,2,1,0:T(8,128)(2,1)}), bf16[8,2,8,1152]{3,2,1,0:T(8,128)(2,1)S(1)}, u32[]{:S(2)}, u32[]{:S(2)}) async-start(bf16[8,2,8,1152]{3,2,1,0:T(8,128)(2,1)} %both.1.after_ref), calls=%async_computation | async-start | bytes 589824 | tf_op jit(solution)/shard_map/all_to_all | solution.py:305
  32.5 2.2 %copy-done = bf16[2,1024,1024]{2,1,0:T(8,128)(2,1)S(1)} copy-done((bf16[2,1024,1024]{2,1,0:T(8,128)(2,1)S(1)}, bf16[2,1024,1024]{2,1,0:T(8,128)(2,1)}, u32[]{:S(2)}) %copy-start) | copy-done | bytes 4194328
  34.7 1.9 %combine1.1 = (bf16[1024,256]{1,0:T(8,128)(2,1)S(1)}, f32[8,128]{1,0:T(8,128)S(1)}) custom-call(bf16[2,1024,1024]{2,1,0:T(8,128)(2,1)S(1)} %copy-done, bf16[1024,256]{1,0:T(8,128)(2,1)S(1)} %copy-done.1, bf16[8,2,8,1152]{3,2,1,0:T(8,128)(2,1)} %both.1.after_ref), custom_call_target="tpu_custom_call" | custom-call | flops 536870912 | bytes 2621440 | tf_op jit(solution)/shard_map/combine1/pallas_call | solution.py:259
  36.7 0.8 copy-done.4
  37.5 7.4 %all-to-all-done.refs_0_ = bf16[8,2,8,1152]{3,2,1,0:T(8,128)(2,1)S(1)} async-done(((bf16[8,2,8,1152]{3,2,1,0:T(8,128)(2,1)}), bf16[8,2,8,1152]{3,2,1,0:T(8,128)(2,1)S(1)}, u32[]{:S(2)}, u32[]{:S(2)}) %all-to-all-start) | async-done | bytes 294944 | tf_op jit(solution)/shard_map/all_to_all | solution.py:305
  45.1 12.7 %all_to_all.20.x_ref = bf16[32,2,1024]{2,1,0:T(2,128)(2,1)S(1)} all-to-all(bf16[32,2,1024]{2,1,0:T(2,128)(2,1)S(1)} %merge.1), channel_id=1, replica_groups=mesh['group'=8,'y'=4,'zh'=2,'quarter'=4] {'group','quarter'}, dimensions={0} | all-to-all | bytes 262144 | tf_op jit(solution)/shard_map/all_to_all | solution.py:309
  57.8 1.6 %copy-done.3 = bf16[1024,1024]{1,0:T(8,128)(2,1)S(1)} copy-done((bf16[1024,1024]{1,0:T(8,128)(2,1)S(1)}, bf16[1024,1024]{1,0:T(8,128)(2,1)}, u32[]{:S(2)}) %copy-start.3) | copy-done | bytes 2097176
  59.4 1.0 expert.1
  60.3 12.7 %all_to_all.21.x_ref = bf16[32,2,1024]{2,1,0:T(2,128)(2,1)S(1)} all-to-all(bf16[32,2,1024]{2,1,0:T(2,128)(2,1)S(1)} %expert.1), channel_id=1, replica_groups=mesh['group'=8,'y'=4,'zh'=2,'quarter'=4] {'group','quarter'}, dimensions={0} | all-to-all | bytes 262144 | tf_op jit(solution)/shard_map/all_to_all | solution.py:311
  73.2 14.5 %all_to_all.22.in_ref = bf16[8,2,8,1024]{3,2,1,0:T(8,128)(2,1)S(1)} all-to-all(bf16[8,2,8,1024]{3,2,1,0:T(8,128)(2,1)S(1)} %total.1), channel_id=1, replica_groups=mesh['group'=8,'y'=4,'zh'=2,'quarter'=4] {'zh','quarter'}, dimensions={0} | all-to-all | bytes 524288 | tf_op jit(solution)/shard_map/all_to_all | solution.py:315
  87.7 0.6 collective-permute-start.11
  88.3 1.3 %collective-permute-start.10 = (bf16[64,1024]{1,0:T(8,128)(2,1)S(1)}, bf16[64,1024]{1,0:T(8,128)(2,1)S(1)}, u32[]{:S(2)}, u32[]{:S(2)}) collective-permute-start(bf16[64,1024]{1,0:T(8,128)(2,1)S(1)} %get-tuple-element.34.refs_1_), channel_id=1, source_target_pairs={{0,8},{8,16},{16,24},{24,0},{1,9},{9,17},{17,25},{25,1},{2,10},{10... | collective-permute-start | bytes 393224 | tf_op jit(solution)/shard_map/ppermute | solution.py:223
  89.6 1.9 %collective-permute-start.9 = (bf16[64,1024]{1,0:T(8,128)(2,1)S(1)}, bf16[64,1024]{1,0:T(8,128)(2,1)S(1)}, u32[]{:S(2)}, u32[]{:S(2)}) collective-permute-start(bf16[64,1024]{1,0:T(8,128)(2,1)S(1)} %get-tuple-element.34.refs_1_), channel_id=1, source_target_pairs={{0,24},{8,0},{16,8},{24,16},{1,25},{9,1},{17,9},{25,17},{2,26},{10... | collective-permute-start | bytes 393224 | tf_op jit(solution)/shard_map/ppermute | solution.py:223
  91.5 1.8 %collective-permute-start.8 = (bf16[64,1024]{1,0:T(8,128)(2,1)S(1)}, bf16[64,1024]{1,0:T(8,128)(2,1)S(1)}, u32[]{:S(2)}, u32[]{:S(2)}) collective-permute-start(bf16[64,1024]{1,0:T(8,128)(2,1)S(1)} %get-tuple-element.32.refs_1_), channel_id=1, source_target_pairs={{0,16},{8,24},{16,0},{24,8},{1,17},{9,25},{17,1},{25,9},{2,18},{10... | collective-permute-start | bytes 393224 | tf_op jit(solution)/shard_map/ppermute | solution.py:223
  93.5 2.1 %collective-permute-done.11.refs_4_ = bf16[64,1024]{1,0:T(8,128)(2,1)S(1)} collective-permute-done((bf16[64,1024]{1,0:T(8,128)(2,1)S(1)}, bf16[64,1024]{1,0:T(8,128)(2,1)S(1)}, u32[]{:S(2)}, u32[]{:S(2)}) %collective-permute-start.11) | collective-permute-done | bytes 131104 | tf_op jit(solution)/shard_map/ppermute | solution.py:223
  95.6 1.0 %collective-permute-start.6 = (bf16[64,1024]{1,0:T(8,128)(2,1)S(1)}, bf16[64,1024]{1,0:T(8,128)(2,1)S(1)}, u32[]{:S(2)}, u32[]{:S(2)}) collective-permute-start(bf16[64,1024]{1,0:T(8,128)(2,1)S(1)} %get-tuple-element.32.refs_1_), channel_id=1, source_target_pairs={{0,24},{8,0},{16,8},{24,16},{1,25},{9,1},{17,9},{25,17},{2,26},{10... | collective-permute-start | bytes 393224 | tf_op jit(solution)/shard_map/ppermute | solution.py:223
  96.6 1.3 %collective-permute-done.10.refs_3_ = bf16[64,1024]{1,0:T(8,128)(2,1)S(1)} collective-permute-done((bf16[64,1024]{1,0:T(8,128)(2,1)S(1)}, bf16[64,1024]{1,0:T(8,128)(2,1)S(1)}, u32[]{:S(2)}, u32[]{:S(2)}) %collective-permute-start.10) | collective-permute-done | bytes 131104 | tf_op jit(solution)/shard_map/ppermute | solution.py:223
  97.9 1.6 %mix0.1.refs_5_ = bf16[2,1024,1024]{2,1,0:T(8,128)(2,1)} custom-call(bf16[1024,256]{1,0:T(8,128)(2,1)S(1)} %get-tuple-element.33.refs_0_, bf16[64,1024]{1,0:T(8,128)(2,1)S(1)} %get-tuple-element.34.refs_1_, bf16[64,1024]{1,0:T(8,128)(2,1)S(1)} %collective-permute-done.9.refs_2_, bf16[64,1024]{1,0:T(8,128)(2,1)S(1)} %collective-permute-done.10.refs_3_, ...), custom_call_target="tpu_custom_call" | custom-call | flops 536870912 | bytes 2621440 | tf_op jit(solution)/shard_map/mix0/pallas_call | solution.py:324
  99.6 1.2 %collective-permute-done.7.refs_3_ = bf16[64,1024]{1,0:T(8,128)(2,1)S(1)} collective-permute-done((bf16[64,1024]{1,0:T(8,128)(2,1)S(1)}, bf16[64,1024]{1,0:T(8,128)(2,1)S(1)}, u32[]{:S(2)}, u32[]{:S(2)}) %collective-permute-start.7) | collective-permute-done | bytes 131104 | tf_op jit(solution)/shard_map/ppermute | solution.py:223
  100.8 1.6 %mix1.1 = bf16[2,1024,1024]{2,1,0:T(8,128)(2,1)} custom-call(bf16[1024,256]{1,0:T(8,128)(2,1)S(1)} %copy-done.5, bf16[64,1024]{1,0:T(8,128)(2,1)S(1)} %get-tuple-element.32.refs_1_, bf16[64,1024]{1,0:T(8,128)(2,1)S(1)} %collective-permute-done.6.refs_2_, bf16[64,1024]{1,0:T(8,128)(2,1)S(1)} %collective-permute-done.7.refs_3_, ...), custom_call_target="tpu_custom_call", output_to_operand_aliasing={{}: (5, {})} | custom-call | flops 536870912 | bytes 2621440 | tf_op jit(solution)/shard_map/mix1/pallas_call | solution.py:324
  (21 shorter events, 0.8 us)
Async XLA Ops:
  3.9 13.7 %copy-start.1 = (bf16[1024,256]{1,0:T(8,128)(2,1)S(1)}, bf16[1024,256]{1,0:T(8,128)(2,1)}, u32[]{:S(2)}) copy-start(bf16[1024,256]{1,0:T(8,128)(2,1)} %get-tuple-element.20.refs_1_.sp_ref) | copy-start | bytes 1572868
  3.9 11.2 %collective-permute-start.3 = (bf16[528,128]{1,0:T(8,128)(2,1)S(1)}, bf16[528,128]{1,0:T(8,128)(2,1)S(1)}, u32[]{:S(2)}, u32[]{:S(2)}) collective-permute-start(bf16[528,128]{1,0:T(8,128)(2,1)S(1)} %get-tuple-element.26), channel_id=1, source_target_pairs={{0,16},{8,24},{16,0},{24,8},{1,17},{9,25},{17,1},{25,9},{2,18},{10... | collective-permute-start | bytes 405512 | tf_op jit(solution)/shard_map/ppermute | solution.py:223
  7.2 12.9 %collective-permute-start.4 = (bf16[528,128]{1,0:T(8,128)(2,1)S(1)}, bf16[528,128]{1,0:T(8,128)(2,1)S(1)}, u32[]{:S(2)}, u32[]{:S(2)}) collective-permute-start(bf16[528,128]{1,0:T(8,128)(2,1)S(1)} %get-tuple-element.27), channel_id=1, source_target_pairs={{0,8},{8,16},{16,24},{24,0},{1,9},{9,17},{17,25},{25,1},{2,10},{10... | collective-permute-start | bytes 405512 | tf_op jit(solution)/shard_map/ppermute | solution.py:223
  7.9 12.2 %collective-permute-start.5 = (bf16[528,128]{1,0:T(8,128)(2,1)S(1)}, bf16[528,128]{1,0:T(8,128)(2,1)S(1)}, u32[]{:S(2)}, u32[]{:S(2)}) collective-permute-start(bf16[528,128]{1,0:T(8,128)(2,1)S(1)} %get-tuple-element.28), channel_id=1, source_target_pairs={{0,24},{8,0},{16,8},{24,16},{1,25},{9,1},{17,9},{25,17},{2,26},{10... | collective-permute-start | bytes 405512 | tf_op jit(solution)/shard_map/ppermute | solution.py:223
  14.2 7.6 %collective-permute-start = (bf16[528,128]{1,0:T(8,128)(2,1)S(1)}, bf16[528,128]{1,0:T(8,128)(2,1)S(1)}, u32[]{:S(2)}, u32[]{:S(2)}) collective-permute-start(bf16[528,128]{1,0:T(8,128)(2,1)S(1)} %get-tuple-element.22), channel_id=1, source_target_pairs={{0,16},{8,24},{16,0},{24,8},{1,17},{9,25},{17,1},{25,9},{2,18},{10... | collective-permute-start | bytes 405512 | tf_op jit(solution)/shard_map/ppermute | solution.py:223
  14.3 8.7 %collective-permute-start.1 = (bf16[528,128]{1,0:T(8,128)(2,1)S(1)}, bf16[528,128]{1,0:T(8,128)(2,1)S(1)}, u32[]{:S(2)}, u32[]{:S(2)}) collective-permute-start(bf16[528,128]{1,0:T(8,128)(2,1)S(1)} %get-tuple-element.23), channel_id=1, source_target_pairs={{0,8},{8,16},{16,24},{24,0},{1,9},{9,17},{17,25},{25,1},{2,10},{10... | collective-permute-start | bytes 405512 | tf_op jit(solution)/shard_map/ppermute | solution.py:223
  15.2 7.8 %collective-permute-start.2 = (bf16[528,128]{1,0:T(8,128)(2,1)S(1)}, bf16[528,128]{1,0:T(8,128)(2,1)S(1)}, u32[]{:S(2)}, u32[]{:S(2)}) collective-permute-start(bf16[528,128]{1,0:T(8,128)(2,1)S(1)} %get-tuple-element.24), channel_id=1, source_target_pairs={{0,24},{8,0},{16,8},{24,16},{1,25},{9,1},{17,9},{25,17},{2,26},{10... | collective-permute-start | bytes 405512 | tf_op jit(solution)/shard_map/ppermute | solution.py:223
  20.1 37.7 %copy-start.2 = (bf16[1024,1024]{1,0:T(8,128)(2,1)S(1)}, bf16[1024,1024]{1,0:T(8,128)(2,1)}, u32[]{:S(2)}) copy-start(bf16[1024,1024]{1,0:T(8,128)(2,1)} %up_ref.1) | copy-start | bytes 6291460
  24.1 20.7 %all-to-all-start = ((bf16[8,2,8,1152]{3,2,1,0:T(8,128)(2,1)}), bf16[8,2,8,1152]{3,2,1,0:T(8,128)(2,1)S(1)}, u32[]{:S(2)}, u32[]{:S(2)}) async-start(bf16[8,2,8,1152]{3,2,1,0:T(8,128)(2,1)} %both.1.after_ref), calls=%async_computation | async-start | bytes 589824 | tf_op jit(solution)/shard_map/all_to_all | solution.py:305
  32.5 2.2 %copy-start = (bf16[2,1024,1024]{2,1,0:T(8,128)(2,1)S(1)}, bf16[2,1024,1024]{2,1,0:T(8,128)(2,1)}, u32[]{:S(2)}) copy-start(bf16[2,1024,1024]{2,1,0:T(8,128)(2,1)} %tok_ref.3) | copy-start | bytes 12582916
  36.6 0.8 copy-start.4
  57.8 1.6 %copy-start.3 = (bf16[1024,1024]{1,0:T(8,128)(2,1)S(1)}, bf16[1024,1024]{1,0:T(8,128)(2,1)}, u32[]{:S(2)}) copy-start(bf16[1024,1024]{1,0:T(8,128)(2,1)} %down_ref.1) | copy-start | bytes 6291460
  60.3 40.4 %copy-start.5 = (bf16[1024,256]{1,0:T(8,128)(2,1)S(1)}, bf16[1024,256]{1,0:T(8,128)(2,1)}, u32[]{:S(2)}) copy-start(bf16[1024,256]{1,0:T(8,128)(2,1)} %copy-done.4) | copy-start | bytes 1572868
  87.7 7.9 %collective-permute-start.11 = (bf16[64,1024]{1,0:T(8,128)(2,1)S(1)}, bf16[64,1024]{1,0:T(8,128)(2,1)S(1)}, u32[]{:S(2)}, u32[]{:S(2)}) collective-permute-start(bf16[64,1024]{1,0:T(8,128)(2,1)S(1)} %get-tuple-element.34.refs_1_), channel_id=1, source_target_pairs={{0,16},{8,24},{16,0},{24,8},{1,17},{9,25},{17,1},{25,9},{2,18},{10... | collective-permute-start | bytes 393224 | tf_op jit(solution)/shard_map/ppermute | solution.py:223
  88.3 9.6 %collective-permute-start.10 = (bf16[64,1024]{1,0:T(8,128)(2,1)S(1)}, bf16[64,1024]{1,0:T(8,128)(2,1)S(1)}, u32[]{:S(2)}, u32[]{:S(2)}) collective-permute-start(bf16[64,1024]{1,0:T(8,128)(2,1)S(1)} %get-tuple-element.34.refs_1_), channel_id=1, source_target_pairs={{0,8},{8,16},{16,24},{24,0},{1,9},{9,17},{17,25},{25,1},{2,10},{10... | collective-permute-start | bytes 393224 | tf_op jit(solution)/shard_map/ppermute | solution.py:223
  89.6 8.3 %collective-permute-start.9 = (bf16[64,1024]{1,0:T(8,128)(2,1)S(1)}, bf16[64,1024]{1,0:T(8,128)(2,1)S(1)}, u32[]{:S(2)}, u32[]{:S(2)}) collective-permute-start(bf16[64,1024]{1,0:T(8,128)(2,1)S(1)} %get-tuple-element.34.refs_1_), channel_id=1, source_target_pairs={{0,24},{8,0},{16,8},{24,16},{1,25},{9,1},{17,9},{25,17},{2,26},{10... | collective-permute-start | bytes 393224 | tf_op jit(solution)/shard_map/ppermute | solution.py:223
  91.5 8.0 %collective-permute-start.8 = (bf16[64,1024]{1,0:T(8,128)(2,1)S(1)}, bf16[64,1024]{1,0:T(8,128)(2,1)S(1)}, u32[]{:S(2)}, u32[]{:S(2)}) collective-permute-start(bf16[64,1024]{1,0:T(8,128)(2,1)S(1)} %get-tuple-element.32.refs_1_), channel_id=1, source_target_pairs={{0,16},{8,24},{16,0},{24,8},{1,17},{9,25},{17,1},{25,9},{2,18},{10... | collective-permute-start | bytes 393224 | tf_op jit(solution)/shard_map/ppermute | solution.py:223
  93.3 7.5 %collective-permute-start.7 = (bf16[64,1024]{1,0:T(8,128)(2,1)S(1)}, bf16[64,1024]{1,0:T(8,128)(2,1)S(1)}, u32[]{:S(2)}, u32[]{:S(2)}) collective-permute-start(bf16[64,1024]{1,0:T(8,128)(2,1)S(1)} %get-tuple-element.32.refs_1_), channel_id=1, source_target_pairs={{0,8},{8,16},{16,24},{24,0},{1,9},{9,17},{17,25},{25,1},{2,10},{10... | collective-permute-start | bytes 393224 | tf_op jit(solution)/shard_map/ppermute | solution.py:223
  95.6 5.2 %collective-permute-start.6 = (bf16[64,1024]{1,0:T(8,128)(2,1)S(1)}, bf16[64,1024]{1,0:T(8,128)(2,1)S(1)}, u32[]{:S(2)}, u32[]{:S(2)}) collective-permute-start(bf16[64,1024]{1,0:T(8,128)(2,1)S(1)} %get-tuple-element.32.refs_1_), channel_id=1, source_target_pairs={{0,24},{8,0},{16,8},{24,16},{1,25},{9,1},{17,9},{25,17},{2,26},{10... | collective-permute-start | bytes 393224 | tf_op jit(solution)/shard_map/ppermute | solution.py:223

commit v7 on v5

--- a/solution.py
+++ b/solution.py
@@ -17,6 +17,7 @@
 STEPS = 4
 MIB = 1 << 20
 BIG = 52
+LATE = 44
 FAR_FIRST = (2, 1, 3)
 FAR_LAST = (0, 1, 3, 2)
 
@@ -30,7 +31,7 @@
 
 
 def params(mib=48):
-    return pltpu.CompilerParams(vmem_limit_bytes=mib * MIB)
+    return pltpu.CompilerParams(vmem_limit_bytes=int(mib * MIB))
 
 
 def name(f, *a):
@@ -61,24 +62,27 @@
     return jnp.where(lane == 0, hi, jnp.where(lane == 1, mid, jnp.where(lane == 2, low, 0.0)))
 
 
-def gather_kernel(clip, groups, ny, nz, tok_hbm, sp_ref, *refs):
+def gather_kernel(clip, groups, ny, nz, tok_in, sp_ref, *refs):
     out_refs, refs = refs[:ny], refs[ny:]
-    ordered_ref, tok_ref, logit_ref, sems = refs[-4:]
-    rows = tok_ref.shape[0] // STEPS
     copies = []
-    first = pltpu.make_async_copy(sp_ref, ordered_ref, sems.at[STEPS])
-    first.start()
-    for i in range(STEPS):
-        part = pl.ds(i * rows, rows)
-        copies.append(pltpu.make_async_copy(tok_hbm.at[clip, part], tok_ref.at[part], sems.at[i]))
-        copies[-1].start()
-    first.wait()
     if clip == 0:
-        refs[0][...] = device_order(ordered_ref[...], groups, ny, nz)
-        ordered_ref = refs[0]
+        ordered_ref, raw_ref, tok_ref, logit_ref, sems = refs
+        rows = tok_ref.shape[0] // STEPS
+        first = pltpu.make_async_copy(sp_ref, raw_ref, sems.at[STEPS])
+        first.start()
+        for i in range(STEPS):
+            part = pl.ds(i * rows, rows)
+            copies.append(pltpu.make_async_copy(tok_in.at[clip, part], tok_ref.at[part], sems.at[i]))
+            copies[-1].start()
+        first.wait()
+        ordered_ref[...] = device_order(raw_ref[...], groups, ny, nz)
+    else:
+        ordered_ref, tok_ref, logit_ref = sp_ref, tok_in.at[clip], refs[0]
+        rows = tok_ref.shape[0] // STEPS
     peak = None
     for i in range(STEPS):
-        copies[i].wait()
+        if copies:
+            copies[i].wait()
         part = slice(i * rows, (i + 1) * rows)
         logits = jnp.dot(tok_ref[part], ordered_ref[...], preferred_element_type=F32)
         logit_ref[part] = logits
@@ -235,7 +239,7 @@
         extra = [jax.ShapeDtypeStruct((width, slots), BF16)] if clip == 0 else []
         return pl.pallas_call(
             name(gather_kernel, clip, groups, ny, nz),
-            in_specs=[anywhere(), anywhere()],
+            in_specs=[anywhere(), anywhere()] if clip == 0 else [vmem(), vmem()],
             out_specs=[vmem()] * (ny + len(extra)),
             out_shape=[jax.ShapeDtypeStruct((nz * groups * (width // LANES) + STAT_ROWS, LANES), BF16)] * ny + extra,
             scratch_shapes=[
@@ -243,8 +247,10 @@
                 pltpu.VMEM((length, width), BF16),
                 pltpu.VMEM((length, slots), F32),
                 pltpu.SemaphoreType.DMA((STEPS + 1,)),
-            ],
-            compiler_params=params(BIG + 1),
+            ]
+            if clip == 0
+            else [pltpu.VMEM((length, slots), F32)],
+            compiler_params=params(BIG + 0.625 if clip == 0 else LATE),
             cost_estimate=pl.CostEstimate(
                 flops=4 * length * width * slots,
                 bytes_accessed=2 * length * width,
@@ -271,7 +277,7 @@
                 jax.ShapeDtypeStruct((length, slots), BF16),
                 jax.ShapeDtypeStruct((8, STAT), F32),
             ],
-            compiler_params=params(BIG),
+            compiler_params=params(LATE),
             cost_estimate=pl.CostEstimate(
                 flops=2 * length * width * slots,
                 bytes_accessed=2 * length * (width + slots),

time: 102 us -> 100 us (0.980)
  Pallas kernels: 18.2 us -> 13.6 us
  waiting for transfers between devices: 5.21 us -> 6.52 us
  starting transfers between devices: 16.7 us -> 17.8 us
    pallas_call x2, Pallas kernels: 5.08 us -> 2.46 us  [combine(): pl.pallas_call(combine_kernel, grid=(2,), in_specs=[pl.BlockSpec((1, half...]
    pallas_call x2, Pallas kernels: 7.66 us -> 5.67 us  [gather(): pl.pallas_call(name(gather_kernel, clip, groups, ny, nz), in_specs=[anywh...]
    ppermute x12, waiting for transfers between devices: 5.21 us -> 6.52 us  [shift(): return lax.ppermute(x, 'y', [(i, (i + k) % ny) for i in range(ny)])]
    ppermute x12, starting transfers between devices: 16.7 us -> 17.8 us  [shift(): return lax.ppermute(x, 'y', [(i, (i + k) % ny) for i in range(ny)])]
  transfers between devices with their start and end apart: 12 -> 12, of which waited for: 3 -> 5; matrix products, arithmetic and copies ran while one was open for 0% -> 0% of each run, Pallas kernels for 11% -> 6%
where the time goes in v7:
time: 100 us; the launch traced here: 99.3 us
  blocking collectives  61.1 us (61%)
  starting transfers between devices  17.8 us (18%)
  Pallas kernels  13.6 us (14%)
  waiting for transfers between devices  6.52 us (7%)
    all_to_all x1, blocking collectives, shards(): arrived = lax.all_to_all(halfway, around, 0, 0, tiled=True)  20.5 us
    ppermute x12, starting transfers between devices, shift(): return lax.ppermute(x, 'y', [(i, (i + k) % ny) for i in range(ny)])  17.8 us
    all_to_all x1, blocking collectives, shards(): ring = lax.all_to_all(slot_out, around, 0, 0, tiled=True)  15.4 us
    all_to_all x1, blocking collectives, shards(): own = lax.all_to_all(slot_in, sharers, 0, 0, tiled=True)  12.7 us
    all_to_all x1, blocking collectives, shards(): back = lax.all_to_all(partial, sharers, 0, 0, tiled=True)  12.5 us
    ppermute x12, waiting for transfers between devices, shift(): return lax.ppermute(x, 'y', [(i, (i + k) % ny) for i in range(ny)])  6.52 us
    pallas_call x2, Pallas kernels, gather(): pl.pallas_call(name(gather_kernel, clip, groups, ny, nz), in_specs=[anywh...  5.67 us
    pallas_call x2, Pallas kernels, shards(): pl.pallas_call(name(mix_kernel, clip, ny), in_specs=[vmem()] * (1 + ny) +...  3.29 us
  transfers between devices with their start and end apart: 12, of which 5 were waited for; matrix products, arithmetic and copies ran while one was open for 0% of the time, Pallas kernels for 6%

profile of v7, /device:TPU:2, one launch (start us, length us, event | category | flops | bytes accessed | tf_op | source)
XLA Modules:
  0.0 99.3 jit_solution(3241689071325420753)
XLA Ops:
  0.0 4.1 %gather0.1 = (bf16[528,128]{1,0:T(8,128)(2,1)S(1)}, bf16[528,128]{1,0:T(8,128)(2,1)S(1)}, bf16[528,128]{1,0:T(8,128)(2,1)S(1)}, bf16[528,128]{1,0:T(8,128)(2,1)S(1)}, bf16[1024,256]{1,0:T(8,128)(2,1)S(1)}) custom-call(bf16[2,1024,1024]{2,1,0:T(8,128)(2,1)} %tok_ref.3, bf16[1024,256]{1,0:T(8,128)(2,1)} %refs_1_.1), custom_call_target="tpu_custom_call" | custom-call | flops 1073741824 | bytes 2097152 | tf_op jit(solution)/shard_map/gather0/pallas_call | solution.py:240
  4.1 3.3 %collective-permute-start.3 = (bf16[528,128]{1,0:T(8,128)(2,1)S(1)}, bf16[528,128]{1,0:T(8,128)(2,1)S(1)}, u32[]{:S(2)}, u32[]{:S(2)}) collective-permute-start(bf16[528,128]{1,0:T(8,128)(2,1)S(1)} %get-tuple-element.28), channel_id=1, source_target_pairs={{0,16},{8,24},{16,0},{24,8},{1,17},{9,25},{17,1},{25,9},{2,18},{10... | collective-permute-start | bytes 405512 | tf_op jit(solution)/shard_map/ppermute | solution.py:226
  7.4 0.7 collective-permute-start.4
  8.0 2.6 %collective-permute-start.5 = (bf16[528,128]{1,0:T(8,128)(2,1)S(1)}, bf16[528,128]{1,0:T(8,128)(2,1)S(1)}, u32[]{:S(2)}, u32[]{:S(2)}) collective-permute-start(bf16[528,128]{1,0:T(8,128)(2,1)S(1)} %get-tuple-element.30), channel_id=1, source_target_pairs={{0,24},{8,0},{16,8},{24,16},{1,25},{9,1},{17,9},{25,17},{2,26},{10... | collective-permute-start | bytes 405512 | tf_op jit(solution)/shard_map/ppermute | solution.py:226
  10.6 1.6 %gather1.1 = (bf16[528,128]{1,0:T(8,128)(2,1)S(1)}, bf16[528,128]{1,0:T(8,128)(2,1)S(1)}, bf16[528,128]{1,0:T(8,128)(2,1)S(1)}, bf16[528,128]{1,0:T(8,128)(2,1)S(1)}) custom-call(bf16[2,1024,1024]{2,1,0:T(8,128)(2,1)S(1)} %copy-done, bf16[1024,256]{1,0:T(8,128)(2,1)S(1)} %get-tuple-element.20.refs_1_.sp_ref), custom_call_target="tpu_custom_call" | custom-call | flops 1073741824 | bytes 2097152 | tf_op jit(solution)/shard_map/gather1/pallas_call | solution.py:240
  12.2 0.1 collective-permute-start
  12.3 0.8 collective-permute-start.1
  13.2 2.5 %collective-permute-start.2 = (bf16[528,128]{1,0:T(8,128)(2,1)S(1)}, bf16[528,128]{1,0:T(8,128)(2,1)S(1)}, u32[]{:S(2)}, u32[]{:S(2)}) collective-permute-start(bf16[528,128]{1,0:T(8,128)(2,1)S(1)} %get-tuple-element.26), channel_id=1, source_target_pairs={{0,24},{8,0},{16,8},{24,16},{1,25},{9,1},{17,9},{25,17},{2,26},{10... | collective-permute-start | bytes 405512 | tf_op jit(solution)/shard_map/ppermute | solution.py:226
  15.6 1.2 %combine0.1 = (bf16[1024,256]{1,0:T(8,128)(2,1)S(1)}, f32[8,128]{1,0:T(8,128)S(1)}) custom-call(bf16[2,1024,1024]{2,1,0:T(8,128)(2,1)S(1)} %copy-done, bf16[1024,256]{1,0:T(8,128)(2,1)S(1)} %get-tuple-element.20.refs_1_.sp_ref, bf16[528,128]{1,0:T(8,128)(2,1)S(1)} %get-tuple-element.21.after_ref.refs_0_), custom_call_target="tpu_custom_call" | custom-call | flops 536870912 | bytes 2621440 | tf_op jit(solution)/shard_map/combine0/pallas_call | solution.py:264
  16.9 0.0 copy-start.2
  16.9 1.2 %combine1.1 = (bf16[1024,256]{1,0:T(8,128)(2,1)S(1)}, f32[8,128]{1,0:T(8,128)S(1)}) custom-call(bf16[2,1024,1024]{2,1,0:T(8,128)(2,1)S(1)} %copy-done, bf16[1024,256]{1,0:T(8,128)(2,1)S(1)} %get-tuple-element.20.refs_1_.sp_ref, f32[8,128]{1,0:T(8,128)S(1)} %get-tuple-element.22.after_ref), custom_call_target="tpu_custom_call" | custom-call | flops 536870912 | bytes 2621440 | tf_op jit(solution)/shard_map/combine1/pallas_call | solution.py:264
  18.2 0.4 halfway.1.refs_4_
  18.5 1.3 %collective-permute-done.refs_1_ = bf16[528,128]{1,0:T(8,128)(2,1)S(1)} collective-permute-done((bf16[528,128]{1,0:T(8,128)(2,1)S(1)}, bf16[528,128]{1,0:T(8,128)(2,1)S(1)}, u32[]{:S(2)}, u32[]{:S(2)}) %collective-permute-start) | collective-permute-done | bytes 135200 | tf_op jit(solution)/shard_map/ppermute | solution.py:226
  19.8 1.1 %collective-permute-done.1.refs_2_ = bf16[528,128]{1,0:T(8,128)(2,1)S(1)} collective-permute-done((bf16[528,128]{1,0:T(8,128)(2,1)S(1)}, bf16[528,128]{1,0:T(8,128)(2,1)S(1)}, u32[]{:S(2)}, u32[]{:S(2)}) %collective-permute-start.1) | collective-permute-done | bytes 135200 | tf_op jit(solution)/shard_map/ppermute | solution.py:226
  21.0 0.4 both.1
  21.4 20.5 %all_to_all.20.refs_0_ = bf16[8,2,8,1152]{3,2,1,0:T(8,128)(2,1)S(1)} all-to-all(bf16[8,2,8,1152]{3,2,1,0:T(8,128)(2,1)S(1)} %both.1), channel_id=1, replica_groups=mesh['group'=8,'y'=4,'zh'=2,'quarter'=4] {'zh','quarter'}, dimensions={0} | all-to-all | bytes 589824 | tf_op jit(solution)/shard_map/all_to_all | solution.py:311
  41.9 0.3 merge.1
  42.2 12.7 %all_to_all.21.x_ref = bf16[32,2,1024]{2,1,0:T(2,128)(2,1)S(1)} all-to-all(bf16[32,2,1024]{2,1,0:T(2,128)(2,1)S(1)} %merge.1), channel_id=1, replica_groups=mesh['group'=8,'y'=4,'zh'=2,'quarter'=4] {'group','quarter'}, dimensions={0} | all-to-all | bytes 262144 | tf_op jit(solution)/shard_map/all_to_all | solution.py:314
  54.9 1.0 expert.1
  55.9 12.5 %all_to_all.22.x_ref = bf16[32,2,1024]{2,1,0:T(2,128)(2,1)S(1)} all-to-all(bf16[32,2,1024]{2,1,0:T(2,128)(2,1)S(1)} %expert.1), channel_id=1, replica_groups=mesh['group'=8,'y'=4,'zh'=2,'quarter'=4] {'group','quarter'}, dimensions={0} | all-to-all | bytes 262144 | tf_op jit(solution)/shard_map/all_to_all | solution.py:316
  68.4 0.1 total.1
  68.5 15.4 %all_to_all.23.in_ref = bf16[8,2,8,1024]{3,2,1,0:T(8,128)(2,1)S(1)} all-to-all(bf16[8,2,8,1024]{3,2,1,0:T(8,128)(2,1)S(1)} %total.1), channel_id=1, replica_groups=mesh['group'=8,'y'=4,'zh'=2,'quarter'=4] {'zh','quarter'}, dimensions={0} | all-to-all | bytes 524288 | tf_op jit(solution)/shard_map/all_to_all | solution.py:320
  84.0 1.2 %collective-permute-start.11 = (bf16[64,1024]{1,0:T(8,128)(2,1)S(1)}, bf16[64,1024]{1,0:T(8,128)(2,1)S(1)}, u32[]{:S(2)}, u32[]{:S(2)}) collective-permute-start(bf16[64,1024]{1,0:T(8,128)(2,1)S(1)} %get-tuple-element.34.refs_1_), channel_id=1, source_target_pairs={{0,16},{8,24},{16,0},{24,8},{1,17},{9,25},{17,1},{25,9},{2,18},{10... | collective-permute-start | bytes 393224 | tf_op jit(solution)/shard_map/ppermute | solution.py:226
  85.2 1.9 %collective-permute-start.10 = (bf16[64,1024]{1,0:T(8,128)(2,1)S(1)}, bf16[64,1024]{1,0:T(8,128)(2,1)S(1)}, u32[]{:S(2)}, u32[]{:S(2)}) collective-permute-start(bf16[64,1024]{1,0:T(8,128)(2,1)S(1)} %get-tuple-element.34.refs_1_), channel_id=1, source_target_pairs={{0,8},{8,16},{16,24},{24,0},{1,9},{9,17},{17,25},{25,1},{2,10},{10... | collective-permute-start | bytes 393224 | tf_op jit(solution)/shard_map/ppermute | solution.py:226
  87.1 1.3 %collective-permute-start.9 = (bf16[64,1024]{1,0:T(8,128)(2,1)S(1)}, bf16[64,1024]{1,0:T(8,128)(2,1)S(1)}, u32[]{:S(2)}, u32[]{:S(2)}) collective-permute-start(bf16[64,1024]{1,0:T(8,128)(2,1)S(1)} %get-tuple-element.34.refs_1_), channel_id=1, source_target_pairs={{0,24},{8,0},{16,8},{24,16},{1,25},{9,1},{17,9},{25,17},{2,26},{10... | collective-permute-start | bytes 393224 | tf_op jit(solution)/shard_map/ppermute | solution.py:226
  88.4 1.2 %collective-permute-start.8 = (bf16[64,1024]{1,0:T(8,128)(2,1)S(1)}, bf16[64,1024]{1,0:T(8,128)(2,1)S(1)}, u32[]{:S(2)}, u32[]{:S(2)}) collective-permute-start(bf16[64,1024]{1,0:T(8,128)(2,1)S(1)} %get-tuple-element.32.refs_1_), channel_id=1, source_target_pairs={{0,16},{8,24},{16,0},{24,8},{1,17},{9,25},{17,1},{25,9},{2,18},{10... | collective-permute-start | bytes 393224 | tf_op jit(solution)/shard_map/ppermute | solution.py:226
  89.6 2.3 %collective-permute-done.11.refs_4_ = bf16[64,1024]{1,0:T(8,128)(2,1)S(1)} collective-permute-done((bf16[64,1024]{1,0:T(8,128)(2,1)S(1)}, bf16[64,1024]{1,0:T(8,128)(2,1)S(1)}, u32[]{:S(2)}, u32[]{:S(2)}) %collective-permute-start.11) | collective-permute-done | bytes 131104 | tf_op jit(solution)/shard_map/ppermute | solution.py:226
  91.9 2.2 %collective-permute-start.6 = (bf16[64,1024]{1,0:T(8,128)(2,1)S(1)}, bf16[64,1024]{1,0:T(8,128)(2,1)S(1)}, u32[]{:S(2)}, u32[]{:S(2)}) collective-permute-start(bf16[64,1024]{1,0:T(8,128)(2,1)S(1)} %get-tuple-element.32.refs_1_), channel_id=1, source_target_pairs={{0,24},{8,0},{16,8},{24,16},{1,25},{9,1},{17,9},{25,17},{2,26},{10... | collective-permute-start | bytes 393224 | tf_op jit(solution)/shard_map/ppermute | solution.py:226
  94.1 0.6 collective-permute-done.10.refs_3_
  94.8 1.6 %mix0.1.refs_5_ = bf16[2,1024,1024]{2,1,0:T(8,128)(2,1)} custom-call(bf16[1024,256]{1,0:T(8,128)(2,1)S(1)} %get-tuple-element.33.refs_0_, bf16[64,1024]{1,0:T(8,128)(2,1)S(1)} %get-tuple-element.34.refs_1_, bf16[64,1024]{1,0:T(8,128)(2,1)S(1)} %collective-permute-done.9.refs_2_, bf16[64,1024]{1,0:T(8,128)(2,1)S(1)} %collective-permute-done.10.refs_3_, ...), custom_call_target="tpu_custom_call" | custom-call | flops 536870912 | bytes 2621440 | tf_op jit(solution)/shard_map/mix0/pallas_call | solution.py:329
  96.4 1.1 %collective-permute-done.7.refs_3_ = bf16[64,1024]{1,0:T(8,128)(2,1)S(1)} collective-permute-done((bf16[64,1024]{1,0:T(8,128)(2,1)S(1)}, bf16[64,1024]{1,0:T(8,128)(2,1)S(1)}, u32[]{:S(2)}, u32[]{:S(2)}) %collective-permute-start.7) | collective-permute-done | bytes 131104 | tf_op jit(solution)/shard_map/ppermute | solution.py:226
  97.5 1.6 %mix1.1 = bf16[2,1024,1024]{2,1,0:T(8,128)(2,1)} custom-call(bf16[1024,256]{1,0:T(8,128)(2,1)S(1)} %get-tuple-element.23.refs_0_, bf16[64,1024]{1,0:T(8,128)(2,1)S(1)} %get-tuple-element.32.refs_1_, bf16[64,1024]{1,0:T(8,128)(2,1)S(1)} %collective-permute-done.6.refs_2_, ...), custom_call_target="tpu_custom_call", output_to_operand_aliasing={{}: (5, {})} | custom-call | flops 536870912 | bytes 2621440 | tf_op jit(solution)/shard_map/mix1/pallas_call | solution.py:329
  (14 shorter events, 0.1 us)
Async XLA Ops:
  0.0 10.6 %copy-start = (bf16[2,1024,1024]{2,1,0:T(8,128)(2,1)S(1)}, bf16[2,1024,1024]{2,1,0:T(8,128)(2,1)}, u32[]{:S(2)}) copy-start(bf16[2,1024,1024]{2,1,0:T(8,128)(2,1)} %tok_ref.3) | copy-start | bytes 12582916
  4.1 9.1 %collective-permute-start.3 = (bf16[528,128]{1,0:T(8,128)(2,1)S(1)}, bf16[528,128]{1,0:T(8,128)(2,1)S(1)}, u32[]{:S(2)}, u32[]{:S(2)}) collective-permute-start(bf16[528,128]{1,0:T(8,128)(2,1)S(1)} %get-tuple-element.28), channel_id=1, source_target_pairs={{0,16},{8,24},{16,0},{24,8},{1,17},{9,25},{17,1},{25,9},{2,18},{10... | collective-permute-start | bytes 405512 | tf_op jit(solution)/shard_map/ppermute | solution.py:226
  7.4 10.8 %collective-permute-start.4 = (bf16[528,128]{1,0:T(8,128)(2,1)S(1)}, bf16[528,128]{1,0:T(8,128)(2,1)S(1)}, u32[]{:S(2)}, u32[]{:S(2)}) collective-permute-start(bf16[528,128]{1,0:T(8,128)(2,1)S(1)} %get-tuple-element.29), channel_id=1, source_target_pairs={{0,8},{8,16},{16,24},{24,0},{1,9},{9,17},{17,25},{25,1},{2,10},{10... | collective-permute-start | bytes 405512 | tf_op jit(solution)/shard_map/ppermute | solution.py:226
  8.0 10.1 %collective-permute-start.5 = (bf16[528,128]{1,0:T(8,128)(2,1)S(1)}, bf16[528,128]{1,0:T(8,128)(2,1)S(1)}, u32[]{:S(2)}, u32[]{:S(2)}) collective-permute-start(bf16[528,128]{1,0:T(8,128)(2,1)S(1)} %get-tuple-element.30), channel_id=1, source_target_pairs={{0,24},{8,0},{16,8},{24,16},{1,25},{9,1},{17,9},{25,17},{2,26},{10... | collective-permute-start | bytes 405512 | tf_op jit(solution)/shard_map/ppermute | solution.py:226
  12.2 7.6 %collective-permute-start = (bf16[528,128]{1,0:T(8,128)(2,1)S(1)}, bf16[528,128]{1,0:T(8,128)(2,1)S(1)}, u32[]{:S(2)}, u32[]{:S(2)}) collective-permute-start(bf16[528,128]{1,0:T(8,128)(2,1)S(1)} %get-tuple-element.24), channel_id=1, source_target_pairs={{0,16},{8,24},{16,0},{24,8},{1,17},{9,25},{17,1},{25,9},{2,18},{10... | collective-permute-start | bytes 405512 | tf_op jit(solution)/shard_map/ppermute | solution.py:226
  12.3 8.7 %collective-permute-start.1 = (bf16[528,128]{1,0:T(8,128)(2,1)S(1)}, bf16[528,128]{1,0:T(8,128)(2,1)S(1)}, u32[]{:S(2)}, u32[]{:S(2)}) collective-permute-start(bf16[528,128]{1,0:T(8,128)(2,1)S(1)} %get-tuple-element.25), channel_id=1, source_target_pairs={{0,8},{8,16},{16,24},{24,0},{1,9},{9,17},{17,25},{25,1},{2,10},{10... | collective-permute-start | bytes 405512 | tf_op jit(solution)/shard_map/ppermute | solution.py:226
  13.2 7.8 %collective-permute-start.2 = (bf16[528,128]{1,0:T(8,128)(2,1)S(1)}, bf16[528,128]{1,0:T(8,128)(2,1)S(1)}, u32[]{:S(2)}, u32[]{:S(2)}) collective-permute-start(bf16[528,128]{1,0:T(8,128)(2,1)S(1)} %get-tuple-element.26), channel_id=1, source_target_pairs={{0,24},{8,0},{16,8},{24,16},{1,25},{9,1},{17,9},{25,17},{2,26},{10... | collective-permute-start | bytes 405512 | tf_op jit(solution)/shard_map/ppermute | solution.py:226
  16.9 38.0 %copy-start.1 = (bf16[1024,1024]{1,0:T(8,128)(2,1)S(1)}, bf16[1024,1024]{1,0:T(8,128)(2,1)}, u32[]{:S(2)}) copy-start(bf16[1024,1024]{1,0:T(8,128)(2,1)} %up_ref.1) | copy-start | bytes 6291460
  16.9 38.0 %copy-start.2 = (bf16[1024,1024]{1,0:T(8,128)(2,1)S(1)}, bf16[1024,1024]{1,0:T(8,128)(2,1)}, u32[]{:S(2)}) copy-start(bf16[1024,1024]{1,0:T(8,128)(2,1)} %down_ref.1) | copy-start | bytes 6291460
  84.0 8.0 %collective-permute-start.11 = (bf16[64,1024]{1,0:T(8,128)(2,1)S(1)}, bf16[64,1024]{1,0:T(8,128)(2,1)S(1)}, u32[]{:S(2)}, u32[]{:S(2)}) collective-permute-start(bf16[64,1024]{1,0:T(8,128)(2,1)S(1)} %get-tuple-element.34.refs_1_), channel_id=1, source_target_pairs={{0,16},{8,24},{16,0},{24,8},{1,17},{9,25},{17,1},{25,9},{2,18},{10... | collective-permute-start | bytes 393224 | tf_op jit(solution)/shard_map/ppermute | solution.py:226
  85.2 9.6 %collective-permute-start.10 = (bf16[64,1024]{1,0:T(8,128)(2,1)S(1)}, bf16[64,1024]{1,0:T(8,128)(2,1)S(1)}, u32[]{:S(2)}, u32[]{:S(2)}) collective-permute-start(bf16[64,1024]{1,0:T(8,128)(2,1)S(1)} %get-tuple-element.34.refs_1_), channel_id=1, source_target_pairs={{0,8},{8,16},{16,24},{24,0},{1,9},{9,17},{17,25},{25,1},{2,10},{10... | collective-permute-start | bytes 393224 | tf_op jit(solution)/shard_map/ppermute | solution.py:226
  87.1 7.7 %collective-permute-start.9 = (bf16[64,1024]{1,0:T(8,128)(2,1)S(1)}, bf16[64,1024]{1,0:T(8,128)(2,1)S(1)}, u32[]{:S(2)}, u32[]{:S(2)}) collective-permute-start(bf16[64,1024]{1,0:T(8,128)(2,1)S(1)} %get-tuple-element.34.refs_1_), channel_id=1, source_target_pairs={{0,24},{8,0},{16,8},{24,16},{1,25},{9,1},{17,9},{25,17},{2,26},{10... | collective-permute-start | bytes 393224 | tf_op jit(solution)/shard_map/ppermute | solution.py:226
  88.4 8.0 %collective-permute-start.8 = (bf16[64,1024]{1,0:T(8,128)(2,1)S(1)}, bf16[64,1024]{1,0:T(8,128)(2,1)S(1)}, u32[]{:S(2)}, u32[]{:S(2)}) collective-permute-start(bf16[64,1024]{1,0:T(8,128)(2,1)S(1)} %get-tuple-element.32.refs_1_), channel_id=1, source_target_pairs={{0,16},{8,24},{16,0},{24,8},{1,17},{9,25},{17,1},{25,9},{2,18},{10... | collective-permute-start | bytes 393224 | tf_op jit(solution)/shard_map/ppermute | solution.py:226
  89.6 7.9 %collective-permute-start.7 = (bf16[64,1024]{1,0:T(8,128)(2,1)S(1)}, bf16[64,1024]{1,0:T(8,128)(2,1)S(1)}, u32[]{:S(2)}, u32[]{:S(2)}) collective-permute-start(bf16[64,1024]{1,0:T(8,128)(2,1)S(1)} %get-tuple-element.32.refs_1_), channel_id=1, source_target_pairs={{0,8},{8,16},{16,24},{24,0},{1,9},{9,17},{17,25},{25,1},{2,10},{10... | collective-permute-start | bytes 393224 | tf_op jit(solution)/shard_map/ppermute | solution.py:226
  91.9 5.6 %collective-permute-start.6 = (bf16[64,1024]{1,0:T(8,128)(2,1)S(1)}, bf16[64,1024]{1,0:T(8,128)(2,1)S(1)}, u32[]{:S(2)}, u32[]{:S(2)}) collective-permute-start(bf16[64,1024]{1,0:T(8,128)(2,1)S(1)} %get-tuple-element.32.refs_1_), channel_id=1, source_target_pairs={{0,24},{8,0},{16,8},{24,16},{1,25},{9,1},{17,9},{25,17},{2,26},{10... | collective-permute-start | bytes 393224 | tf_op jit(solution)/shard_map/ppermute | solution.py:226

commit v8 on v7

--- a/solution.py
+++ b/solution.py
@@ -14,7 +14,8 @@
 LANES = 128
 STAT = LANES
 STAT_ROWS = 16
-STEPS = 4
+STEPS = 8
+PIECES = 4
 MIB = 1 << 20
 BIG = 52
 LATE = 44
@@ -41,13 +42,11 @@
     return body
 
 
-def device_order(slot_params, groups, ny, nz):
-    slots = slot_params.shape[1]
+def device_order(slots, groups, ny, nz):
     col = lax.broadcasted_iota(jnp.int32, (1, slots), 1)
     at_y = (col // (nz * groups) + lax.axis_index("y")) % ny
     slot = (col % groups * ny + at_y) * nz + col // groups % nz
-    perm = (lax.broadcasted_iota(jnp.int32, (slots, slots), 0) == slot).astype(F32).astype(BF16)
-    return jnp.dot(slot_params, perm, preferred_element_type=F32).astype(BF16)
+    return (lax.broadcasted_iota(jnp.int32, (slots, slots), 0) == slot).astype(F32).astype(BF16)
 
 
 def thirds(lse):
@@ -68,14 +67,21 @@
     if clip == 0:
         ordered_ref, raw_ref, tok_ref, logit_ref, sems = refs
         rows = tok_ref.shape[0] // STEPS
-        first = pltpu.make_async_copy(sp_ref, raw_ref, sems.at[STEPS])
-        first.start()
+        some = raw_ref.shape[0] // PIECES
+        first = []
+        for i in range(PIECES):
+            part = pl.ds(i * some, some)
+            first.append(pltpu.make_async_copy(sp_ref.at[part], raw_ref.at[part], sems.at[STEPS + i]))
+            first[-1].start()
         for i in range(STEPS):
             part = pl.ds(i * rows, rows)
             copies.append(pltpu.make_async_copy(tok_in.at[clip, part], tok_ref.at[part], sems.at[i]))
             copies[-1].start()
-        first.wait()
-        ordered_ref[...] = device_order(raw_ref[...], groups, ny, nz)
+        perm = device_order(raw_ref.shape[1], groups, ny, nz)
+        for i in range(PIECES):
+            first[i].wait()
+            part = slice(i * some, (i + 1) * some)
+            ordered_ref[part] = jnp.dot(raw_ref[part], perm, preferred_element_type=F32).astype(BF16)
     else:
         ordered_ref, tok_ref, logit_ref = sp_ref, tok_in.at[clip], refs[0]
         rows = tok_ref.shape[0] // STEPS
@@ -246,7 +252,7 @@
                 pltpu.VMEM((width, slots), BF16),
                 pltpu.VMEM((length, width), BF16),
                 pltpu.VMEM((length, slots), F32),
-                pltpu.SemaphoreType.DMA((STEPS + 1,)),
+                pltpu.SemaphoreType.DMA((STEPS + PIECES,)),
             ]
             if clip == 0
             else [pltpu.VMEM((length, slots), F32)],

time: 100 us -> 101 us (1.010)
    pallas_call x2, Pallas kernels: 5.67 us -> 6.75 us  [gather(): pl.pallas_call(name(gather_kernel, clip, groups, ny, nz), in_specs=[anywh...]
where the time goes in v8:
time: 101 us
  blocking collectives  61.2 us (61%)
  starting transfers between devices  17.9 us (18%)
  Pallas kernels  14.6 us (14%)
  waiting for transfers between devices  6.56 us (6%)
    all_to_all x1, blocking collectives, shards(): arrived = lax.all_to_all(halfway, around, 0, 0, tiled=True)  20.5 us
    ppermute x12, starting transfers between devices, shift(): return lax.ppermute(x, 'y', [(i, (i + k) % ny) for i in range(ny)])  17.9 us
    all_to_all x1, blocking collectives, shards(): ring = lax.all_to_all(slot_out, around, 0, 0, tiled=True)  15.4 us
    all_to_all x1, blocking collectives, shards(): own = lax.all_to_all(slot_in, sharers, 0, 0, tiled=True)  12.7 us
    all_to_all x1, blocking collectives, shards(): back = lax.all_to_all(partial, sharers, 0, 0, tiled=True)  12.5 us
    pallas_call x2, Pallas kernels, gather(): pl.pallas_call(name(gather_kernel, clip, groups, ny, nz), in_specs=[anywh...  6.75 us
    ppermute x12, waiting for transfers between devices, shift(): return lax.ppermute(x, 'y', [(i, (i + k) % ny) for i in range(ny)])  6.56 us
    pallas_call x2, Pallas kernels, shards(): pl.pallas_call(name(mix_kernel, clip, ny), in_specs=[vmem()] * (1 + ny) +...  3.23 us
  transfers between devices with their start and end apart: 12, of which 5 were waited for; matrix products, arithmetic and copies ran while one was open for 0% of the time, Pallas kernels for 6%

profile of v8, /device:TPU:2, one launch (start us, length us, event | category | flops | bytes accessed | tf_op | source)
XLA Modules:
  0.0 100.6 jit_solution(268016568542339463)
XLA Ops:
  0.0 5.1 %gather0.1 = (bf16[528,128]{1,0:T(8,128)(2,1)S(1)}, bf16[528,128]{1,0:T(8,128)(2,1)S(1)}, bf16[528,128]{1,0:T(8,128)(2,1)S(1)}, bf16[528,128]{1,0:T(8,128)(2,1)S(1)}, bf16[1024,256]{1,0:T(8,128)(2,1)S(1)}) custom-call(bf16[2,1024,1024]{2,1,0:T(8,128)(2,1)} %tok_ref.3, bf16[1024,256]{1,0:T(8,128)(2,1)} %refs_1_.1), custom_call_target="tpu_custom_call" | custom-call | flops 1073741824 | bytes 2097152 | tf_op jit(solution)/shard_map/gather0/pallas_call | solution.py:246
  5.1 3.3 %collective-permute-start.3 = (bf16[528,128]{1,0:T(8,128)(2,1)S(1)}, bf16[528,128]{1,0:T(8,128)(2,1)S(1)}, u32[]{:S(2)}, u32[]{:S(2)}) collective-permute-start(bf16[528,128]{1,0:T(8,128)(2,1)S(1)} %get-tuple-element.28), channel_id=1, source_target_pairs={{0,16},{8,24},{16,0},{24,8},{1,17},{9,25},{17,1},{25,9},{2,18},{10... | collective-permute-start | bytes 405512 | tf_op jit(solution)/shard_map/ppermute | solution.py:232
  8.4 0.7 collective-permute-start.4
  9.1 2.6 %collective-permute-start.5 = (bf16[528,128]{1,0:T(8,128)(2,1)S(1)}, bf16[528,128]{1,0:T(8,128)(2,1)S(1)}, u32[]{:S(2)}, u32[]{:S(2)}) collective-permute-start(bf16[528,128]{1,0:T(8,128)(2,1)S(1)} %get-tuple-element.30), channel_id=1, source_target_pairs={{0,24},{8,0},{16,8},{24,16},{1,25},{9,1},{17,9},{25,17},{2,26},{10... | collective-permute-start | bytes 405512 | tf_op jit(solution)/shard_map/ppermute | solution.py:232
  11.7 1.6 %gather1.1 = (bf16[528,128]{1,0:T(8,128)(2,1)S(1)}, bf16[528,128]{1,0:T(8,128)(2,1)S(1)}, bf16[528,128]{1,0:T(8,128)(2,1)S(1)}, bf16[528,128]{1,0:T(8,128)(2,1)S(1)}) custom-call(bf16[2,1024,1024]{2,1,0:T(8,128)(2,1)S(1)} %copy-done, bf16[1024,256]{1,0:T(8,128)(2,1)S(1)} %get-tuple-element.20.refs_1_.sp_ref), custom_call_target="tpu_custom_call" | custom-call | flops 1073741824 | bytes 2097152 | tf_op jit(solution)/shard_map/gather1/pallas_call | solution.py:246
  13.3 0.1 collective-permute-start
  13.4 0.9 collective-permute-start.1
  14.2 2.5 %collective-permute-start.2 = (bf16[528,128]{1,0:T(8,128)(2,1)S(1)}, bf16[528,128]{1,0:T(8,128)(2,1)S(1)}, u32[]{:S(2)}, u32[]{:S(2)}) collective-permute-start(bf16[528,128]{1,0:T(8,128)(2,1)S(1)} %get-tuple-element.26), channel_id=1, source_target_pairs={{0,24},{8,0},{16,8},{24,16},{1,25},{9,1},{17,9},{25,17},{2,26},{10... | collective-permute-start | bytes 405512 | tf_op jit(solution)/shard_map/ppermute | solution.py:232
  16.7 1.2 %combine0.1 = (bf16[1024,256]{1,0:T(8,128)(2,1)S(1)}, f32[8,128]{1,0:T(8,128)S(1)}) custom-call(bf16[2,1024,1024]{2,1,0:T(8,128)(2,1)S(1)} %copy-done, bf16[1024,256]{1,0:T(8,128)(2,1)S(1)} %get-tuple-element.20.refs_1_.sp_ref, bf16[528,128]{1,0:T(8,128)(2,1)S(1)} %get-tuple-element.21.after_ref.refs_0_), custom_call_target="tpu_custom_call" | custom-call | flops 536870912 | bytes 2621440 | tf_op jit(solution)/shard_map/combine0/pallas_call | solution.py:270
  17.9 0.0 copy-start.1
  18.0 1.2 %combine1.1 = (bf16[1024,256]{1,0:T(8,128)(2,1)S(1)}, f32[8,128]{1,0:T(8,128)S(1)}) custom-call(bf16[2,1024,1024]{2,1,0:T(8,128)(2,1)S(1)} %copy-done, bf16[1024,256]{1,0:T(8,128)(2,1)S(1)} %get-tuple-element.20.refs_1_.sp_ref, f32[8,128]{1,0:T(8,128)S(1)} %get-tuple-element.22.after_ref), custom_call_target="tpu_custom_call" | custom-call | flops 536870912 | bytes 2621440 | tf_op jit(solution)/shard_map/combine1/pallas_call | solution.py:270
  19.2 0.4 halfway.1.refs_4_
  19.6 1.3 %collective-permute-done.refs_1_ = bf16[528,128]{1,0:T(8,128)(2,1)S(1)} collective-permute-done((bf16[528,128]{1,0:T(8,128)(2,1)S(1)}, bf16[528,128]{1,0:T(8,128)(2,1)S(1)}, u32[]{:S(2)}, u32[]{:S(2)}) %collective-permute-start) | collective-permute-done | bytes 135200 | tf_op jit(solution)/shard_map/ppermute | solution.py:232
  20.9 1.1 %collective-permute-done.1.refs_2_ = bf16[528,128]{1,0:T(8,128)(2,1)S(1)} collective-permute-done((bf16[528,128]{1,0:T(8,128)(2,1)S(1)}, bf16[528,128]{1,0:T(8,128)(2,1)S(1)}, u32[]{:S(2)}, u32[]{:S(2)}) %collective-permute-start.1) | collective-permute-done | bytes 135200 | tf_op jit(solution)/shard_map/ppermute | solution.py:232
  22.1 0.4 both.1
  22.5 20.5 %all_to_all.20.refs_0_ = bf16[8,2,8,1152]{3,2,1,0:T(8,128)(2,1)S(1)} all-to-all(bf16[8,2,8,1152]{3,2,1,0:T(8,128)(2,1)S(1)} %both.1), channel_id=1, replica_groups=mesh['group'=8,'y'=4,'zh'=2,'quarter'=4] {'zh','quarter'}, dimensions={0} | all-to-all | bytes 589824 | tf_op jit(solution)/shard_map/all_to_all | solution.py:317
  43.0 0.3 merge.1
  43.3 12.7 %all_to_all.21.x_ref = bf16[32,2,1024]{2,1,0:T(2,128)(2,1)S(1)} all-to-all(bf16[32,2,1024]{2,1,0:T(2,128)(2,1)S(1)} %merge.1), channel_id=1, replica_groups=mesh['group'=8,'y'=4,'zh'=2,'quarter'=4] {'group','quarter'}, dimensions={0} | all-to-all | bytes 262144 | tf_op jit(solution)/shard_map/all_to_all | solution.py:320
  56.0 1.0 expert.1
  56.9 12.5 %all_to_all.22.x_ref = bf16[32,2,1024]{2,1,0:T(2,128)(2,1)S(1)} all-to-all(bf16[32,2,1024]{2,1,0:T(2,128)(2,1)S(1)} %expert.1), channel_id=1, replica_groups=mesh['group'=8,'y'=4,'zh'=2,'quarter'=4] {'group','quarter'}, dimensions={0} | all-to-all | bytes 262144 | tf_op jit(solution)/shard_map/all_to_all | solution.py:322
  69.5 0.1 total.1
  69.6 15.4 %all_to_all.23.in_ref = bf16[8,2,8,1024]{3,2,1,0:T(8,128)(2,1)S(1)} all-to-all(bf16[8,2,8,1024]{3,2,1,0:T(8,128)(2,1)S(1)} %total.1), channel_id=1, replica_groups=mesh['group'=8,'y'=4,'zh'=2,'quarter'=4] {'zh','quarter'}, dimensions={0} | all-to-all | bytes 524288 | tf_op jit(solution)/shard_map/all_to_all | solution.py:326
  85.0 1.4 %collective-permute-start.11 = (bf16[64,1024]{1,0:T(8,128)(2,1)S(1)}, bf16[64,1024]{1,0:T(8,128)(2,1)S(1)}, u32[]{:S(2)}, u32[]{:S(2)}) collective-permute-start(bf16[64,1024]{1,0:T(8,128)(2,1)S(1)} %get-tuple-element.34.refs_1_), channel_id=1, source_target_pairs={{0,16},{8,24},{16,0},{24,8},{1,17},{9,25},{17,1},{25,9},{2,18},{10... | collective-permute-start | bytes 393224 | tf_op jit(solution)/shard_map/ppermute | solution.py:232
  86.4 1.9 %collective-permute-start.10 = (bf16[64,1024]{1,0:T(8,128)(2,1)S(1)}, bf16[64,1024]{1,0:T(8,128)(2,1)S(1)}, u32[]{:S(2)}, u32[]{:S(2)}) collective-permute-start(bf16[64,1024]{1,0:T(8,128)(2,1)S(1)} %get-tuple-element.34.refs_1_), channel_id=1, source_target_pairs={{0,8},{8,16},{16,24},{24,0},{1,9},{9,17},{17,25},{25,1},{2,10},{10... | collective-permute-start | bytes 393224 | tf_op jit(solution)/shard_map/ppermute | solution.py:232
  88.3 1.4 %collective-permute-start.9 = (bf16[64,1024]{1,0:T(8,128)(2,1)S(1)}, bf16[64,1024]{1,0:T(8,128)(2,1)S(1)}, u32[]{:S(2)}, u32[]{:S(2)}) collective-permute-start(bf16[64,1024]{1,0:T(8,128)(2,1)S(1)} %get-tuple-element.34.refs_1_), channel_id=1, source_target_pairs={{0,24},{8,0},{16,8},{24,16},{1,25},{9,1},{17,9},{25,17},{2,26},{10... | collective-permute-start | bytes 393224 | tf_op jit(solution)/shard_map/ppermute | solution.py:232
  89.7 1.2 %collective-permute-start.8 = (bf16[64,1024]{1,0:T(8,128)(2,1)S(1)}, bf16[64,1024]{1,0:T(8,128)(2,1)S(1)}, u32[]{:S(2)}, u32[]{:S(2)}) collective-permute-start(bf16[64,1024]{1,0:T(8,128)(2,1)S(1)} %get-tuple-element.32.refs_1_), channel_id=1, source_target_pairs={{0,16},{8,24},{16,0},{24,8},{1,17},{9,25},{17,1},{25,9},{2,18},{10... | collective-permute-start | bytes 393224 | tf_op jit(solution)/shard_map/ppermute | solution.py:232
  90.9 2.3 %collective-permute-done.11.refs_4_ = bf16[64,1024]{1,0:T(8,128)(2,1)S(1)} collective-permute-done((bf16[64,1024]{1,0:T(8,128)(2,1)S(1)}, bf16[64,1024]{1,0:T(8,128)(2,1)S(1)}, u32[]{:S(2)}, u32[]{:S(2)}) %collective-permute-start.11) | collective-permute-done | bytes 131104 | tf_op jit(solution)/shard_map/ppermute | solution.py:232
  93.2 2.2 %collective-permute-start.6 = (bf16[64,1024]{1,0:T(8,128)(2,1)S(1)}, bf16[64,1024]{1,0:T(8,128)(2,1)S(1)}, u32[]{:S(2)}, u32[]{:S(2)}) collective-permute-start(bf16[64,1024]{1,0:T(8,128)(2,1)S(1)} %get-tuple-element.32.refs_1_), channel_id=1, source_target_pairs={{0,24},{8,0},{16,8},{24,16},{1,25},{9,1},{17,9},{25,17},{2,26},{10... | collective-permute-start | bytes 393224 | tf_op jit(solution)/shard_map/ppermute | solution.py:232
  95.4 0.6 collective-permute-done.10.refs_3_
  96.0 1.6 %mix0.1.refs_5_ = bf16[2,1024,1024]{2,1,0:T(8,128)(2,1)} custom-call(bf16[1024,256]{1,0:T(8,128)(2,1)S(1)} %get-tuple-element.33.refs_0_, bf16[64,1024]{1,0:T(8,128)(2,1)S(1)} %get-tuple-element.34.refs_1_, bf16[64,1024]{1,0:T(8,128)(2,1)S(1)} %collective-permute-done.9.refs_2_, bf16[64,1024]{1,0:T(8,128)(2,1)S(1)} %collective-permute-done.10.refs_3_, ...), custom_call_target="tpu_custom_call" | custom-call | flops 536870912 | bytes 2621440 | tf_op jit(solution)/shard_map/mix0/pallas_call | solution.py:335
  97.7 1.1 %collective-permute-done.7.refs_3_ = bf16[64,1024]{1,0:T(8,128)(2,1)S(1)} collective-permute-done((bf16[64,1024]{1,0:T(8,128)(2,1)S(1)}, bf16[64,1024]{1,0:T(8,128)(2,1)S(1)}, u32[]{:S(2)}, u32[]{:S(2)}) %collective-permute-start.7) | collective-permute-done | bytes 131104 | tf_op jit(solution)/shard_map/ppermute | solution.py:232
  98.8 1.6 %mix1.1 = bf16[2,1024,1024]{2,1,0:T(8,128)(2,1)} custom-call(bf16[1024,256]{1,0:T(8,128)(2,1)S(1)} %get-tuple-element.23.refs_0_, bf16[64,1024]{1,0:T(8,128)(2,1)S(1)} %get-tuple-element.32.refs_1_, bf16[64,1024]{1,0:T(8,128)(2,1)S(1)} %collective-permute-done.6.refs_2_, ...), custom_call_target="tpu_custom_call", output_to_operand_aliasing={{}: (5, {})} | custom-call | flops 536870912 | bytes 2621440 | tf_op jit(solution)/shard_map/mix1/pallas_call | solution.py:335
  (14 shorter events, 0.1 us)
Async XLA Ops:
  0.0 11.7 %copy-start = (bf16[2,1024,1024]{2,1,0:T(8,128)(2,1)S(1)}, bf16[2,1024,1024]{2,1,0:T(8,128)(2,1)}, u32[]{:S(2)}) copy-start(bf16[2,1024,1024]{2,1,0:T(8,128)(2,1)} %tok_ref.3) | copy-start | bytes 12582916
  5.1 9.1 %collective-permute-start.3 = (bf16[528,128]{1,0:T(8,128)(2,1)S(1)}, bf16[528,128]{1,0:T(8,128)(2,1)S(1)}, u32[]{:S(2)}, u32[]{:S(2)}) collective-permute-start(bf16[528,128]{1,0:T(8,128)(2,1)S(1)} %get-tuple-element.28), channel_id=1, source_target_pairs={{0,16},{8,24},{16,0},{24,8},{1,17},{9,25},{17,1},{25,9},{2,18},{10... | collective-permute-start | bytes 405512 | tf_op jit(solution)/shard_map/ppermute | solution.py:232
  8.4 10.8 %collective-permute-start.4 = (bf16[528,128]{1,0:T(8,128)(2,1)S(1)}, bf16[528,128]{1,0:T(8,128)(2,1)S(1)}, u32[]{:S(2)}, u32[]{:S(2)}) collective-permute-start(bf16[528,128]{1,0:T(8,128)(2,1)S(1)} %get-tuple-element.29), channel_id=1, source_target_pairs={{0,8},{8,16},{16,24},{24,0},{1,9},{9,17},{17,25},{25,1},{2,10},{10... | collective-permute-start | bytes 405512 | tf_op jit(solution)/shard_map/ppermute | solution.py:232
  9.1 10.1 %collective-permute-start.5 = (bf16[528,128]{1,0:T(8,128)(2,1)S(1)}, bf16[528,128]{1,0:T(8,128)(2,1)S(1)}, u32[]{:S(2)}, u32[]{:S(2)}) collective-permute-start(bf16[528,128]{1,0:T(8,128)(2,1)S(1)} %get-tuple-element.30), channel_id=1, source_target_pairs={{0,24},{8,0},{16,8},{24,16},{1,25},{9,1},{17,9},{25,17},{2,26},{10... | collective-permute-start | bytes 405512 | tf_op jit(solution)/shard_map/ppermute | solution.py:232
  13.3 7.6 %collective-permute-start = (bf16[528,128]{1,0:T(8,128)(2,1)S(1)}, bf16[528,128]{1,0:T(8,128)(2,1)S(1)}, u32[]{:S(2)}, u32[]{:S(2)}) collective-permute-start(bf16[528,128]{1,0:T(8,128)(2,1)S(1)} %get-tuple-element.24), channel_id=1, source_target_pairs={{0,16},{8,24},{16,0},{24,8},{1,17},{9,25},{17,1},{25,9},{2,18},{10... | collective-permute-start | bytes 405512 | tf_op jit(solution)/shard_map/ppermute | solution.py:232
  13.4 8.7 %collective-permute-start.1 = (bf16[528,128]{1,0:T(8,128)(2,1)S(1)}, bf16[528,128]{1,0:T(8,128)(2,1)S(1)}, u32[]{:S(2)}, u32[]{:S(2)}) collective-permute-start(bf16[528,128]{1,0:T(8,128)(2,1)S(1)} %get-tuple-element.25), channel_id=1, source_target_pairs={{0,8},{8,16},{16,24},{24,0},{1,9},{9,17},{17,25},{25,1},{2,10},{10... | collective-permute-start | bytes 405512 | tf_op jit(solution)/shard_map/ppermute | solution.py:232
  14.2 7.8 %collective-permute-start.2 = (bf16[528,128]{1,0:T(8,128)(2,1)S(1)}, bf16[528,128]{1,0:T(8,128)(2,1)S(1)}, u32[]{:S(2)}, u32[]{:S(2)}) collective-permute-start(bf16[528,128]{1,0:T(8,128)(2,1)S(1)} %get-tuple-element.26), channel_id=1, source_target_pairs={{0,24},{8,0},{16,8},{24,16},{1,25},{9,1},{17,9},{25,17},{2,26},{10... | collective-permute-start | bytes 405512 | tf_op jit(solution)/shard_map/ppermute | solution.py:232
  17.9 38.0 %copy-start.1 = (bf16[1024,1024]{1,0:T(8,128)(2,1)S(1)}, bf16[1024,1024]{1,0:T(8,128)(2,1)}, u32[]{:S(2)}) copy-start(bf16[1024,1024]{1,0:T(8,128)(2,1)} %up_ref.1) | copy-start | bytes 6291460
  18.0 38.0 %copy-start.2 = (bf16[1024,1024]{1,0:T(8,128)(2,1)S(1)}, bf16[1024,1024]{1,0:T(8,128)(2,1)}, u32[]{:S(2)}) copy-start(bf16[1024,1024]{1,0:T(8,128)(2,1)} %down_ref.1) | copy-start | bytes 6291460
  85.0 8.2 %collective-permute-start.11 = (bf16[64,1024]{1,0:T(8,128)(2,1)S(1)}, bf16[64,1024]{1,0:T(8,128)(2,1)S(1)}, u32[]{:S(2)}, u32[]{:S(2)}) collective-permute-start(bf16[64,1024]{1,0:T(8,128)(2,1)S(1)} %get-tuple-element.34.refs_1_), channel_id=1, source_target_pairs={{0,16},{8,24},{16,0},{24,8},{1,17},{9,25},{17,1},{25,9},{2,18},{10... | collective-permute-start | bytes 393224 | tf_op jit(solution)/shard_map/ppermute | solution.py:232
  86.4 9.6 %collective-permute-start.10 = (bf16[64,1024]{1,0:T(8,128)(2,1)S(1)}, bf16[64,1024]{1,0:T(8,128)(2,1)S(1)}, u32[]{:S(2)}, u32[]{:S(2)}) collective-permute-start(bf16[64,1024]{1,0:T(8,128)(2,1)S(1)} %get-tuple-element.34.refs_1_), channel_id=1, source_target_pairs={{0,8},{8,16},{16,24},{24,0},{1,9},{9,17},{17,25},{25,1},{2,10},{10... | collective-permute-start | bytes 393224 | tf_op jit(solution)/shard_map/ppermute | solution.py:232
  88.3 7.7 %collective-permute-start.9 = (bf16[64,1024]{1,0:T(8,128)(2,1)S(1)}, bf16[64,1024]{1,0:T(8,128)(2,1)S(1)}, u32[]{:S(2)}, u32[]{:S(2)}) collective-permute-start(bf16[64,1024]{1,0:T(8,128)(2,1)S(1)} %get-tuple-element.34.refs_1_), channel_id=1, source_target_pairs={{0,24},{8,0},{16,8},{24,16},{1,25},{9,1},{17,9},{25,17},{2,26},{10... | collective-permute-start | bytes 393224 | tf_op jit(solution)/shard_map/ppermute | solution.py:232
  89.7 8.0 %collective-permute-start.8 = (bf16[64,1024]{1,0:T(8,128)(2,1)S(1)}, bf16[64,1024]{1,0:T(8,128)(2,1)S(1)}, u32[]{:S(2)}, u32[]{:S(2)}) collective-permute-start(bf16[64,1024]{1,0:T(8,128)(2,1)S(1)} %get-tuple-element.32.refs_1_), channel_id=1, source_target_pairs={{0,16},{8,24},{16,0},{24,8},{1,17},{9,25},{17,1},{25,9},{2,18},{10... | collective-permute-start | bytes 393224 | tf_op jit(solution)/shard_map/ppermute | solution.py:232
  90.9 7.9 %collective-permute-start.7 = (bf16[64,1024]{1,0:T(8,128)(2,1)S(1)}, bf16[64,1024]{1,0:T(8,128)(2,1)S(1)}, u32[]{:S(2)}, u32[]{:S(2)}) collective-permute-start(bf16[64,1024]{1,0:T(8,128)(2,1)S(1)} %get-tuple-element.32.refs_1_), channel_id=1, source_target_pairs={{0,8},{8,16},{16,24},{24,0},{1,9},{9,17},{17,25},{25,1},{2,10},{10... | collective-permute-start | bytes 393224 | tf_op jit(solution)/shard_map/ppermute | solution.py:232
  93.2 5.6 %collective-permute-start.6 = (bf16[64,1024]{1,0:T(8,128)(2,1)S(1)}, bf16[64,1024]{1,0:T(8,128)(2,1)S(1)}, u32[]{:S(2)}, u32[]{:S(2)}) collective-permute-start(bf16[64,1024]{1,0:T(8,128)(2,1)S(1)} %get-tuple-element.32.refs_1_), channel_id=1, source_target_pairs={{0,24},{8,0},{16,8},{24,16},{1,25},{9,1},{17,9},{25,17},{2,26},{10... | collective-permute-start | bytes 393224 | tf_op jit(solution)/shard_map/ppermute | solution.py:232

commit v9 on v7

--- a/solution.py
+++ b/solution.py
@@ -14,6 +14,7 @@
 LANES = 128
 STAT = LANES
 STAT_ROWS = 16
+FETCHES = 2
 STEPS = 4
 MIB = 1 << 20
 BIG = 52
@@ -41,13 +42,11 @@
     return body
 
 
-def device_order(slot_params, groups, ny, nz):
-    slots = slot_params.shape[1]
+def device_order(slots, groups, ny, nz):
     col = lax.broadcasted_iota(jnp.int32, (1, slots), 1)
     at_y = (col // (nz * groups) + lax.axis_index("y")) % ny
     slot = (col % groups * ny + at_y) * nz + col // groups % nz
-    perm = (lax.broadcasted_iota(jnp.int32, (slots, slots), 0) == slot).astype(F32).astype(BF16)
-    return jnp.dot(slot_params, perm, preferred_element_type=F32).astype(BF16)
+    return (lax.broadcasted_iota(jnp.int32, (slots, slots), 0) == slot).astype(F32).astype(BF16)
 
 
 def thirds(lse):
@@ -65,22 +64,24 @@
 def gather_kernel(clip, groups, ny, nz, tok_in, sp_ref, *refs):
     out_refs, refs = refs[:ny], refs[ny:]
     copies = []
+    parts = FETCHES if clip == 0 else STEPS
     if clip == 0:
         ordered_ref, raw_ref, tok_ref, logit_ref, sems = refs
-        rows = tok_ref.shape[0] // STEPS
-        first = pltpu.make_async_copy(sp_ref, raw_ref, sems.at[STEPS])
+        rows = tok_ref.shape[0] // parts
+        first = pltpu.make_async_copy(sp_ref, raw_ref, sems.at[parts])
         first.start()
-        for i in range(STEPS):
+        for i in range(parts):
             part = pl.ds(i * rows, rows)
             copies.append(pltpu.make_async_copy(tok_in.at[clip, part], tok_ref.at[part], sems.at[i]))
             copies[-1].start()
+        perm = device_order(raw_ref.shape[1], groups, ny, nz)
         first.wait()
-        ordered_ref[...] = device_order(raw_ref[...], groups, ny, nz)
+        ordered_ref[...] = jnp.dot(raw_ref[...], perm, preferred_element_type=F32).astype(BF16)
     else:
         ordered_ref, tok_ref, logit_ref = sp_ref, tok_in.at[clip], refs[0]
-        rows = tok_ref.shape[0] // STEPS
+        rows = tok_ref.shape[0] // parts
     peak = None
-    for i in range(STEPS):
+    for i in range(parts):
         if copies:
             copies[i].wait()
         part = slice(i * rows, (i + 1) * rows)
@@ -246,7 +247,7 @@
                 pltpu.VMEM((width, slots), BF16),
                 pltpu.VMEM((length, width), BF16),
                 pltpu.VMEM((length, slots), F32),
-                pltpu.SemaphoreType.DMA((STEPS + 1,)),
+                pltpu.SemaphoreType.DMA((FETCHES + 1,)),
             ]
             if clip == 0
             else [pltpu.VMEM((length, slots), F32)],

time: 100 us -> 100 us (level)
  no operation moved by 1% of the time
where the time goes in v9:
time: 100 us; the launch traced here: 99.1 us
  blocking collectives  61.1 us (61%)
  starting transfers between devices  17.8 us (18%)
  Pallas kernels  13.3 us (13%)
  waiting for transfers between devices  6.5 us (6%)
    all_to_all x1, blocking collectives, shards(): arrived = lax.all_to_all(halfway, around, 0, 0, tiled=True)  20.5 us
    ppermute x12, starting transfers between devices, shift(): return lax.ppermute(x, 'y', [(i, (i + k) % ny) for i in range(ny)])  17.8 us
    all_to_all x1, blocking collectives, shards(): ring = lax.all_to_all(slot_out, around, 0, 0, tiled=True)  15.4 us
    all_to_all x1, blocking collectives, shards(): own = lax.all_to_all(slot_in, sharers, 0, 0, tiled=True)  12.7 us
    all_to_all x1, blocking collectives, shards(): back = lax.all_to_all(partial, sharers, 0, 0, tiled=True)  12.5 us
    ppermute x12, waiting for transfers between devices, shift(): return lax.ppermute(x, 'y', [(i, (i + k) % ny) for i in range(ny)])  6.5 us
    pallas_call x2, Pallas kernels, gather(): pl.pallas_call(name(gather_kernel, clip, groups, ny, nz), in_specs=[anywh...  5.42 us
    pallas_call x2, Pallas kernels, shards(): pl.pallas_call(name(mix_kernel, clip, ny), in_specs=[vmem()] * (1 + ny) +...  3.29 us
  transfers between devices with their start and end apart: 12, of which 5 were waited for; matrix products, arithmetic and copies ran while one was open for 0% of the time, Pallas kernels for 6%

profile of v9, /device:TPU:2, one launch (start us, length us, event | category | flops | bytes accessed | tf_op | source)
XLA Modules:
  0.0 99.1 jit_solution(13645046912904102166)
XLA Ops:
  0.0 3.8 %gather0.1 = (bf16[528,128]{1,0:T(8,128)(2,1)S(1)}, bf16[528,128]{1,0:T(8,128)(2,1)S(1)}, bf16[528,128]{1,0:T(8,128)(2,1)S(1)}, bf16[528,128]{1,0:T(8,128)(2,1)S(1)}, bf16[1024,256]{1,0:T(8,128)(2,1)S(1)}) custom-call(bf16[2,1024,1024]{2,1,0:T(8,128)(2,1)} %tok_ref.3, bf16[1024,256]{1,0:T(8,128)(2,1)} %refs_1_.1), custom_call_target="tpu_custom_call" | custom-call | flops 1073741824 | bytes 2097152 | tf_op jit(solution)/shard_map/gather0/pallas_call | solution.py:241
  3.8 3.3 %collective-permute-start.3 = (bf16[528,128]{1,0:T(8,128)(2,1)S(1)}, bf16[528,128]{1,0:T(8,128)(2,1)S(1)}, u32[]{:S(2)}, u32[]{:S(2)}) collective-permute-start(bf16[528,128]{1,0:T(8,128)(2,1)S(1)} %get-tuple-element.28), channel_id=1, source_target_pairs={{0,16},{8,24},{16,0},{24,8},{1,17},{9,25},{17,1},{25,9},{2,18},{10... | collective-permute-start | bytes 405512 | tf_op jit(solution)/shard_map/ppermute | solution.py:227
  7.1 0.7 collective-permute-start.4
  7.8 2.6 %collective-permute-start.5 = (bf16[528,128]{1,0:T(8,128)(2,1)S(1)}, bf16[528,128]{1,0:T(8,128)(2,1)S(1)}, u32[]{:S(2)}, u32[]{:S(2)}) collective-permute-start(bf16[528,128]{1,0:T(8,128)(2,1)S(1)} %get-tuple-element.30), channel_id=1, source_target_pairs={{0,24},{8,0},{16,8},{24,16},{1,25},{9,1},{17,9},{25,17},{2,26},{10... | collective-permute-start | bytes 405512 | tf_op jit(solution)/shard_map/ppermute | solution.py:227
  10.3 1.6 %gather1.1 = (bf16[528,128]{1,0:T(8,128)(2,1)S(1)}, bf16[528,128]{1,0:T(8,128)(2,1)S(1)}, bf16[528,128]{1,0:T(8,128)(2,1)S(1)}, bf16[528,128]{1,0:T(8,128)(2,1)S(1)}) custom-call(bf16[2,1024,1024]{2,1,0:T(8,128)(2,1)S(1)} %copy-done, bf16[1024,256]{1,0:T(8,128)(2,1)S(1)} %get-tuple-element.20.refs_1_.sp_ref), custom_call_target="tpu_custom_call" | custom-call | flops 1073741824 | bytes 2097152 | tf_op jit(solution)/shard_map/gather1/pallas_call | solution.py:241
  12.0 0.1 collective-permute-start
  12.1 0.8 collective-permute-start.1
  12.9 2.5 %collective-permute-start.2 = (bf16[528,128]{1,0:T(8,128)(2,1)S(1)}, bf16[528,128]{1,0:T(8,128)(2,1)S(1)}, u32[]{:S(2)}, u32[]{:S(2)}) collective-permute-start(bf16[528,128]{1,0:T(8,128)(2,1)S(1)} %get-tuple-element.26), channel_id=1, source_target_pairs={{0,24},{8,0},{16,8},{24,16},{1,25},{9,1},{17,9},{25,17},{2,26},{10... | collective-permute-start | bytes 405512 | tf_op jit(solution)/shard_map/ppermute | solution.py:227
  15.4 1.2 %combine0.1 = (bf16[1024,256]{1,0:T(8,128)(2,1)S(1)}, f32[8,128]{1,0:T(8,128)S(1)}) custom-call(bf16[2,1024,1024]{2,1,0:T(8,128)(2,1)S(1)} %copy-done, bf16[1024,256]{1,0:T(8,128)(2,1)S(1)} %get-tuple-element.20.refs_1_.sp_ref, bf16[528,128]{1,0:T(8,128)(2,1)S(1)} %get-tuple-element.21.after_ref.refs_0_), custom_call_target="tpu_custom_call" | custom-call | flops 536870912 | bytes 2621440 | tf_op jit(solution)/shard_map/combine0/pallas_call | solution.py:265
  16.6 0.0 copy-start.1
  16.6 1.2 %combine1.1 = (bf16[1024,256]{1,0:T(8,128)(2,1)S(1)}, f32[8,128]{1,0:T(8,128)S(1)}) custom-call(bf16[2,1024,1024]{2,1,0:T(8,128)(2,1)S(1)} %copy-done, bf16[1024,256]{1,0:T(8,128)(2,1)S(1)} %get-tuple-element.20.refs_1_.sp_ref, f32[8,128]{1,0:T(8,128)S(1)} %get-tuple-element.22.after_ref), custom_call_target="tpu_custom_call" | custom-call | flops 536870912 | bytes 2621440 | tf_op jit(solution)/shard_map/combine1/pallas_call | solution.py:265
  17.9 0.4 halfway.1.refs_4_
  18.3 1.3 %collective-permute-done.refs_1_ = bf16[528,128]{1,0:T(8,128)(2,1)S(1)} collective-permute-done((bf16[528,128]{1,0:T(8,128)(2,1)S(1)}, bf16[528,128]{1,0:T(8,128)(2,1)S(1)}, u32[]{:S(2)}, u32[]{:S(2)}) %collective-permute-start) | collective-permute-done | bytes 135200 | tf_op jit(solution)/shard_map/ppermute | solution.py:227
  19.6 1.1 %collective-permute-done.1.refs_2_ = bf16[528,128]{1,0:T(8,128)(2,1)S(1)} collective-permute-done((bf16[528,128]{1,0:T(8,128)(2,1)S(1)}, bf16[528,128]{1,0:T(8,128)(2,1)S(1)}, u32[]{:S(2)}, u32[]{:S(2)}) %collective-permute-start.1) | collective-permute-done | bytes 135200 | tf_op jit(solution)/shard_map/ppermute | solution.py:227
  20.7 0.4 both.1
  21.1 20.5 %all_to_all.20.refs_0_ = bf16[8,2,8,1152]{3,2,1,0:T(8,128)(2,1)S(1)} all-to-all(bf16[8,2,8,1152]{3,2,1,0:T(8,128)(2,1)S(1)} %both.1), channel_id=1, replica_groups=mesh['group'=8,'y'=4,'zh'=2,'quarter'=4] {'zh','quarter'}, dimensions={0} | all-to-all | bytes 589824 | tf_op jit(solution)/shard_map/all_to_all | solution.py:312
  41.6 0.3 merge.1
  41.9 12.7 %all_to_all.21.x_ref = bf16[32,2,1024]{2,1,0:T(2,128)(2,1)S(1)} all-to-all(bf16[32,2,1024]{2,1,0:T(2,128)(2,1)S(1)} %merge.1), channel_id=1, replica_groups=mesh['group'=8,'y'=4,'zh'=2,'quarter'=4] {'group','quarter'}, dimensions={0} | all-to-all | bytes 262144 | tf_op jit(solution)/shard_map/all_to_all | solution.py:315
  54.6 1.0 expert.1
  55.6 12.5 %all_to_all.22.x_ref = bf16[32,2,1024]{2,1,0:T(2,128)(2,1)S(1)} all-to-all(bf16[32,2,1024]{2,1,0:T(2,128)(2,1)S(1)} %expert.1), channel_id=1, replica_groups=mesh['group'=8,'y'=4,'zh'=2,'quarter'=4] {'group','quarter'}, dimensions={0} | all-to-all | bytes 262144 | tf_op jit(solution)/shard_map/all_to_all | solution.py:317
  68.1 0.1 total.1
  68.3 15.4 %all_to_all.23.in_ref = bf16[8,2,8,1024]{3,2,1,0:T(8,128)(2,1)S(1)} all-to-all(bf16[8,2,8,1024]{3,2,1,0:T(8,128)(2,1)S(1)} %total.1), channel_id=1, replica_groups=mesh['group'=8,'y'=4,'zh'=2,'quarter'=4] {'zh','quarter'}, dimensions={0} | all-to-all | bytes 524288 | tf_op jit(solution)/shard_map/all_to_all | solution.py:321
  83.7 1.2 %collective-permute-start.11 = (bf16[64,1024]{1,0:T(8,128)(2,1)S(1)}, bf16[64,1024]{1,0:T(8,128)(2,1)S(1)}, u32[]{:S(2)}, u32[]{:S(2)}) collective-permute-start(bf16[64,1024]{1,0:T(8,128)(2,1)S(1)} %get-tuple-element.34.refs_1_), channel_id=1, source_target_pairs={{0,16},{8,24},{16,0},{24,8},{1,17},{9,25},{17,1},{25,9},{2,18},{10... | collective-permute-start | bytes 393224 | tf_op jit(solution)/shard_map/ppermute | solution.py:227
  84.9 1.9 %collective-permute-start.10 = (bf16[64,1024]{1,0:T(8,128)(2,1)S(1)}, bf16[64,1024]{1,0:T(8,128)(2,1)S(1)}, u32[]{:S(2)}, u32[]{:S(2)}) collective-permute-start(bf16[64,1024]{1,0:T(8,128)(2,1)S(1)} %get-tuple-element.34.refs_1_), channel_id=1, source_target_pairs={{0,8},{8,16},{16,24},{24,0},{1,9},{9,17},{17,25},{25,1},{2,10},{10... | collective-permute-start | bytes 393224 | tf_op jit(solution)/shard_map/ppermute | solution.py:227
  86.8 1.3 %collective-permute-start.9 = (bf16[64,1024]{1,0:T(8,128)(2,1)S(1)}, bf16[64,1024]{1,0:T(8,128)(2,1)S(1)}, u32[]{:S(2)}, u32[]{:S(2)}) collective-permute-start(bf16[64,1024]{1,0:T(8,128)(2,1)S(1)} %get-tuple-element.34.refs_1_), channel_id=1, source_target_pairs={{0,24},{8,0},{16,8},{24,16},{1,25},{9,1},{17,9},{25,17},{2,26},{10... | collective-permute-start | bytes 393224 | tf_op jit(solution)/shard_map/ppermute | solution.py:227
  88.2 1.2 %collective-permute-start.8 = (bf16[64,1024]{1,0:T(8,128)(2,1)S(1)}, bf16[64,1024]{1,0:T(8,128)(2,1)S(1)}, u32[]{:S(2)}, u32[]{:S(2)}) collective-permute-start(bf16[64,1024]{1,0:T(8,128)(2,1)S(1)} %get-tuple-element.32.refs_1_), channel_id=1, source_target_pairs={{0,16},{8,24},{16,0},{24,8},{1,17},{9,25},{17,1},{25,9},{2,18},{10... | collective-permute-start | bytes 393224 | tf_op jit(solution)/shard_map/ppermute | solution.py:227
  89.3 2.3 %collective-permute-done.11.refs_4_ = bf16[64,1024]{1,0:T(8,128)(2,1)S(1)} collective-permute-done((bf16[64,1024]{1,0:T(8,128)(2,1)S(1)}, bf16[64,1024]{1,0:T(8,128)(2,1)S(1)}, u32[]{:S(2)}, u32[]{:S(2)}) %collective-permute-start.11) | collective-permute-done | bytes 131104 | tf_op jit(solution)/shard_map/ppermute | solution.py:227
  91.7 2.2 %collective-permute-start.6 = (bf16[64,1024]{1,0:T(8,128)(2,1)S(1)}, bf16[64,1024]{1,0:T(8,128)(2,1)S(1)}, u32[]{:S(2)}, u32[]{:S(2)}) collective-permute-start(bf16[64,1024]{1,0:T(8,128)(2,1)S(1)} %get-tuple-element.32.refs_1_), channel_id=1, source_target_pairs={{0,24},{8,0},{16,8},{24,16},{1,25},{9,1},{17,9},{25,17},{2,26},{10... | collective-permute-start | bytes 393224 | tf_op jit(solution)/shard_map/ppermute | solution.py:227
  93.9 0.6 collective-permute-done.10.refs_3_
  94.5 1.6 %mix0.1.refs_5_ = bf16[2,1024,1024]{2,1,0:T(8,128)(2,1)} custom-call(bf16[1024,256]{1,0:T(8,128)(2,1)S(1)} %get-tuple-element.33.refs_0_, bf16[64,1024]{1,0:T(8,128)(2,1)S(1)} %get-tuple-element.34.refs_1_, bf16[64,1024]{1,0:T(8,128)(2,1)S(1)} %collective-permute-done.9.refs_2_, bf16[64,1024]{1,0:T(8,128)(2,1)S(1)} %collective-permute-done.10.refs_3_, ...), custom_call_target="tpu_custom_call" | custom-call | flops 536870912 | bytes 2621440 | tf_op jit(solution)/shard_map/mix0/pallas_call | solution.py:330
  96.2 1.1 %collective-permute-done.7.refs_3_ = bf16[64,1024]{1,0:T(8,128)(2,1)S(1)} collective-permute-done((bf16[64,1024]{1,0:T(8,128)(2,1)S(1)}, bf16[64,1024]{1,0:T(8,128)(2,1)S(1)}, u32[]{:S(2)}, u32[]{:S(2)}) %collective-permute-start.7) | collective-permute-done | bytes 131104 | tf_op jit(solution)/shard_map/ppermute | solution.py:227
  97.3 1.6 %mix1.1 = bf16[2,1024,1024]{2,1,0:T(8,128)(2,1)} custom-call(bf16[1024,256]{1,0:T(8,128)(2,1)S(1)} %get-tuple-element.23.refs_0_, bf16[64,1024]{1,0:T(8,128)(2,1)S(1)} %get-tuple-element.32.refs_1_, bf16[64,1024]{1,0:T(8,128)(2,1)S(1)} %collective-permute-done.6.refs_2_, ...), custom_call_target="tpu_custom_call", output_to_operand_aliasing={{}: (5, {})} | custom-call | flops 536870912 | bytes 2621440 | tf_op jit(solution)/shard_map/mix1/pallas_call | solution.py:330
  (14 shorter events, 0.1 us)
Async XLA Ops:
  0.0 10.3 %copy-start = (bf16[2,1024,1024]{2,1,0:T(8,128)(2,1)S(1)}, bf16[2,1024,1024]{2,1,0:T(8,128)(2,1)}, u32[]{:S(2)}) copy-start(bf16[2,1024,1024]{2,1,0:T(8,128)(2,1)} %tok_ref.3) | copy-start | bytes 12582916
  3.8 9.1 %collective-permute-start.3 = (bf16[528,128]{1,0:T(8,128)(2,1)S(1)}, bf16[528,128]{1,0:T(8,128)(2,1)S(1)}, u32[]{:S(2)}, u32[]{:S(2)}) collective-permute-start(bf16[528,128]{1,0:T(8,128)(2,1)S(1)} %get-tuple-element.28), channel_id=1, source_target_pairs={{0,16},{8,24},{16,0},{24,8},{1,17},{9,25},{17,1},{25,9},{2,18},{10... | collective-permute-start | bytes 405512 | tf_op jit(solution)/shard_map/ppermute | solution.py:227
  7.1 10.8 %collective-permute-start.4 = (bf16[528,128]{1,0:T(8,128)(2,1)S(1)}, bf16[528,128]{1,0:T(8,128)(2,1)S(1)}, u32[]{:S(2)}, u32[]{:S(2)}) collective-permute-start(bf16[528,128]{1,0:T(8,128)(2,1)S(1)} %get-tuple-element.29), channel_id=1, source_target_pairs={{0,8},{8,16},{16,24},{24,0},{1,9},{9,17},{17,25},{25,1},{2,10},{10... | collective-permute-start | bytes 405512 | tf_op jit(solution)/shard_map/ppermute | solution.py:227
  7.8 10.1 %collective-permute-start.5 = (bf16[528,128]{1,0:T(8,128)(2,1)S(1)}, bf16[528,128]{1,0:T(8,128)(2,1)S(1)}, u32[]{:S(2)}, u32[]{:S(2)}) collective-permute-start(bf16[528,128]{1,0:T(8,128)(2,1)S(1)} %get-tuple-element.30), channel_id=1, source_target_pairs={{0,24},{8,0},{16,8},{24,16},{1,25},{9,1},{17,9},{25,17},{2,26},{10... | collective-permute-start | bytes 405512 | tf_op jit(solution)/shard_map/ppermute | solution.py:227
  12.0 7.6 %collective-permute-start = (bf16[528,128]{1,0:T(8,128)(2,1)S(1)}, bf16[528,128]{1,0:T(8,128)(2,1)S(1)}, u32[]{:S(2)}, u32[]{:S(2)}) collective-permute-start(bf16[528,128]{1,0:T(8,128)(2,1)S(1)} %get-tuple-element.24), channel_id=1, source_target_pairs={{0,16},{8,24},{16,0},{24,8},{1,17},{9,25},{17,1},{25,9},{2,18},{10... | collective-permute-start | bytes 405512 | tf_op jit(solution)/shard_map/ppermute | solution.py:227
  12.1 8.7 %collective-permute-start.1 = (bf16[528,128]{1,0:T(8,128)(2,1)S(1)}, bf16[528,128]{1,0:T(8,128)(2,1)S(1)}, u32[]{:S(2)}, u32[]{:S(2)}) collective-permute-start(bf16[528,128]{1,0:T(8,128)(2,1)S(1)} %get-tuple-element.25), channel_id=1, source_target_pairs={{0,8},{8,16},{16,24},{24,0},{1,9},{9,17},{17,25},{25,1},{2,10},{10... | collective-permute-start | bytes 405512 | tf_op jit(solution)/shard_map/ppermute | solution.py:227
  12.9 7.8 %collective-permute-start.2 = (bf16[528,128]{1,0:T(8,128)(2,1)S(1)}, bf16[528,128]{1,0:T(8,128)(2,1)S(1)}, u32[]{:S(2)}, u32[]{:S(2)}) collective-permute-start(bf16[528,128]{1,0:T(8,128)(2,1)S(1)} %get-tuple-element.26), channel_id=1, source_target_pairs={{0,24},{8,0},{16,8},{24,16},{1,25},{9,1},{17,9},{25,17},{2,26},{10... | collective-permute-start | bytes 405512 | tf_op jit(solution)/shard_map/ppermute | solution.py:227
  16.6 38.0 %copy-start.1 = (bf16[1024,1024]{1,0:T(8,128)(2,1)S(1)}, bf16[1024,1024]{1,0:T(8,128)(2,1)}, u32[]{:S(2)}) copy-start(bf16[1024,1024]{1,0:T(8,128)(2,1)} %up_ref.1) | copy-start | bytes 6291460
  16.6 38.0 %copy-start.2 = (bf16[1024,1024]{1,0:T(8,128)(2,1)S(1)}, bf16[1024,1024]{1,0:T(8,128)(2,1)}, u32[]{:S(2)}) copy-start(bf16[1024,1024]{1,0:T(8,128)(2,1)} %down_ref.1) | copy-start | bytes 6291460
  83.7 8.0 %collective-permute-start.11 = (bf16[64,1024]{1,0:T(8,128)(2,1)S(1)}, bf16[64,1024]{1,0:T(8,128)(2,1)S(1)}, u32[]{:S(2)}, u32[]{:S(2)}) collective-permute-start(bf16[64,1024]{1,0:T(8,128)(2,1)S(1)} %get-tuple-element.34.refs_1_), channel_id=1, source_target_pairs={{0,16},{8,24},{16,0},{24,8},{1,17},{9,25},{17,1},{25,9},{2,18},{10... | collective-permute-start | bytes 393224 | tf_op jit(solution)/shard_map/ppermute | solution.py:227
  84.9 9.6 %collective-permute-start.10 = (bf16[64,1024]{1,0:T(8,128)(2,1)S(1)}, bf16[64,1024]{1,0:T(8,128)(2,1)S(1)}, u32[]{:S(2)}, u32[]{:S(2)}) collective-permute-start(bf16[64,1024]{1,0:T(8,128)(2,1)S(1)} %get-tuple-element.34.refs_1_), channel_id=1, source_target_pairs={{0,8},{8,16},{16,24},{24,0},{1,9},{9,17},{17,25},{25,1},{2,10},{10... | collective-permute-start | bytes 393224 | tf_op jit(solution)/shard_map/ppermute | solution.py:227
  86.8 7.7 %collective-permute-start.9 = (bf16[64,1024]{1,0:T(8,128)(2,1)S(1)}, bf16[64,1024]{1,0:T(8,128)(2,1)S(1)}, u32[]{:S(2)}, u32[]{:S(2)}) collective-permute-start(bf16[64,1024]{1,0:T(8,128)(2,1)S(1)} %get-tuple-element.34.refs_1_), channel_id=1, source_target_pairs={{0,24},{8,0},{16,8},{24,16},{1,25},{9,1},{17,9},{25,17},{2,26},{10... | collective-permute-start | bytes 393224 | tf_op jit(solution)/shard_map/ppermute | solution.py:227
  88.2 8.0 %collective-permute-start.8 = (bf16[64,1024]{1,0:T(8,128)(2,1)S(1)}, bf16[64,1024]{1,0:T(8,128)(2,1)S(1)}, u32[]{:S(2)}, u32[]{:S(2)}) collective-permute-start(bf16[64,1024]{1,0:T(8,128)(2,1)S(1)} %get-tuple-element.32.refs_1_), channel_id=1, source_target_pairs={{0,16},{8,24},{16,0},{24,8},{1,17},{9,25},{17,1},{25,9},{2,18},{10... | collective-permute-start | bytes 393224 | tf_op jit(solution)/shard_map/ppermute | solution.py:227
  89.3 7.9 %collective-permute-start.7 = (bf16[64,1024]{1,0:T(8,128)(2,1)S(1)}, bf16[64,1024]{1,0:T(8,128)(2,1)S(1)}, u32[]{:S(2)}, u32[]{:S(2)}) collective-permute-start(bf16[64,1024]{1,0:T(8,128)(2,1)S(1)} %get-tuple-element.32.refs_1_), channel_id=1, source_target_pairs={{0,8},{8,16},{16,24},{24,0},{1,9},{9,17},{17,25},{25,1},{2,10},{10... | collective-permute-start | bytes 393224 | tf_op jit(solution)/shard_map/ppermute | solution.py:227
  91.7 5.6 %collective-permute-start.6 = (bf16[64,1024]{1,0:T(8,128)(2,1)S(1)}, bf16[64,1024]{1,0:T(8,128)(2,1)S(1)}, u32[]{:S(2)}, u32[]{:S(2)}) collective-permute-start(bf16[64,1024]{1,0:T(8,128)(2,1)S(1)} %get-tuple-element.32.refs_1_), channel_id=1, source_target_pairs={{0,24},{8,0},{16,8},{24,16},{1,25},{9,1},{17,9},{25,17},{2,26},{10... | collective-permute-start | bytes 393224 | tf_op jit(solution)/shard_map/ppermute | solution.py:227

commit v10 on v9

--- a/solution.py
+++ b/solution.py
@@ -14,7 +14,7 @@
 LANES = 128
 STAT = LANES
 STAT_ROWS = 16
-FETCHES = 2
+FETCHES = 1
 STEPS = 4
 MIB = 1 << 20
 BIG = 52

time: 100 us -> 101 us (1.010)
  no operation moved by 1% of the time
where the time goes in v10:
time: 101 us; the launch traced here: 99.8 us
  blocking collectives  61.1 us (60%)
  starting transfers between devices  17.8 us (18%)
  Pallas kernels  14.1 us (14%)
  waiting for transfers between devices  6.49 us (6%)
    all_to_all x1, blocking collectives, shards(): arrived = lax.all_to_all(halfway, around, 0, 0, tiled=True)  20.5 us
    ppermute x12, starting transfers between devices, shift(): return lax.ppermute(x, 'y', [(i, (i + k) % ny) for i in range(ny)])  17.8 us
    all_to_all x1, blocking collectives, shards(): ring = lax.all_to_all(slot_out, around, 0, 0, tiled=True)  15.4 us
    all_to_all x1, blocking collectives, shards(): own = lax.all_to_all(slot_in, sharers, 0, 0, tiled=True)  12.7 us
    all_to_all x1, blocking collectives, shards(): back = lax.all_to_all(partial, sharers, 0, 0, tiled=True)  12.5 us
    ppermute x12, waiting for transfers between devices, shift(): return lax.ppermute(x, 'y', [(i, (i + k) % ny) for i in range(ny)])  6.49 us
    pallas_call x2, Pallas kernels, gather(): pl.pallas_call(name(gather_kernel, clip, groups, ny, nz), in_specs=[anywh...  6.14 us
    pallas_call x2, Pallas kernels, shards(): pl.pallas_call(name(mix_kernel, clip, ny), in_specs=[vmem()] * (1 + ny) +...  3.29 us
  transfers between devices with their start and end apart: 12, of which 5 were waited for; matrix products, arithmetic and copies ran while one was open for 0% of the time, Pallas kernels for 6%

profile of v10, /device:TPU:2, one launch (start us, length us, event | category | flops | bytes accessed | tf_op | source)
XLA Modules:
  0.0 99.8 jit_solution(12150809850261263099)
XLA Ops:
  0.0 4.5 %gather0.1 = (bf16[528,128]{1,0:T(8,128)(2,1)S(1)}, bf16[528,128]{1,0:T(8,128)(2,1)S(1)}, bf16[528,128]{1,0:T(8,128)(2,1)S(1)}, bf16[528,128]{1,0:T(8,128)(2,1)S(1)}, bf16[1024,256]{1,0:T(8,128)(2,1)S(1)}) custom-call(bf16[2,1024,1024]{2,1,0:T(8,128)(2,1)} %tok_ref.3, bf16[1024,256]{1,0:T(8,128)(2,1)} %refs_1_.1), custom_call_target="tpu_custom_call" | custom-call | flops 1073741824 | bytes 2097152 | tf_op jit(solution)/shard_map/gather0/pallas_call | solution.py:241
  4.5 3.3 %collective-permute-start.3 = (bf16[528,128]{1,0:T(8,128)(2,1)S(1)}, bf16[528,128]{1,0:T(8,128)(2,1)S(1)}, u32[]{:S(2)}, u32[]{:S(2)}) collective-permute-start(bf16[528,128]{1,0:T(8,128)(2,1)S(1)} %get-tuple-element.28), channel_id=1, source_target_pairs={{0,16},{8,24},{16,0},{24,8},{1,17},{9,25},{17,1},{25,9},{2,18},{10... | collective-permute-start | bytes 405512 | tf_op jit(solution)/shard_map/ppermute | solution.py:227
  7.8 0.7 collective-permute-start.4
  8.5 2.6 %collective-permute-start.5 = (bf16[528,128]{1,0:T(8,128)(2,1)S(1)}, bf16[528,128]{1,0:T(8,128)(2,1)S(1)}, u32[]{:S(2)}, u32[]{:S(2)}) collective-permute-start(bf16[528,128]{1,0:T(8,128)(2,1)S(1)} %get-tuple-element.30), channel_id=1, source_target_pairs={{0,24},{8,0},{16,8},{24,16},{1,25},{9,1},{17,9},{25,17},{2,26},{10... | collective-permute-start | bytes 405512 | tf_op jit(solution)/shard_map/ppermute | solution.py:227
  11.1 1.6 %gather1.1 = (bf16[528,128]{1,0:T(8,128)(2,1)S(1)}, bf16[528,128]{1,0:T(8,128)(2,1)S(1)}, bf16[528,128]{1,0:T(8,128)(2,1)S(1)}, bf16[528,128]{1,0:T(8,128)(2,1)S(1)}) custom-call(bf16[2,1024,1024]{2,1,0:T(8,128)(2,1)S(1)} %copy-done, bf16[1024,256]{1,0:T(8,128)(2,1)S(1)} %get-tuple-element.20.refs_1_.sp_ref), custom_call_target="tpu_custom_call" | custom-call | flops 1073741824 | bytes 2097152 | tf_op jit(solution)/shard_map/gather1/pallas_call | solution.py:241
  12.7 0.1 collective-permute-start
  12.8 0.8 collective-permute-start.1
  13.6 2.5 %collective-permute-start.2 = (bf16[528,128]{1,0:T(8,128)(2,1)S(1)}, bf16[528,128]{1,0:T(8,128)(2,1)S(1)}, u32[]{:S(2)}, u32[]{:S(2)}) collective-permute-start(bf16[528,128]{1,0:T(8,128)(2,1)S(1)} %get-tuple-element.26), channel_id=1, source_target_pairs={{0,24},{8,0},{16,8},{24,16},{1,25},{9,1},{17,9},{25,17},{2,26},{10... | collective-permute-start | bytes 405512 | tf_op jit(solution)/shard_map/ppermute | solution.py:227
  16.1 1.2 %combine0.1 = (bf16[1024,256]{1,0:T(8,128)(2,1)S(1)}, f32[8,128]{1,0:T(8,128)S(1)}) custom-call(bf16[2,1024,1024]{2,1,0:T(8,128)(2,1)S(1)} %copy-done, bf16[1024,256]{1,0:T(8,128)(2,1)S(1)} %get-tuple-element.20.refs_1_.sp_ref, bf16[528,128]{1,0:T(8,128)(2,1)S(1)} %get-tuple-element.21.after_ref.refs_0_), custom_call_target="tpu_custom_call" | custom-call | flops 536870912 | bytes 2621440 | tf_op jit(solution)/shard_map/combine0/pallas_call | solution.py:265
  17.3 0.0 copy-start.1
  17.4 1.2 %combine1.1 = (bf16[1024,256]{1,0:T(8,128)(2,1)S(1)}, f32[8,128]{1,0:T(8,128)S(1)}) custom-call(bf16[2,1024,1024]{2,1,0:T(8,128)(2,1)S(1)} %copy-done, bf16[1024,256]{1,0:T(8,128)(2,1)S(1)} %get-tuple-element.20.refs_1_.sp_ref, f32[8,128]{1,0:T(8,128)S(1)} %get-tuple-element.22.after_ref), custom_call_target="tpu_custom_call" | custom-call | flops 536870912 | bytes 2621440 | tf_op jit(solution)/shard_map/combine1/pallas_call | solution.py:265
  18.6 0.4 halfway.1.refs_4_
  19.0 1.3 %collective-permute-done.refs_1_ = bf16[528,128]{1,0:T(8,128)(2,1)S(1)} collective-permute-done((bf16[528,128]{1,0:T(8,128)(2,1)S(1)}, bf16[528,128]{1,0:T(8,128)(2,1)S(1)}, u32[]{:S(2)}, u32[]{:S(2)}) %collective-permute-start) | collective-permute-done | bytes 135200 | tf_op jit(solution)/shard_map/ppermute | solution.py:227
  20.3 1.1 %collective-permute-done.1.refs_2_ = bf16[528,128]{1,0:T(8,128)(2,1)S(1)} collective-permute-done((bf16[528,128]{1,0:T(8,128)(2,1)S(1)}, bf16[528,128]{1,0:T(8,128)(2,1)S(1)}, u32[]{:S(2)}, u32[]{:S(2)}) %collective-permute-start.1) | collective-permute-done | bytes 135200 | tf_op jit(solution)/shard_map/ppermute | solution.py:227
  21.5 0.4 both.1
  21.8 20.5 %all_to_all.20.refs_0_ = bf16[8,2,8,1152]{3,2,1,0:T(8,128)(2,1)S(1)} all-to-all(bf16[8,2,8,1152]{3,2,1,0:T(8,128)(2,1)S(1)} %both.1), channel_id=1, replica_groups=mesh['group'=8,'y'=4,'zh'=2,'quarter'=4] {'zh','quarter'}, dimensions={0} | all-to-all | bytes 589824 | tf_op jit(solution)/shard_map/all_to_all | solution.py:312
  42.4 0.3 merge.1
  42.6 12.7 %all_to_all.21.x_ref = bf16[32,2,1024]{2,1,0:T(2,128)(2,1)S(1)} all-to-all(bf16[32,2,1024]{2,1,0:T(2,128)(2,1)S(1)} %merge.1), channel_id=1, replica_groups=mesh['group'=8,'y'=4,'zh'=2,'quarter'=4] {'group','quarter'}, dimensions={0} | all-to-all | bytes 262144 | tf_op jit(solution)/shard_map/all_to_all | solution.py:315
  55.3 1.0 expert.1
  56.3 12.5 %all_to_all.22.x_ref = bf16[32,2,1024]{2,1,0:T(2,128)(2,1)S(1)} all-to-all(bf16[32,2,1024]{2,1,0:T(2,128)(2,1)S(1)} %expert.1), channel_id=1, replica_groups=mesh['group'=8,'y'=4,'zh'=2,'quarter'=4] {'group','quarter'}, dimensions={0} | all-to-all | bytes 262144 | tf_op jit(solution)/shard_map/all_to_all | solution.py:317
  68.9 0.1 total.1
  69.0 15.4 %all_to_all.23.in_ref = bf16[8,2,8,1024]{3,2,1,0:T(8,128)(2,1)S(1)} all-to-all(bf16[8,2,8,1024]{3,2,1,0:T(8,128)(2,1)S(1)} %total.1), channel_id=1, replica_groups=mesh['group'=8,'y'=4,'zh'=2,'quarter'=4] {'zh','quarter'}, dimensions={0} | all-to-all | bytes 524288 | tf_op jit(solution)/shard_map/all_to_all | solution.py:321
  84.4 1.2 %collective-permute-start.11 = (bf16[64,1024]{1,0:T(8,128)(2,1)S(1)}, bf16[64,1024]{1,0:T(8,128)(2,1)S(1)}, u32[]{:S(2)}, u32[]{:S(2)}) collective-permute-start(bf16[64,1024]{1,0:T(8,128)(2,1)S(1)} %get-tuple-element.34.refs_1_), channel_id=1, source_target_pairs={{0,16},{8,24},{16,0},{24,8},{1,17},{9,25},{17,1},{25,9},{2,18},{10... | collective-permute-start | bytes 393224 | tf_op jit(solution)/shard_map/ppermute | solution.py:227
  85.6 1.9 %collective-permute-start.10 = (bf16[64,1024]{1,0:T(8,128)(2,1)S(1)}, bf16[64,1024]{1,0:T(8,128)(2,1)S(1)}, u32[]{:S(2)}, u32[]{:S(2)}) collective-permute-start(bf16[64,1024]{1,0:T(8,128)(2,1)S(1)} %get-tuple-element.34.refs_1_), channel_id=1, source_target_pairs={{0,8},{8,16},{16,24},{24,0},{1,9},{9,17},{17,25},{25,1},{2,10},{10... | collective-permute-start | bytes 393224 | tf_op jit(solution)/shard_map/ppermute | solution.py:227
  87.5 1.3 %collective-permute-start.9 = (bf16[64,1024]{1,0:T(8,128)(2,1)S(1)}, bf16[64,1024]{1,0:T(8,128)(2,1)S(1)}, u32[]{:S(2)}, u32[]{:S(2)}) collective-permute-start(bf16[64,1024]{1,0:T(8,128)(2,1)S(1)} %get-tuple-element.34.refs_1_), channel_id=1, source_target_pairs={{0,24},{8,0},{16,8},{24,16},{1,25},{9,1},{17,9},{25,17},{2,26},{10... | collective-permute-start | bytes 393224 | tf_op jit(solution)/shard_map/ppermute | solution.py:227
  88.9 1.2 %collective-permute-start.8 = (bf16[64,1024]{1,0:T(8,128)(2,1)S(1)}, bf16[64,1024]{1,0:T(8,128)(2,1)S(1)}, u32[]{:S(2)}, u32[]{:S(2)}) collective-permute-start(bf16[64,1024]{1,0:T(8,128)(2,1)S(1)} %get-tuple-element.32.refs_1_), channel_id=1, source_target_pairs={{0,16},{8,24},{16,0},{24,8},{1,17},{9,25},{17,1},{25,9},{2,18},{10... | collective-permute-start | bytes 393224 | tf_op jit(solution)/shard_map/ppermute | solution.py:227
  90.1 2.3 %collective-permute-done.11.refs_4_ = bf16[64,1024]{1,0:T(8,128)(2,1)S(1)} collective-permute-done((bf16[64,1024]{1,0:T(8,128)(2,1)S(1)}, bf16[64,1024]{1,0:T(8,128)(2,1)S(1)}, u32[]{:S(2)}, u32[]{:S(2)}) %collective-permute-start.11) | collective-permute-done | bytes 131104 | tf_op jit(solution)/shard_map/ppermute | solution.py:227
  92.4 2.2 %collective-permute-start.6 = (bf16[64,1024]{1,0:T(8,128)(2,1)S(1)}, bf16[64,1024]{1,0:T(8,128)(2,1)S(1)}, u32[]{:S(2)}, u32[]{:S(2)}) collective-permute-start(bf16[64,1024]{1,0:T(8,128)(2,1)S(1)} %get-tuple-element.32.refs_1_), channel_id=1, source_target_pairs={{0,24},{8,0},{16,8},{24,16},{1,25},{9,1},{17,9},{25,17},{2,26},{10... | collective-permute-start | bytes 393224 | tf_op jit(solution)/shard_map/ppermute | solution.py:227
  94.6 0.6 collective-permute-done.10.refs_3_
  95.2 1.6 %mix0.1.refs_5_ = bf16[2,1024,1024]{2,1,0:T(8,128)(2,1)} custom-call(bf16[1024,256]{1,0:T(8,128)(2,1)S(1)} %get-tuple-element.33.refs_0_, bf16[64,1024]{1,0:T(8,128)(2,1)S(1)} %get-tuple-element.34.refs_1_, bf16[64,1024]{1,0:T(8,128)(2,1)S(1)} %collective-permute-done.9.refs_2_, bf16[64,1024]{1,0:T(8,128)(2,1)S(1)} %collective-permute-done.10.refs_3_, ...), custom_call_target="tpu_custom_call" | custom-call | flops 536870912 | bytes 2621440 | tf_op jit(solution)/shard_map/mix0/pallas_call | solution.py:330
  96.9 1.1 %collective-permute-done.7.refs_3_ = bf16[64,1024]{1,0:T(8,128)(2,1)S(1)} collective-permute-done((bf16[64,1024]{1,0:T(8,128)(2,1)S(1)}, bf16[64,1024]{1,0:T(8,128)(2,1)S(1)}, u32[]{:S(2)}, u32[]{:S(2)}) %collective-permute-start.7) | collective-permute-done | bytes 131104 | tf_op jit(solution)/shard_map/ppermute | solution.py:227
  98.0 1.6 %mix1.1 = bf16[2,1024,1024]{2,1,0:T(8,128)(2,1)} custom-call(bf16[1024,256]{1,0:T(8,128)(2,1)S(1)} %get-tuple-element.23.refs_0_, bf16[64,1024]{1,0:T(8,128)(2,1)S(1)} %get-tuple-element.32.refs_1_, bf16[64,1024]{1,0:T(8,128)(2,1)S(1)} %collective-permute-done.6.refs_2_, ...), custom_call_target="tpu_custom_call", output_to_operand_aliasing={{}: (5, {})} | custom-call | flops 536870912 | bytes 2621440 | tf_op jit(solution)/shard_map/mix1/pallas_call | solution.py:330
  (14 shorter events, 0.1 us)
Async XLA Ops:
  0.0 11.1 %copy-start = (bf16[2,1024,1024]{2,1,0:T(8,128)(2,1)S(1)}, bf16[2,1024,1024]{2,1,0:T(8,128)(2,1)}, u32[]{:S(2)}) copy-start(bf16[2,1024,1024]{2,1,0:T(8,128)(2,1)} %tok_ref.3) | copy-start | bytes 12582916
  4.5 9.1 %collective-permute-start.3 = (bf16[528,128]{1,0:T(8,128)(2,1)S(1)}, bf16[528,128]{1,0:T(8,128)(2,1)S(1)}, u32[]{:S(2)}, u32[]{:S(2)}) collective-permute-start(bf16[528,128]{1,0:T(8,128)(2,1)S(1)} %get-tuple-element.28), channel_id=1, source_target_pairs={{0,16},{8,24},{16,0},{24,8},{1,17},{9,25},{17,1},{25,9},{2,18},{10... | collective-permute-start | bytes 405512 | tf_op jit(solution)/shard_map/ppermute | solution.py:227
  7.8 10.8 %collective-permute-start.4 = (bf16[528,128]{1,0:T(8,128)(2,1)S(1)}, bf16[528,128]{1,0:T(8,128)(2,1)S(1)}, u32[]{:S(2)}, u32[]{:S(2)}) collective-permute-start(bf16[528,128]{1,0:T(8,128)(2,1)S(1)} %get-tuple-element.29), channel_id=1, source_target_pairs={{0,8},{8,16},{16,24},{24,0},{1,9},{9,17},{17,25},{25,1},{2,10},{10... | collective-permute-start | bytes 405512 | tf_op jit(solution)/shard_map/ppermute | solution.py:227
  8.5 10.1 %collective-permute-start.5 = (bf16[528,128]{1,0:T(8,128)(2,1)S(1)}, bf16[528,128]{1,0:T(8,128)(2,1)S(1)}, u32[]{:S(2)}, u32[]{:S(2)}) collective-permute-start(bf16[528,128]{1,0:T(8,128)(2,1)S(1)} %get-tuple-element.30), channel_id=1, source_target_pairs={{0,24},{8,0},{16,8},{24,16},{1,25},{9,1},{17,9},{25,17},{2,26},{10... | collective-permute-start | bytes 405512 | tf_op jit(solution)/shard_map/ppermute | solution.py:227
  12.7 7.6 %collective-permute-start = (bf16[528,128]{1,0:T(8,128)(2,1)S(1)}, bf16[528,128]{1,0:T(8,128)(2,1)S(1)}, u32[]{:S(2)}, u32[]{:S(2)}) collective-permute-start(bf16[528,128]{1,0:T(8,128)(2,1)S(1)} %get-tuple-element.24), channel_id=1, source_target_pairs={{0,16},{8,24},{16,0},{24,8},{1,17},{9,25},{17,1},{25,9},{2,18},{10... | collective-permute-start | bytes 405512 | tf_op jit(solution)/shard_map/ppermute | solution.py:227
  12.8 8.7 %collective-permute-start.1 = (bf16[528,128]{1,0:T(8,128)(2,1)S(1)}, bf16[528,128]{1,0:T(8,128)(2,1)S(1)}, u32[]{:S(2)}, u32[]{:S(2)}) collective-permute-start(bf16[528,128]{1,0:T(8,128)(2,1)S(1)} %get-tuple-element.25), channel_id=1, source_target_pairs={{0,8},{8,16},{16,24},{24,0},{1,9},{9,17},{17,25},{25,1},{2,10},{10... | collective-permute-start | bytes 405512 | tf_op jit(solution)/shard_map/ppermute | solution.py:227
  13.6 7.8 %collective-permute-start.2 = (bf16[528,128]{1,0:T(8,128)(2,1)S(1)}, bf16[528,128]{1,0:T(8,128)(2,1)S(1)}, u32[]{:S(2)}, u32[]{:S(2)}) collective-permute-start(bf16[528,128]{1,0:T(8,128)(2,1)S(1)} %get-tuple-element.26), channel_id=1, source_target_pairs={{0,24},{8,0},{16,8},{24,16},{1,25},{9,1},{17,9},{25,17},{2,26},{10... | collective-permute-start | bytes 405512 | tf_op jit(solution)/shard_map/ppermute | solution.py:227
  17.3 38.0 %copy-start.1 = (bf16[1024,1024]{1,0:T(8,128)(2,1)S(1)}, bf16[1024,1024]{1,0:T(8,128)(2,1)}, u32[]{:S(2)}) copy-start(bf16[1024,1024]{1,0:T(8,128)(2,1)} %up_ref.1) | copy-start | bytes 6291460
  17.3 38.0 %copy-start.2 = (bf16[1024,1024]{1,0:T(8,128)(2,1)S(1)}, bf16[1024,1024]{1,0:T(8,128)(2,1)}, u32[]{:S(2)}) copy-start(bf16[1024,1024]{1,0:T(8,128)(2,1)} %down_ref.1) | copy-start | bytes 6291460
  84.4 8.0 %collective-permute-start.11 = (bf16[64,1024]{1,0:T(8,128)(2,1)S(1)}, bf16[64,1024]{1,0:T(8,128)(2,1)S(1)}, u32[]{:S(2)}, u32[]{:S(2)}) collective-permute-start(bf16[64,1024]{1,0:T(8,128)(2,1)S(1)} %get-tuple-element.34.refs_1_), channel_id=1, source_target_pairs={{0,16},{8,24},{16,0},{24,8},{1,17},{9,25},{17,1},{25,9},{2,18},{10... | collective-permute-start | bytes 393224 | tf_op jit(solution)/shard_map/ppermute | solution.py:227
  85.6 9.6 %collective-permute-start.10 = (bf16[64,1024]{1,0:T(8,128)(2,1)S(1)}, bf16[64,1024]{1,0:T(8,128)(2,1)S(1)}, u32[]{:S(2)}, u32[]{:S(2)}) collective-permute-start(bf16[64,1024]{1,0:T(8,128)(2,1)S(1)} %get-tuple-element.34.refs_1_), channel_id=1, source_target_pairs={{0,8},{8,16},{16,24},{24,0},{1,9},{9,17},{17,25},{25,1},{2,10},{10... | collective-permute-start | bytes 393224 | tf_op jit(solution)/shard_map/ppermute | solution.py:227
  87.5 7.7 %collective-permute-start.9 = (bf16[64,1024]{1,0:T(8,128)(2,1)S(1)}, bf16[64,1024]{1,0:T(8,128)(2,1)S(1)}, u32[]{:S(2)}, u32[]{:S(2)}) collective-permute-start(bf16[64,1024]{1,0:T(8,128)(2,1)S(1)} %get-tuple-element.34.refs_1_), channel_id=1, source_target_pairs={{0,24},{8,0},{16,8},{24,16},{1,25},{9,1},{17,9},{25,17},{2,26},{10... | collective-permute-start | bytes 393224 | tf_op jit(solution)/shard_map/ppermute | solution.py:227
  88.9 8.0 %collective-permute-start.8 = (bf16[64,1024]{1,0:T(8,128)(2,1)S(1)}, bf16[64,1024]{1,0:T(8,128)(2,1)S(1)}, u32[]{:S(2)}, u32[]{:S(2)}) collective-permute-start(bf16[64,1024]{1,0:T(8,128)(2,1)S(1)} %get-tuple-element.32.refs_1_), channel_id=1, source_target_pairs={{0,16},{8,24},{16,0},{24,8},{1,17},{9,25},{17,1},{25,9},{2,18},{10... | collective-permute-start | bytes 393224 | tf_op jit(solution)/shard_map/ppermute | solution.py:227
  90.1 7.9 %collective-permute-start.7 = (bf16[64,1024]{1,0:T(8,128)(2,1)S(1)}, bf16[64,1024]{1,0:T(8,128)(2,1)S(1)}, u32[]{:S(2)}, u32[]{:S(2)}) collective-permute-start(bf16[64,1024]{1,0:T(8,128)(2,1)S(1)} %get-tuple-element.32.refs_1_), channel_id=1, source_target_pairs={{0,8},{8,16},{16,24},{24,0},{1,9},{9,17},{17,25},{25,1},{2,10},{10... | collective-permute-start | bytes 393224 | tf_op jit(solution)/shard_map/ppermute | solution.py:227
  92.4 5.6 %collective-permute-start.6 = (bf16[64,1024]{1,0:T(8,128)(2,1)S(1)}, bf16[64,1024]{1,0:T(8,128)(2,1)S(1)}, u32[]{:S(2)}, u32[]{:S(2)}) collective-permute-start(bf16[64,1024]{1,0:T(8,128)(2,1)S(1)} %get-tuple-element.32.refs_1_), channel_id=1, source_target_pairs={{0,24},{8,0},{16,8},{24,16},{1,25},{9,1},{17,9},{25,17},{2,26},{10... | collective-permute-start | bytes 393224 | tf_op jit(solution)/shard_map/ppermute | solution.py:227
